TPU v7x, 128 devices: a whole 4x4x4 slice. The times are simulated.
128 devices in a mesh: dp: 2 (over x_hi), ctx: 8 (over z, x_lo), tensor: 8 (over y, core).
Axes of the slice: x: 4 (x_hi: 2, x_lo: 2; x = x_hi * 2 + x_lo), y: 4, z: 4, core: 2. Of those that a mesh axis runs over, the one named last changes fastest.
Arguments:
- tokens: bfloat16 [2048, 3072], P(('dp', 'ctx'), 'tensor'), may hold values from -6 to 6
- d_out: bfloat16 [2048, 3072], P(('dp', 'ctx'), 'tensor'), may hold values from -6 to 6
- routes: int32 [2048, 2], P(('dp', 'ctx')), may hold values from 0 to 7, all different within a row; in each aligned block of 128 rows (0 to 127, 128 to 255, ...) at most 64 rows name the same one
- probs: bfloat16 [2048, 2], P(('dp', 'ctx')), may hold values from 0.049804688 to 1
- w_gate: bfloat16 [8, 3072, 8192], P('ctx', None, ('dp', 'tensor')), may hold values from -0.109375 to 0.109375
- w_up: bfloat16 [8, 3072, 8192], P('ctx', None, ('dp', 'tensor')), may hold values from -0.109375 to 0.109375
- w_down: bfloat16 [8, 8192, 3072], P('ctx', ('dp', 'tensor')), may hold values from -0.0625 to 0.0625
Outputs:
- d_tokens: bfloat16 [2048, 3072], P(('dp', 'ctx'), 'tensor')
- d_probs: float32 [2048, 2], P(('dp', 'ctx'))
- grad_gate: bfloat16 [8, 3072, 8192], P('ctx', None, ('dp', 'tensor'))
- grad_up: bfloat16 [8, 3072, 8192], P('ctx', None, ('dp', 'tensor'))
- grad_down: bfloat16 [8, 8192, 3072], P('ctx', ('dp', 'tensor'))
Inputs may be any that keep to these rules, and one draw needn't show every extreme that they name: `routes`: the two experts of a token differ. Among the 128 tokens of one device no expert is named more than 64 times, a bound that some block reaches.
All inputs are finite; a program needn't handle non-finite values.
Results may differ from a plain program's by a relative error of at most 0.0075.
Values may be sent and summed in bfloat16 or wider, within the bound.
No kernel may reach another device: no remote copies, remote signals or barrier semaphores. Data moves between devices by JAX's collectives and lax.ppermute only.
A program may use at most 128 MiB of HBM per device.

v0:
```python
import jax
import jax.numpy as jnp
from jax import lax
from jax.sharding import PartitionSpec as P


def silu_parts(pre_gate):
    sigma = jax.nn.sigmoid(pre_gate)
    return (pre_gate * sigma, sigma * (1.0 + pre_gate * (1.0 - sigma)))


def expert_rows(rows_in, grads_in, weights_row, gate_weight, up_weight, down_weight):
    pre_gate = jnp.dot(rows_in, gate_weight, preferred_element_type=jnp.float32)
    pre_up = jnp.dot(rows_in, up_weight, preferred_element_type=jnp.float32)
    active, slope = silu_parts(pre_gate)
    hidden = (active * pre_up).astype(jnp.bfloat16)
    backward = lax.dot_general(
        grads_in, down_weight, (((1,), (1,)), ((), ())), preferred_element_type=jnp.float32
    )
    prob_grad = jnp.sum(hidden.astype(jnp.float32) * backward, axis=1)
    hidden_grad = weights_row[:, None] * backward
    gate_grad = (hidden_grad * pre_up * slope).astype(jnp.bfloat16)
    up_grad = (hidden_grad * active).astype(jnp.bfloat16)
    scaled = (weights_row[:, None] * hidden.astype(jnp.float32)).astype(jnp.bfloat16)
    return (gate_grad, up_grad, prob_grad, scaled)


def weight_grads(rows_in, grads_in, gate_grad, up_grad, scaled):
    contract = (((0,), (0,)), ((), ()))
    gate_total = lax.dot_general(rows_in, gate_grad, contract, preferred_element_type=jnp.float32)
    up_total = lax.dot_general(rows_in, up_grad, contract, preferred_element_type=jnp.float32)
    down_total = lax.dot_general(scaled, grads_in, contract, preferred_element_type=jnp.float32)
    return (gate_total, up_total, down_total)


def duplicate(array, copies):
    widened = jnp.broadcast_to(array[None], (copies,) + array.shape)
    return widened.reshape((copies * array.shape[0],) + array.shape[1:])


def on_device(tokens, d_out, routes, probs, w_gate, w_up, w_down):
    whole_x, whole_dy = (
        lax.all_gather(tokens, "tensor", axis=1, tiled=True),
        lax.all_gather(d_out, "tensor", axis=1, tiled=True),
    )
    token_rows = whole_x.shape[0]
    features = whole_x.shape[1]
    ctx_size = lax.axis_size("ctx")
    dp_size = lax.axis_size("dp")
    tensor_size = lax.axis_size("tensor")
    capacity = 4 * token_rows // ctx_size
    flat_ids = routes.reshape(-1)
    one_hot = (flat_ids[:, None] == jnp.arange(ctx_size, dtype=jnp.int32)[None, :]).astype(
        jnp.int32
    )
    position = jnp.sum((jnp.cumsum(one_hot, axis=0) - one_hot) * one_hot, axis=1)
    target = flat_ids * capacity + position
    source = jnp.arange(2 * token_rows, dtype=jnp.int32) // 2
    send_x = (
        jnp.zeros((ctx_size * capacity, features), jnp.bfloat16).at[target].set(whole_x[source])
    )
    send_dy = (
        jnp.zeros((ctx_size * capacity, features), jnp.bfloat16).at[target].set(whole_dy[source])
    )
    send_prob = jnp.zeros((ctx_size * capacity,), jnp.bfloat16).at[target].set(probs.reshape(-1))
    send_x = send_x.reshape(ctx_size, capacity, features)
    send_dy = send_dy.reshape(ctx_size, capacity, features)
    send_prob = send_prob.reshape(ctx_size, capacity)
    recv_x, recv_dy, recv_prob = (
        lax.all_to_all(
            duplicate(send_x, dp_size), ("dp", "ctx"), split_axis=0, concat_axis=0, tiled=True
        ),
        lax.all_to_all(
            duplicate(send_dy, dp_size), ("dp", "ctx"), split_axis=0, concat_axis=0, tiled=True
        ),
        lax.all_to_all(
            duplicate(send_prob, dp_size), ("dp", "ctx"), split_axis=0, concat_axis=0, tiled=True
        ),
    )
    total_rows = dp_size * ctx_size * capacity
    rows_in = recv_x.reshape(total_rows, features)
    grads_in = recv_dy.reshape(total_rows, features)
    weights_row = recv_prob.reshape(total_rows).astype(jnp.float32)
    gate_local = w_gate[0]
    up_local = w_up[0]
    down_local = w_down[0]
    hidden_units = gate_local.shape[1]
    gate_grad, up_grad, prob_grad, scaled = expert_rows(
        rows_in, grads_in, weights_row, gate_local, up_local, down_local
    )
    gate_sum, up_sum, down_sum = weight_grads(rows_in, grads_in, gate_grad, up_grad, scaled)
    rows_per = ctx_size * capacity
    slice_width = features // tensor_size
    gate_split = gate_grad.reshape(dp_size, rows_per, hidden_units)
    up_split = up_grad.reshape(dp_size, rows_per, hidden_units)
    gate_cols = gate_local.reshape(tensor_size, slice_width, hidden_units)
    up_cols = up_local.reshape(tensor_size, slice_width, hidden_units)
    term = jnp.einsum("arf,tdf->atrd", gate_split, gate_cols, preferred_element_type=jnp.float32)
    term = term + jnp.einsum("arf,tdf->atrd", up_split, up_cols, preferred_element_type=jnp.float32)
    term = term.reshape(dp_size * tensor_size * rows_per, slice_width)
    token_grad = lax.psum_scatter(term, ("dp", "tensor"), scatter_dimension=0, tiled=True)
    prob_total = lax.psum(prob_grad, ("dp", "tensor"))
    prob_mine = lax.dynamic_slice_in_dim(prob_total, lax.axis_index("dp") * rows_per, rows_per)
    back_grad, back_prob = (
        lax.all_to_all(
            token_grad.reshape(ctx_size, capacity, slice_width),
            "ctx",
            split_axis=0,
            concat_axis=0,
            tiled=True,
        ),
        lax.all_to_all(
            prob_mine.reshape(ctx_size, capacity), "ctx", split_axis=0, concat_axis=0, tiled=True
        ),
    )
    slot_grad = back_grad.reshape(ctx_size * capacity, slice_width)[target]
    d_tokens = jnp.sum(slot_grad.reshape(token_rows, 2, slice_width), axis=1).astype(jnp.bfloat16)
    d_probs = back_prob.reshape(-1)[target].reshape(token_rows, 2)
    return (
        d_tokens,
        d_probs,
        gate_sum.astype(jnp.bfloat16)[None],
        up_sum.astype(jnp.bfloat16)[None],
        down_sum.astype(jnp.bfloat16)[None],
    )


def solution(mesh):
    in_specs = (
        P(("dp", "ctx"), "tensor"),
        P(("dp", "ctx"), "tensor"),
        P(("dp", "ctx"), None),
        P(("dp", "ctx"), None),
        P("ctx", None, ("dp", "tensor")),
        P("ctx", None, ("dp", "tensor")),
        P("ctx", ("dp", "tensor"), None),
    )
    out_specs = (
        P(("dp", "ctx"), "tensor"),
        P(("dp", "ctx"), None),
        P("ctx", None, ("dp", "tensor")),
        P("ctx", None, ("dp", "tensor")),
        P("ctx", ("dp", "tensor"), None),
    )
    return jax.shard_map(
        on_device, mesh=mesh, in_specs=in_specs, out_specs=out_specs, check_vma=False
    )
```

profile of v0, /device:TPU:2, one launch (start us, length us, event | category | flops | bytes accessed | tf_op | source)
XLA Modules:
  0.0 458.9 jit_solution(5517416819911114519)
XLA Ops:
  7.2 0.8 broadcast_multiply_fusion
  8.0 0.9 copy.23
  8.9 0.1 eq.29
  9.1 0.1 eq.25
  9.2 0.8 copy.25
  10.0 0.1 reshape.210
  10.1 0.1 copy.22
  10.3 0.1 mul.62
  10.4 0.6 reduce-window.6
  11.0 0.2 slice_reduce_fusion
  11.3 0.1 fusion.21
  11.4 2.2 scatter_custom_fusion
  13.5 0.1 broadcast_in_dim.21
  13.6 0.6 copy.26
  14.2 8.3 %all-to-all-start = ((bf16[16,1,64]{2,1,0:T(2,128)(2,1)}), bf16[16,1,64]{2,1,0:T(2,128)(2,1)S(1)}, u32[]{:S(2)}, u32[]{:S(2)}) async-start(bf16[16,1,64]{2,1,0:T(2,128)(2,1)} %copy.26), calls=%async_computation | async-start | bytes 16384 | tf_op jit(solution)/shard_map/all_to_all | solution.py:76
  22.6 15.4 %all_gather.7 = bf16[128,3072]{1,0:T(8,128)(2,1)} all-gather(bf16[128,384]{1,0:T(8,128)(2,1)} %param.7), channel_id=1, replica_groups=mesh['dp'=2,'ctx'=8,'tensor'=8] {'tensor'}, dimensions={1}, use_global_device_ids=true | all-gather | bytes 884736 | tf_op jit(solution)/shard_map/all_gather | solution.py:43
  37.9 9.3 %scatter_custom_fusion.2 = bf16[512,3072]{1,0:T(8,128)(2,1)} fusion(s32[256]{0:T(256)S(1)} %bitcast.82, bf16[128,3072]{1,0:T(8,128)(2,1)} %all_gather.7, s32[1024]{0:T(1024)S(1)} %pad_clamp_fusion.1, bf16[]{:T(256)} %constant.16.clone.1), kind=kCustom, calls=%fused_computation.29 | custom fusion | bytes 3146240 | tf_op jit(solution)/shard_map/scatter | solution.py:60
  47.3 5.3 %broadcast_in_dim.49 = bf16[2,8,64,3072]{3,2,1,0:T(8,128)(2,1)} broadcast(bf16[8,64,3072]{2,1,0:T(8,128)(2,1)} %bitcast.77), dimensions={1,2,3} | broadcast | bytes 9437184 | tf_op jit(solution)/shard_map/broadcast_in_dim | solution.py:37
  52.6 7.4 %all-to-all-start.2 = ((bf16[16,64,3072]{2,1,0:T(8,128)(2,1)}), bf16[16,64,3072]{2,1,0:T(8,128)(2,1)}, u32[]{:S(2)}, u32[]{:S(2)}) async-start(bf16[16,64,3072]{2,1,0:T(8,128)(2,1)} %bitcast.75), calls=%async_computation.2 | async-start | bytes 12582912 | tf_op jit(solution)/shard_map/all_to_all | solution.py:70
  60.0 15.1 %all_gather.6 = bf16[128,3072]{1,0:T(8,128)(2,1)} all-gather(bf16[128,384]{1,0:T(8,128)(2,1)S(1)} %copy-done.5), channel_id=1, replica_groups=mesh['dp'=2,'ctx'=8,'tensor'=8] {'tensor'}, dimensions={1}, use_global_device_ids=true | all-gather | bytes 884736 | tf_op jit(solution)/shard_map/all_gather | solution.py:44
  75.1 9.3 %scatter_custom_fusion.1 = bf16[512,3072]{1,0:T(8,128)(2,1)} fusion(s32[256]{0:T(256)S(1)} %bitcast.83, bf16[128,3072]{1,0:T(8,128)(2,1)} %all_gather.6, s32[1024]{0:T(1024)S(1)} %pad_clamp_fusion.1, bf16[]{:T(256)} %constant.16.clone.1), kind=kCustom, calls=%fused_computation.31 | custom fusion | bytes 3146240 | tf_op jit(solution)/shard_map/scatter | solution.py:63
  84.4 88.8 %all-to-all-done.2 = bf16[16,64,3072]{2,1,0:T(8,128)(2,1)} async-done(((bf16[16,64,3072]{2,1,0:T(8,128)(2,1)}), bf16[16,64,3072]{2,1,0:T(8,128)(2,1)}, u32[]{:S(2)}, u32[]{:S(2)}) %all-to-all-start.2) | async-done | bytes 6291488 | tf_op jit(solution)/shard_map/all_to_all | solution.py:70
  173.2 5.3 %broadcast_in_dim.47 = bf16[2,8,64,3072]{3,2,1,0:T(8,128)(2,1)} broadcast(bf16[8,64,3072]{2,1,0:T(8,128)(2,1)} %bitcast.76), dimensions={1,2,3} | broadcast | bytes 9437184 | tf_op jit(solution)/shard_map/broadcast_in_dim | solution.py:37
  178.5 4.5 all-to-all-start.1
  183.1 0.2 reduce-scatter.2.cloned.1.call-start
  183.4 7.7 %fusion.3 = f32[1024,512]{1,0:T(8,128)} fusion(bf16[1024,3072]{1,0:T(8,128)(2,1)} %bitcast.12, bf16[1,3072,512]{2,1,0:T(8,128)(2,1)S(1)} %copy-done), kind=kOutput, calls=%fused_computation.14 | convolution fusion | flops 3221225472 | bytes 11534336 | tf_op jit(solution)/shard_map/dot_general | solution.py:13
  191.1 7.5 %fusion.5 = f32[1024,512]{1,0:T(8,128)} fusion(bf16[1024,3072]{1,0:T(8,128)(2,1)} %bitcast.12, bf16[1,3072,512]{2,1,0:T(8,128)(2,1)S(1)} %copy-done.2), kind=kOutput, calls=%fused_computation.16 | convolution fusion | flops 3221225472 | bytes 11534336 | tf_op jit(solution)/shard_map/dot_general | solution.py:14
  198.6 90.2 %all-to-all-done.1 = bf16[16,64,3072]{2,1,0:T(8,128)(2,1)} async-done(((bf16[16,64,3072]{2,1,0:T(8,128)(2,1)}), bf16[16,64,3072]{2,1,0:T(8,128)(2,1)}, u32[]{:S(2)}, u32[]{:S(2)}) %all-to-all-start.1) | async-done | bytes 6291488 | tf_op jit(solution)/shard_map/all_to_all | solution.py:73
  288.8 10.4 %fusion.9 = (f32[1024]{0:T(1024)S(1)}, bf16[1024,512]{1,0:T(8,128)(2,1)}, bf16[1024,512]{1,0:T(8,128)(2,1)S(1)}, bf16[1024,512]{1,0:T(8,128)(2,1)S(1)}) fusion(f32[1024,512]{1,0:T(8,128)} %fusion.5, f32[1024,512]{1,0:T(8,128)} %fusion.3, f32[1024]{0:T(1024)S(1)} %reshape.173, bf16[1024,3072]{1,0:T(8,128)(2,1)} %bitcast.8, bf16[1,512,3072]{2,1,0:T(8,128)(2,1)} %param.13), kind=kOutput, calls=%fused_computation.22 | convolution fusion | flops 3231185920 | bytes 16785408 | tf_op jit(solution)/shard_map/dot_general | solution.py:17
  299.2 3.5 fusion.25
  302.7 6.8 %convolution_add_fusion = f32[2,512,8,384]{3,1,2,0:T(8,128)} fusion(f32[2,512,8,384]{3,1,2,0:T(8,128)S(1)} %fusion.25, bf16[2,512,512,1]{2,1,3,0:T(8,128)(2,1)S(1)} %bitcast.79, bf16[8,384,512,1]{2,1,0,3:T(8,128)(2,1)S(1)} %bitcast.78), kind=kOutput, calls=%fused_computation.13 | convolution fusion | flops 3224371200 | bytes 29360128 | tf_op jit(solution)/shard_map/arf,tdf->atrd/dot_general | solution.py:99
  309.5 33.3 %psum.7 = f32[1024]{0:T(1024)S(1)} all-reduce(f32[1024]{0:T(1024)S(1)} %get-tuple-element.20), channel_id=1, replica_groups=mesh['dp'=2,'ctx'=8,'tensor'=8] {'dp','tensor'}, use_global_device_ids=true, to_apply=%region_9.10 | all-reduce | flops 1024 | bytes 8192 | tf_op jit(solution)/shard_map/psum | solution.py:102
  342.8 0.1 dynamic_slice.3
  342.9 0.7 all_to_all.26
  343.5 5.7 %all-to-all-start.4 = ((f32[8,1,64]{2,1,0:T(1,128)}), f32[8,1,64]{2,1,0:T(1,128)S(1)}, u32[]{:S(2)}, u32[]{:S(2)}) async-start(f32[8,1,64]{2,1,0:T(1,128)} %all_to_all.26), calls=%async_computation.5 | async-start | bytes 8192 | tf_op jit(solution)/shard_map/all_to_all | solution.py:112
  349.2 7.9 %fusion.2 = bf16[1,512,3072]{2,1,0:T(8,128)(2,1)} fusion(bf16[1024,3072]{1,0:T(8,128)(2,1)} %bitcast.8, bf16[1024,512]{1,0:T(8,128)(2,1)S(1)} %copy-done.8, f32[1024]{0:T(1024)S(1)} %reshape.173), kind=kOutput, calls=%fused_computation.12 | convolution fusion | flops 3224371200 | bytes 10489856 | tf_op jit(solution)/shard_map/dot_general | solution.py:32
  357.1 7.8 %fusion = bf16[1,3072,512]{2,1,0:T(8,128)(2,1)} fusion(bf16[1024,3072]{1,0:T(8,128)(2,1)} %bitcast.12, bf16[1024,512]{1,0:T(8,128)(2,1)S(1)} %copy-done.7), kind=kOutput, calls=%fused_computation.10 | convolution fusion | flops 3222798336 | bytes 10485760 | tf_op jit(solution)/shard_map/dot_general | solution.py:30
  364.9 63.4 %reduce-scatter.2.cloned.1.call-done = f32[512,384]{1,0:T(8,128)} async-done(((f32[8192,384]{1,0:T(8,128)}), f32[512,384]{1,0:T(8,128)}) %reduce-scatter.2.cloned.1.call-update) | async-done | bytes 786448 | tf_op jit(solution)/shard_map/reduce_scatter | solution.py:101
  428.3 5.9 %all-to-all-start.3 = ((f32[8,64,384]{2,1,0:T(8,128)}), f32[8,64,384]{2,1,0:T(8,128)}, u32[]{:S(2)}, u32[]{:S(2)}) async-start(f32[8,64,384]{2,1,0:T(8,128)} %bitcast.80), calls=%async_computation.4 | async-start | bytes 1572864 | tf_op jit(solution)/shard_map/all_to_all | solution.py:105
  434.2 8.3 %fusion.1 = bf16[1,3072,512]{2,1,0:T(8,128)(2,1)} fusion(bf16[1024,3072]{1,0:T(8,128)(2,1)} %bitcast.12, bf16[1024,512]{1,0:T(8,128)(2,1)} %copy-done.4), kind=kOutput, calls=%fused_computation.11 | convolution fusion | flops 3222798336 | bytes 10485760 | tf_op jit(solution)/shard_map/dot_general | solution.py:31
  442.5 0.5 broadcast.152
  443.0 0.7 reduce.9
  443.8 1.9 gather_fusion.1
  445.7 0.1 reshape.172
  445.9 0.6 copy.27
  446.5 3.0 gather_fusion
  449.5 1.2 reshape.170
  450.7 1.1 reduce_sum.31
  (33 shorter events, 0.3 us)
Async XLA Ops:
  7.2 176.2 %copy-start = (bf16[1,3072,512]{2,1,0:T(8,128)(2,1)S(1)}, bf16[1,3072,512]{2,1,0:T(8,128)(2,1)}, u32[]{:S(2)}) copy-start(bf16[1,3072,512]{2,1,0:T(8,128)(2,1)} %param.11) | copy-start | bytes 9437188
  14.2 33.0 %all-to-all-start = ((bf16[16,1,64]{2,1,0:T(2,128)(2,1)}), bf16[16,1,64]{2,1,0:T(2,128)(2,1)S(1)}, u32[]{:S(2)}, u32[]{:S(2)}) async-start(bf16[16,1,64]{2,1,0:T(2,128)(2,1)} %copy.26), calls=%async_computation | async-start | bytes 16384 | tf_op jit(solution)/shard_map/all_to_all | solution.py:76
  52.6 7.4 %copy-start.5 = (bf16[128,384]{1,0:T(8,128)(2,1)S(1)}, bf16[128,384]{1,0:T(8,128)(2,1)}, u32[]{:S(2)}) copy-start(bf16[128,384]{1,0:T(8,128)(2,1)} %param.8) | copy-start | bytes 294916
  52.6 120.6 %all-to-all-start.2 = ((bf16[16,64,3072]{2,1,0:T(8,128)(2,1)}), bf16[16,64,3072]{2,1,0:T(8,128)(2,1)}, u32[]{:S(2)}, u32[]{:S(2)}) async-start(bf16[16,64,3072]{2,1,0:T(8,128)(2,1)} %bitcast.75), calls=%async_computation.2 | async-start | bytes 12582912 | tf_op jit(solution)/shard_map/all_to_all | solution.py:70
  178.5 110.2 %all-to-all-start.1 = ((bf16[16,64,3072]{2,1,0:T(8,128)(2,1)}), bf16[16,64,3072]{2,1,0:T(8,128)(2,1)}, u32[]{:S(2)}, u32[]{:S(2)}) async-start(bf16[16,64,3072]{2,1,0:T(8,128)(2,1)} %bitcast.74), calls=%async_computation.1 | async-start | bytes 12582912 | tf_op jit(solution)/shard_map/all_to_all | solution.py:73
  183.1 245.2 %reduce-scatter.2.cloned.1.call-start = ((), (), s32[]{:S(2)}) async-start(), calls=%async_computation.6 | async-start | bytes 13369344 | tf_op jit(solution)/shard_map/reduce_scatter | solution.py:101
  183.4 7.7 %copy-start.2 = (bf16[1,3072,512]{2,1,0:T(8,128)(2,1)S(1)}, bf16[1,3072,512]{2,1,0:T(8,128)(2,1)}, u32[]{:S(2)}) copy-start(bf16[1,3072,512]{2,1,0:T(8,128)(2,1)} %param.12) | copy-start | bytes 9437188
  299.2 3.5 copy-start.6
  299.2 3.5 copy-start.4
  299.2 3.5 copy-start.3
  309.4 39.8 %copy-start.8 = (bf16[1024,512]{1,0:T(8,128)(2,1)S(1)}, bf16[1024,512]{1,0:T(8,128)(2,1)}, u32[]{:S(2)}) copy-start(bf16[1024,512]{1,0:T(8,128)(2,1)} %get-tuple-element.21) | copy-start | bytes 3145732
  343.5 21.4 %all-to-all-start.4 = ((f32[8,1,64]{2,1,0:T(1,128)}), f32[8,1,64]{2,1,0:T(1,128)S(1)}, u32[]{:S(2)}, u32[]{:S(2)}) async-start(f32[8,1,64]{2,1,0:T(1,128)} %all_to_all.26), calls=%async_computation.5 | async-start | bytes 8192 | tf_op jit(solution)/shard_map/all_to_all | solution.py:112
  349.2 7.9 %copy-start.7 = (bf16[1024,512]{1,0:T(8,128)(2,1)S(1)}, bf16[1024,512]{1,0:T(8,128)(2,1)}, u32[]{:S(2)}) copy-start(bf16[1024,512]{1,0:T(8,128)(2,1)} %copy-done.6) | copy-start | bytes 3145732
  428.3 18.2 %all-to-all-start.3 = ((f32[8,64,384]{2,1,0:T(8,128)}), f32[8,64,384]{2,1,0:T(8,128)}, u32[]{:S(2)}, u32[]{:S(2)}) async-start(f32[8,64,384]{2,1,0:T(8,128)} %bitcast.80), calls=%async_computation.4 | async-start | bytes 1572864 | tf_op jit(solution)/shard_map/all_to_all | solution.py:105
  434.2 17.7 %copy-start.1 = (bf16[1,3072,512]{2,1,0:T(8,128)(2,1)S(1)}, bf16[1,3072,512]{2,1,0:T(8,128)(2,1)}, u32[]{:S(2)}) copy-start(bf16[1,3072,512]{2,1,0:T(8,128)(2,1)} %param.11) | copy-start | bytes 9437188
Sparse Core Ops, SparseCore 0:
  309.6 118.6 reduce-scatter.1
where the time goes:
time: 468 us; the launch traced here: 459 us
  waiting for transfers between devices  242 us (52%)
  blocking collectives  63.8 us (14%)
  matrix products  59.8 us (13%)
  local copies, waits for them, and re-layouts  43.1 us (9%)
  starting transfers between devices  32 us (7%)
  between operations  14.4 us (3%)
    all_to_all x1, waiting for transfers between devices, on_device(): lax.all_to_all(duplicate(send_dy, dp_size), ('dp', 'ctx'), split_axis=0,...  90.2 us
    all_to_all x1, waiting for transfers between devices, on_device(): lax.all_to_all(duplicate(send_x, dp_size), ('dp', 'ctx'), split_axis=0, c...  88.8 us
    reduce_scatter x1, waiting for transfers between devices, on_device(): lax.psum_scatter(term, ('dp', 'tensor'), scatter_dimension=0, tiled=True)  63.4 us
    psum x1, blocking collectives, on_device(): prob_total = lax.psum(prob_grad, ('dp', 'tensor'))  33.3 us
    scatter x2, local copies, waits for them, and re-layouts, on_device(): jnp.zeros((ctx_size * capacity, features), jnp.bfloat16).at[target]  18.6 us
    all_gather x1, blocking collectives, on_device(): lax.all_gather(tokens, 'tensor', axis=1, tiled=True)  15.4 us
    all_gather x1, blocking collectives, on_device(): lax.all_gather(d_out, 'tensor', axis=1, tiled=True)  15.1 us
    broadcast_in_dim x3, local copies, waits for them, and re-layouts, duplicate(): widened = jnp.broadcast_to(array[None], (copies,) + array.shape)  10.8 us
  transfers between devices with their start and end apart: 6, of which 3 were waited for; matrix products, arithmetic and copies ran while one was open for 13% of the time, Pallas kernels for 0%

commit v1 on v0

v1 whole, which is shorter than its diff:
```python
import jax
import jax.numpy as jnp
from jax import lax
from jax.experimental import pallas as pl
from jax.experimental.pallas import tpu as pltpu
from jax.sharding import PartitionSpec as P

BF = jnp.bfloat16
F32 = jnp.float32
VMEM_LIMIT = 56 * 1024 * 1024
EXPERTS = 8
CAP = 64
TOK = 128
COLS = 384
ROWS = 1024
HID = 512
NT = (((1,), (1,)), ((), ()))
TN = (((0,), (0,)), ((), ()))


def dot(a, b, dims=(((1,), (0,)), ((), ()))):
    return lax.dot_general(a, b, dims, preferred_element_type=F32)


def call(body, outs, grid=None, scratch=(), flops=0, nbytes=0, **specs):
    params = dict(vmem_limit_bytes=VMEM_LIMIT)
    return pl.pallas_call(
        body,
        out_shape=outs,
        compiler_params=pltpu.CompilerParams(**params),
        cost_estimate=pl.CostEstimate(flops=flops, bytes_accessed=nbytes, transcendentals=0),
        **specs,
    )


def sds(shape, dtype=BF):
    return jax.ShapeDtypeStruct(shape, dtype)


def slot_masks(routes):
    expert = lax.broadcasted_iota(jnp.int32, (EXPERTS, TOK), 0)
    first = routes[0:1, :] == expert
    second = routes[1:2, :] == expert
    named = jnp.where(first | second, 1.0, 0.0).astype(F32)
    before = lax.broadcasted_iota(jnp.int32, (TOK, TOK), 0)
    after = lax.broadcasted_iota(jnp.int32, (TOK, TOK), 1)
    earlier = jnp.where(before < after, 1.0, 0.0).astype(BF)
    rank = dot(named.astype(BF), earlier)
    slot = jnp.where(named > 0.0, rank, -1.0)
    return first, second, slot


def one_hot(slot, expert):
    place = lax.broadcasted_iota(jnp.int32, (CAP, TOK), 0).astype(F32)
    return jnp.where(slot[expert : expert + 1, :] == place, 1.0, 0.0)


def dispatch_x_body(routes, tokens, out):
    _, _, slot = slot_masks(routes[...])
    select = jnp.concatenate([one_hot(slot, e) for e in range(EXPERTS)], axis=0).astype(BF)
    rows = dot(select, tokens[...]).astype(BF).reshape(EXPERTS, CAP, COLS)
    out[0:EXPERTS] = rows
    out[EXPERTS : 2 * EXPERTS] = rows


def dispatch_g_body(routes, probs, g0, g1, g2, g3, out):
    first, _, slot = slot_masks(routes[...])
    weight = jnp.where(first, probs[0:1, :], probs[1:2, :])
    select = jnp.concatenate(
        [one_hot(slot, e) * weight[e : e + 1, :] for e in range(EXPERTS)], axis=0
    ).astype(BF)
    for i, g in enumerate((g0, g1, g2, g3)):
        rows = dot(select, g[...]).astype(BF).reshape(EXPERTS, CAP, COLS)
        out[0:EXPERTS, :, i * COLS : (i + 1) * COLS] = rows
        out[EXPERTS : 2 * EXPERTS, :, i * COLS : (i + 1) * COLS] = rows


def slice_of(t, dy, sibling):
    core = t % 2
    core = 1 - core if sibling else core
    return ((t // 2 + dy) % 4) * 2 + core


def plain_call(body, t, ins, outs, scratch, copies, flops, nbytes):
    anywhere = pl.BlockSpec(memory_space=pltpu.HBM)
    return pl.pallas_call(
        body,
        out_shape=outs,
        in_specs=[pl.BlockSpec(memory_space=pltpu.SMEM)] + [anywhere] * len(ins),
        out_specs=[anywhere] * len(outs),
        scratch_shapes=[pltpu.VMEM(shape, dtype) for shape, dtype in scratch]
        + [pltpu.SemaphoreType.DMA((copies,))],
        compiler_params=pltpu.CompilerParams(vmem_limit_bytes=VMEM_LIMIT),
        cost_estimate=pl.CostEstimate(flops=flops, bytes_accessed=nbytes, transcendentals=0),
    )(t, *ins)


class Copies:
    def __init__(self, sems):
        self.sems, self.used = sems, 0

    def start(self, src, dst):
        copy = pltpu.make_async_copy(src, dst, self.sems.at[self.used])
        self.used += 1
        copy.start()
        return copy


def wait_all(copies):
    for copy in copies:
        copy.wait()


def slice_at(t, dy, sibling):
    return pl.ds(pl.multiple_of(slice_of(t[0], dy, sibling) * COLS, COLS), COLS)


def lanes(dy):
    return slice(dy * COLS, (dy + 1) * COLS)


def down_columns(copies, t, wd, into, sibling):
    return [
        copies.start(
            wd.at[:, pl.ds(pl.multiple_of(slice_of(t[0], dy, sibling) * COLS, 128), COLS)],
            into.at[:, lanes(dy)],
        )
        for dy in range(4)
    ]


def gate_up_rows(copies, t, wg, wu, into, steps, sibling):
    started = []
    for i, dy in enumerate(steps):
        at = slice_at(t, dy, sibling)
        started.append(copies.start(wg.at[at, :], into.at[lanes(i), 0:HID]))
        started.append(copies.start(wu.at[at, :], into.at[lanes(i), HID : 2 * HID]))
    return started


def chunks(rows):
    return [slice(r, r + rows) for r in range(0, ROWS, rows)]


def back_own_body(t, g, wd, out, g_v, w_v, out_v, sems):
    copies = Copies(sems)
    w_in = down_columns(copies, t, wd, w_v, False)
    g_in = [copies.start(g.at[c], g_v.at[c]) for c in chunks(256)]
    wait_all(w_in)
    done = []
    for c, g_copy in zip(chunks(256), g_in):
        g_copy.wait()
        out_v[c] = dot(g_v[c], w_v[...], NT)
        done.append(copies.start(out_v.at[c], out.at[c]))
    wait_all(done)


def split_lanes(value):
    upper = value.astype(BF).astype(F32)
    lower = value - upper
    lane = lax.broadcasted_iota(jnp.int32, (value.shape[0], 128), 1)
    return jnp.where(lane == 0, upper, jnp.where(lane == 1, lower, 0.0)).astype(BF)


def back_body(t, g, own, act, slope, hidden, wd, wg, wu, grads, prob, *refs):
    parts = refs[:4]
    g_v, own_v, act_v, slope_v, hidden_v, wd_v, w_v, grads_v, prob_v, part_v, sems = refs[4:]
    copies = Copies(sems)
    wd_in = down_columns(copies, t, wd, wd_v, True)
    pairs = ((g, g_v), (own, own_v), (act, act_v), (slope, slope_v), (hidden, hidden_v))
    rows = chunks(256)
    ins = [[copies.start(a.at[rows[0]], b.at[rows[0]]) for a, b in pairs]]
    w_in = gate_up_rows(copies, t, wg, wu, w_v, range(4), True)
    ins += [[copies.start(a.at[c], b.at[c]) for a, b in pairs] for c in rows[1:]]
    done = []
    for i, c in enumerate(rows):
        if i == 0:
            wait_all(wd_in)
        wait_all(ins[i])
        back = own_v[c] + dot(g_v[c], wd_v[...], NT)
        prob_v[c] = split_lanes(
            jnp.sum(hidden_v[c].astype(F32) * back, axis=1, keepdims=True)
        )
        grads_v[c, 0:HID] = (back * slope_v[c]).astype(BF)
        grads_v[c, HID : 2 * HID] = (back * act_v[c]).astype(BF)
        if i == 0:
            wait_all(w_in)
        part_v[c] = dot(grads_v[c], w_v[...], NT).astype(BF)
        done.append(copies.start(grads_v.at[c], grads.at[c]))
        done.append(copies.start(prob_v.at[c], prob.at[c]))
        for dy in range(4):
            done.append(copies.start(part_v.at[c, lanes(dy)], parts[dy].at[c]))
    wait_all(done)


def sums_body(t, grads, prob, prob_sib, s1, s2, s3, wg, wu, out1, out2, out3, *refs):
    grads_v, prob_v, sib_v, p1, p2, p3, w_v, o1, o2, o3, sems = refs
    copies = Copies(sems)
    w_in = gate_up_rows(copies, t, wg, wu, w_v, (2, 1, 3), False)
    pairs = ((grads, grads_v), (prob, prob_v), (prob_sib, sib_v), (s2, p2), (s1, p1), (s3, p3))
    rows = chunks(256)
    ins = [[copies.start(a.at[c], b.at[c]) for a, b in pairs] for c in rows]
    wait_all(w_in)
    done = []
    for c, started in zip(rows, ins):
        wait_all(started)
        part = dot(grads_v[c], w_v[...], NT)
        for i, (p, o) in enumerate(((p2, o2), (p1, o1), (p3, o3))):
            o[c, 0:COLS] = (part[:, lanes(i)] + p[c].astype(F32)).astype(BF)
        both = prob_v[c].astype(F32) + sib_v[c].astype(F32)
        o2[c, COLS : COLS + 128] = split_lanes(jnp.sum(both, axis=1, keepdims=True))
        for o, out in ((o2, out2), (o1, out1), (o3, out3)):
            done.append(copies.start(o.at[c], out.at[c]))
    wait_all(done)


def last_sum_body(t, grads, s0, left, right, wg, wu, out, *refs):
    grads_v, s_v, l_v, r_v, w_v, o_v, sems = refs
    copies = Copies(sems)
    w_in = gate_up_rows(copies, t, wg, wu, w_v, (0,), False)
    pairs = ((grads, grads_v), (s0, s_v), (left, l_v), (right, r_v))
    rows = chunks(256)
    ins = [[copies.start(a.at[c], b.at[c]) for a, b in pairs] for c in rows]
    wait_all(w_in)
    done = []
    for c, started in zip(rows, ins):
        wait_all(started)
        part = dot(grads_v[c], w_v[...], NT)
        part += s_v[c].astype(F32) + l_v[c].astype(F32) + r_v[c].astype(F32)
        o_v[c] = part.astype(BF)
        done.append(copies.start(o_v.at[c], out.at[c]))
    wait_all(done)


def forward_body(t, *refs):
    xs, (wg, wu), (act, slope, hidden) = refs[:8], refs[8:10], refs[10:13]
    x_v, wg_v, wu_v, act_v, slope_v, hidden_v, sems = refs[13:]
    copies = Copies(sems)
    rows = chunks(256)

    def x_chunk(c):
        return [
            copies.start(
                x.at[c],
                x_v.at[
                    c,
                    pl.ds(
                        pl.multiple_of(slice_of(t[0], i % 4, i >= 4) * COLS, 128), COLS
                    ),
                ],
            )
            for i, x in enumerate(xs)
        ]

    ins = [x_chunk(rows[0])]
    wg_in = copies.start(wg, wg_v)
    wu_in = copies.start(wu, wu_v)
    ins += [x_chunk(c) for c in rows[1:]]
    done = []
    for i, c in enumerate(rows):
        wait_all(ins[i])
        if i == 0:
            wg_in.wait()
        gate = dot(x_v[c], wg_v[...])
        if i == 0:
            wu_in.wait()
        up = dot(x_v[c], wu_v[...])
        sigma = jax.nn.sigmoid(gate)
        active = gate * sigma
        act_v[c] = active
        slope_v[c] = up * (sigma * (1.0 + gate * (1.0 - sigma)))
        hidden_v[c] = (active * up).astype(BF)
        for a, b in ((act_v, act), (slope_v, slope), (hidden_v, hidden)):
            done.append(copies.start(a.at[c], b.at[c]))
    wait_all(done)


def weights_gate_up_body(t, grads, *refs):
    xs = refs[:8]
    out_gate, out_up = refs[8:10]
    for i in range(8):
        place = slice_of(t[0], i % 4, i >= 4)
        at = pl.ds(pl.multiple_of(place * COLS, COLS), COLS)
        both = dot(xs[i][...], grads[...], TN).astype(BF)
        out_gate[at, :] = both[:, 0:HID]
        out_up[at, :] = both[:, HID : 2 * HID]


def weights_down_body(t, hidden, own, sib, out, h_v, own_v, sib_v, ht_v, out_v, sems):
    copies = Copies(sems)
    h_in = copies.start(hidden, h_v)
    pairs = [(side, half) for side in range(2) for half in range(2)]
    g_in = []
    for side, half in pairs:
        cols = slice(half * 2 * COLS, (half + 1) * 2 * COLS)
        src, dst = ((own, own_v), (sib, sib_v))[side]
        g_in.append(copies.start(src.at[:, cols], dst.at[:, cols]))
    h_in.wait()
    ht_v[...] = h_v[...].T
    done = []
    for (side, half), started in zip(pairs, g_in):
        started.wait()
        cols = slice(half * 2 * COLS, (half + 1) * 2 * COLS)
        part = dot(ht_v[...], (own_v, sib_v)[side][:, cols]).astype(BF)
        for j in range(2):
            dy = half * 2 + j
            place = out_v.at[:, slice((side * 4 + dy) * COLS, (side * 4 + dy + 1) * COLS)]
            place[...] = part[:, lanes(j)]
            at = pl.ds(pl.multiple_of(slice_of(t[0], dy, side == 1) * COLS, 128), COLS)
            done.append(copies.start(place, out.at[:, at]))
    wait_all(done)


def selection(routes):
    first, second, slot = slot_masks(routes)
    hots = [one_hot(slot, e) for e in range(EXPERTS)]
    both = jnp.concatenate(hots, axis=0).astype(BF)
    parts = [
        jnp.concatenate(
            [hots[e] * jnp.where(m[e : e + 1, :], 1.0, 0.0) for e in range(EXPERTS)], axis=0
        ).astype(BF)
        for m in (first, second)
    ]
    return both, parts


def combine_far_body(routes, rows, out, prob_out):
    both, parts = selection(routes[...])
    half = EXPERTS * CAP
    total = dot(both, rows[0:half, 0:COLS], TN) + dot(both, rows[half : 2 * half, 0:COLS], TN)
    out[...] = total.astype(BF)
    lanes = rows[0:half, COLS : COLS + 128], rows[half : 2 * half, COLS : COLS + 128]
    for k in range(2):
        value = dot(lanes[0], parts[k], TN) + dot(lanes[1], parts[k], TN)
        prob_out[k : k + 1, :] = value[0:1, :] + value[1:2, :]
    prob_out[2:8, :] = jnp.zeros((6, TOK), F32)


def finish_body(routes, probs, rows, far, q0, q1, q2, q3, out, prob_out):
    both, _ = selection(routes[...])
    half = EXPERTS * CAP
    total = dot(both, rows[0:half, :], TN) + dot(both, rows[half : 2 * half, :], TN)
    out[...] = (total + far[...].astype(F32)).astype(BF)
    prob = q0[0:2, :] + q1[0:2, :] + q2[0:2, :] + q3[0:2, :]
    prob_out[...] = prob / probs[...]


def on_device(tokens, d_out, routes, probs, w_gate, w_up, w_down):
    wg, wu, wd = w_gate[0], w_up[0], w_down[0]
    t = lax.axis_index("tensor").astype(jnp.int32).reshape(1)
    routes_t = routes.T
    probs_t = probs.T.astype(F32)

    def from_y(x, dy):
        return lax.ppermute(
            x, "tensor", [(i, ((i // 2 - dy) % 4) * 2 + i % 2) for i in range(8)]
        )

    def from_sibling(x):
        return lax.ppermute(x, "tensor", [(i, i ^ 1) for i in range(8)])

    def exchange(x):
        got = lax.all_to_all(x, ("dp", "ctx"), split_axis=0, concat_axis=0, tiled=True)
        return got.reshape(ROWS, x.shape[2])

    def after(x, *others):
        return lax.optimization_barrier((x,) + others)[0]

    MB = 1 << 20
    wide = 4 * COLS
    with jax.named_scope("dispatch"):
        gs = [d_out] + [from_y(d_out, dy) for dy in (1, 2, 3)]
        send_x = call(dispatch_x_body, sds((16, CAP, COLS)), flops=10**8, nbytes=MB)(routes_t, tokens)
        x0 = exchange(send_x)
        send_g = call(dispatch_g_body, sds((16, CAP, wide)), flops=2 * 10**8, nbytes=4 * MB)(
            routes_t, probs_t, *gs
        )
    with jax.named_scope("gather"):
        xs = [x0] + [from_y(x0, dy) for dy in (1, 2, 3)]
        x0_sib = from_sibling(x0)
        xs = xs + [x0_sib] + [from_sibling(x) for x in xs[1:]]
        g_own = exchange(after(send_g, x0))
    with jax.named_scope("forward"):
        act, slope, hidden = plain_call(
            forward_body,
            t,
            xs + [wg, wu],
            [sds((ROWS, HID), F32), sds((ROWS, HID), F32), sds((ROWS, HID))],
            [((ROWS, 8 * COLS), BF), ((8 * COLS, HID), BF), ((8 * COLS, HID), BF)]
            + [((ROWS, HID), F32), ((ROWS, HID), F32), ((ROWS, HID), BF)],
            46,
            6_500_000_000,
            18 * MB,
        )
        g_own = after(g_own, hidden)
        g_sib = from_sibling(g_own)
    with jax.named_scope("backward"):
        (back,) = plain_call(
            back_own_body,
            t,
            [g_own, wd],
            [sds((ROWS, HID), F32)],
            [((ROWS, wide), BF), ((HID, wide), BF), ((ROWS, HID), F32)],
            12,
            1_600_000_000,
            7 * MB,
        )
        got = plain_call(
            back_body,
            t,
            [g_sib, back, act, slope, hidden, wd, wg, wu],
            [sds((ROWS, 2 * HID)), sds((ROWS, 128))] + [sds((ROWS, COLS))] * 4,
            [((ROWS, wide), BF)]
            + [((ROWS, HID), F32)] * 3
            + [((ROWS, HID), BF), ((HID, wide), BF), ((wide, 2 * HID), BF)]
            + [((ROWS, 2 * HID), BF), ((ROWS, 128), BF), ((ROWS, wide), BF)],
            56,
            4_800_000_000,
            24 * MB,
        )
        grads, prob = got[:2]
        prob_sib = from_sibling(prob)
        part_sib = [from_sibling(p) for p in got[2:]]
    with jax.named_scope("weights_down"):
        (grad_down,) = plain_call(
            weights_down_body,
            t,
            [after(hidden, grads), g_own, g_sib],
            [sds((HID, 8 * COLS))],
            [((ROWS, HID), BF), ((ROWS, wide), BF), ((ROWS, wide), BF)]
            + [((HID, ROWS), BF), ((HID, 8 * COLS), BF)],
            13,
            3_300_000_000,
            10 * MB,
        )
    with jax.named_scope("sums"):
        out1, out2, out3 = plain_call(
            sums_body,
            t,
            [after(grads, grad_down), prob, prob_sib] + part_sib[1:] + [wg, wu],
            [sds((ROWS, COLS)), sds((ROWS, COLS + 128)), sds((ROWS, COLS))],
            [((ROWS, 2 * HID), BF), ((ROWS, 128), BF), ((ROWS, 128), BF)]
            + [((ROWS, COLS), BF)] * 3
            + [((3 * COLS, 2 * HID), BF)]
            + [((ROWS, COLS), BF), ((ROWS, COLS + 128), BF), ((ROWS, COLS), BF)],
            42,
            2_400_000_000,
            10 * MB,
        )
        left = from_y(out1, 3)
        right = from_y(out3, 1)
        far = exchange(out2.reshape(16, CAP, COLS + 128))
    vm = pl.BlockSpec(memory_space=pltpu.VMEM)
    sm = pl.BlockSpec(memory_space=pltpu.SMEM)
    with jax.named_scope("weights_gate_up"):
        grad_gate, grad_up = call(
            weights_gate_up_body,
            [sds((8 * COLS, HID))] * 2,
            flops=6_500_000_000,
            nbytes=15 * MB,
            in_specs=[sm] + [vm] * 9,
            out_specs=[vm] * 2,
        )(t, after(grads, out1, out2, out3), *xs)
    with jax.named_scope("last_sum"):
        (near,) = plain_call(
            last_sum_body,
            t,
            [after(grads, grad_gate), part_sib[0], left, right, wg, wu],
            [sds((ROWS, COLS))],
            [((ROWS, 2 * HID), BF)]
            + [((ROWS, COLS), BF)] * 3
            + [((COLS, 2 * HID), BF), ((ROWS, COLS), BF)],
            22,
            800_000_000,
            6 * MB,
        )
        near_rows = exchange(near.reshape(16, CAP, COLS))
    with jax.named_scope("finish"):
        far_part, prob_part = call(
            combine_far_body, [sds((TOK, COLS)), sds((8, TOK), F32)], flops=10**8, nbytes=MB
        )(routes_t, far)
        far_part = from_y(far_part, 2)
        probs_all = [prob_part] + [from_y(prob_part, dy) for dy in (1, 2, 3)]
        d_tokens, d_probs = call(
            finish_body, [sds((TOK, COLS)), sds((2, TOK), F32)], flops=10**8, nbytes=MB
        )(routes_t, probs_t, near_rows, far_part, *probs_all)
    return d_tokens, d_probs.T, grad_gate[None], grad_up[None], grad_down[None]


def solution(mesh):
    in_specs = (
        P(("dp", "ctx"), "tensor"),
        P(("dp", "ctx"), "tensor"),
        P(("dp", "ctx"), None),
        P(("dp", "ctx"), None),
        P("ctx", None, ("dp", "tensor")),
        P("ctx", None, ("dp", "tensor")),
        P("ctx", ("dp", "tensor"), None),
    )
    out_specs = (
        P(("dp", "ctx"), "tensor"),
        P(("dp", "ctx"), None),
        P("ctx", None, ("dp", "tensor")),
        P("ctx", None, ("dp", "tensor")),
        P("ctx", ("dp", "tensor"), None),
    )
    return jax.shard_map(
        on_device, mesh=mesh, in_specs=in_specs, out_specs=out_specs, check_vma=False
    )
```

time: 468 us -> 179 us (0.38); the launches traced: 459 us -> 178 us
  waiting for transfers between devices: 242 us -> 49.1 us
  Pallas kernels: 0 us -> 67.5 us
  blocking collectives: 63.8 us -> 0 us
  matrix products: 59.8 us -> 0 us
  local copies, waits for them, and re-layouts: 43.1 us -> 9.27 us
  starting transfers between devices: 32 us -> 49.9 us
  between operations: 14.4 us -> 0.88 us
    all_to_all x5 -> x4, waiting for transfers between devices: 179 us -> 2.11 us  [exchange(): lax.all_to_all(x, ('dp', 'ctx'), split_axis=0, concat_axis=0, tiled=True)]
    pallas_call x0 -> x11, Pallas kernels: none -> 67.5 us  [the longest x6 44.9 us: plain_call(): pl.pallas_call(body, out_shape=outs, in_specs=[pl.BlockSpec(memory_space=...]
    reduce_scatter x1 -> x0, waiting for transfers between devices: 63.4 us -> none  [on_device(): lax.psum_scatter(term, ('dp', 'tensor'), scatter_dimension=0, tiled=True)]
    dot_general x8 -> x0, matrix products: 59.8 us -> none  [the longest x1 10.4 us: expert_rows(): lax.dot_general(grads_in, down_weight, (((1,), (1,)), ((), ())), preferre...]
    ppermute x0 -> x22, waiting for transfers between devices: none -> 46.9 us  [the longest x12 43.8 us: from_y(): lax.ppermute(x, 'tensor', [(i, (i // 2 - dy) % 4 * 2 + i % 2) for i in ra...]
    psum x1 -> x0, blocking collectives: 33.3 us -> none  [on_device(): prob_total = lax.psum(prob_grad, ('dp', 'tensor'))]
    all_gather x2 -> x0, blocking collectives: 30.5 us -> none  [the longest x1 15.4 us: on_device(): lax.all_gather(tokens, 'tensor', axis=1, tiled=True)]
    scatter x3 -> x0, local copies, waits for them, and re-layouts: 20.7 us -> none  [the longest x2 18.6 us: on_device(): jnp.zeros((ctx_size * capacity, features), jnp.bfloat16).at[target]]
  transfers between devices with their start and end apart: 6 -> 26, of which waited for: 3 -> 12; matrix products, arithmetic and copies ran while one was open for 13% -> 1% of each run, Pallas kernels for 0% -> 26%
where the time goes in v1:
time: 179 us; the launch traced here: 178 us
  Pallas kernels  67.5 us (38%)
  starting transfers between devices  49.9 us (28%)
  waiting for transfers between devices  49.1 us (27%)
  local copies, waits for them, and re-layouts  9.27 us (5%)
    pallas_call x6, Pallas kernels, plain_call(): pl.pallas_call(body, out_shape=outs, in_specs=[pl.BlockSpec(memory_space=...  44.9 us
    ppermute x12, waiting for transfers between devices, from_y(): lax.ppermute(x, 'tensor', [(i, (i // 2 - dy) % 4 * 2 + i % 2) for i in ra...  43.8 us
    all_to_all x4, starting transfers between devices, exchange(): lax.all_to_all(x, ('dp', 'ctx'), split_axis=0, concat_axis=0, tiled=True)  30 us
    ppermute x12, starting transfers between devices, from_y(): lax.ppermute(x, 'tensor', [(i, (i // 2 - dy) % 4 * 2 + i % 2) for i in ra...  18.2 us
    pallas_call x1, Pallas kernels, on_device(): call(weights_gate_up_body, [sds((8 * COLS, HID))] * 2, flops=6500000000,...  12.4 us
    unnamed x40, local copies, waits for them, and re-layouts  9.27 us
  transfers between devices with their start and end apart: 26, of which 12 were waited for; matrix products, arithmetic and copies ran while one was open for 1% of the time, Pallas kernels for 26%

profile of v1, /device:TPU:2, one launch (start us, length us, event | category | flops | bytes accessed | tf_op | source)
XLA Modules:
  0.0 177.9 jit_solution(12262681997739434667)
XLA Ops:
  0.6 2.2 %dispatch.3 = bf16[16,64,384]{2,1,0:T(8,128)(2,1)} custom-call(s32[2,128]{1,0:T(2,128)} %bitcast.40, bf16[128,384]{1,0:T(8,128)(2,1)} %tokens.1), custom_call_target="tpu_custom_call" | custom-call | flops 100000000 | bytes 1048576 | tf_op jit(solution)/shard_map/dispatch/pallas_call | solution.py:373
  2.8 8.3 %all-to-all-start = ((bf16[16,64,384]{2,1,0:T(8,128)(2,1)}), bf16[16,64,384]{2,1,0:T(8,128)(2,1)S(1)}, u32[]{:S(2)}, u32[]{:S(2)}) async-start(bf16[16,64,384]{2,1,0:T(8,128)(2,1)} %dispatch.3), calls=%async_computation | async-start | bytes 1572864 | tf_op jit(solution)/shard_map/dispatch/all_to_all | solution.py:363
  11.1 3.2 %collective-permute-start.1 = (bf16[128,384]{1,0:T(8,128)(2,1)}, bf16[128,384]{1,0:T(8,128)(2,1)S(1)}, u32[]{:S(2)}, u32[]{:S(2)}) collective-permute-start(bf16[128,384]{1,0:T(8,128)(2,1)} %g0.1), channel_id=1, source_target_pairs={{0,4},{1,5},{2,6},{3,7},{4,0},{5,1},{6,2},{7,3},{8,12},{9,13},{10,... | collective-permute-start | bytes 294920 | tf_op jit(solution)/shard_map/dispatch/ppermute | solution.py:355
  14.3 1.1 collective-permute-start
  15.4 1.0 collective-permute-start.2
  16.3 1.2 convert_bitcast_fusion.probs
  17.6 0.5 collective-permute-done.1.g2
  18.1 1.2 collective-permute-done.g1
  19.3 2.1 %collective-permute-done.2.g3 = bf16[128,384]{1,0:T(8,128)(2,1)S(1)} collective-permute-done((bf16[128,384]{1,0:T(8,128)(2,1)}, bf16[128,384]{1,0:T(8,128)(2,1)S(1)}, u32[]{:S(2)}, u32[]{:S(2)}) %collective-permute-start.2) | collective-permute-done | bytes 98336 | tf_op jit(solution)/shard_map/dispatch/ppermute | solution.py:355
  21.4 0.6 copy-done.14
  22.1 3.4 %dispatch.2 = bf16[16,64,1536]{2,1,0:T(8,128)(2,1)} custom-call(s32[2,128]{1,0:T(2,128)} %bitcast.41, f32[2,128]{1,0:T(2,128)} %convert_bitcast_fusion.probs, bf16[128,384]{1,0:T(8,128)(2,1)} %g0.1, bf16[128,384]{1,0:T(8,128)(2,1)} %copy-done.13, bf16[128,384]{1,0:T(8,128)(2,1)} %copy-done.12, bf16[128,384]{1,0:T(8,128)(2,1)} %copy-done.14), custom_call_target="tpu_custom_call" | custom-call | flops 200000000 | bytes 4194304 | tf_op jit(solution)/shard_map/dispatch/pallas_call | solution.py:375
  25.5 1.0 copy-done.10
  26.4 7.2 %all-to-all-start.1 = ((bf16[16,64,1536]{2,1,0:T(8,128)(2,1)}), bf16[16,64,1536]{2,1,0:T(8,128)(2,1)S(1)}, u32[]{:S(2)}, u32[]{:S(2)}) async-start(bf16[16,64,1536]{2,1,0:T(8,128)(2,1)} %dispatch.2), calls=%async_computation.1 | async-start | bytes 6291456 | tf_op jit(solution)/shard_map/gather/all_to_all | solution.py:363
  33.6 2.6 %collective-permute-start.4 = (bf16[1024,384]{1,0:T(8,128)(2,1)}, bf16[1024,384]{1,0:T(8,128)(2,1)}, u32[]{:S(2)}, u32[]{:S(2)}) collective-permute-start(bf16[1024,384]{1,0:T(8,128)(2,1)} %bitcast.35), channel_id=1, source_target_pairs={{0,4},{1,5},{2,6},{3,7},{4,0},{5,1},{6,2},{7,3},{8,12},{9,13},{10,... | collective-permute-start | bytes 2359304 | tf_op jit(solution)/shard_map/gather/ppermute | solution.py:355
  36.3 0.9 collective-permute-start.3
  37.2 17.9 %collective-permute-done.5.refs_3_ = bf16[1024,384]{1,0:T(8,128)(2,1)} collective-permute-done((bf16[1024,384]{1,0:T(8,128)(2,1)}, bf16[1024,384]{1,0:T(8,128)(2,1)}, u32[]{:S(2)}, u32[]{:S(2)}) %collective-permute-start.5) | collective-permute-done | bytes 786464 | tf_op jit(solution)/shard_map/gather/ppermute | solution.py:355
  55.1 13.7 %collective-permute-done.4.refs_2_ = bf16[1024,384]{1,0:T(8,128)(2,1)} collective-permute-done((bf16[1024,384]{1,0:T(8,128)(2,1)}, bf16[1024,384]{1,0:T(8,128)(2,1)}, u32[]{:S(2)}, u32[]{:S(2)}) %collective-permute-start.4) | collective-permute-done | bytes 786464 | tf_op jit(solution)/shard_map/gather/ppermute | solution.py:355
  68.8 0.6 collective-permute-done.3.refs_1_
  69.4 2.0 %collective-permute-done.8.refs_6_ = bf16[1024,384]{1,0:T(8,128)(2,1)} collective-permute-done((bf16[1024,384]{1,0:T(8,128)(2,1)}, bf16[1024,384]{1,0:T(8,128)(2,1)}, u32[]{:S(2)}, u32[]{:S(2)}) %collective-permute-start.8) | collective-permute-done | bytes 786464 | tf_op jit(solution)/shard_map/gather/ppermute | solution.py:360
  71.4 1.1 collective-permute-done.7.refs_5_
  72.5 11.3 %forward.1 = (f32[1024,512]{1,0:T(8,128)}, f32[1024,512]{1,0:T(8,128)}, bf16[1024,512]{1,0:T(8,128)(2,1)}) custom-call(s32[1]{0:T(128)} %bitcast.2.t, bf16[1024,384]{1,0:T(8,128)(2,1)} %bitcast.38, bf16[1024,384]{1,0:T(8,128)(2,1)} %collective-permute-done.3.refs_1_, bf16[1024,384]{1,0:T(8,128)(2,1)} %collective-permute-done.4.refs_2_, ...), custom_call_target="tpu_custom_call" | custom-call | flops 6499999744 | bytes 18874368 | tf_op jit(solution)/shard_map/forward/pallas_call | solution.py:86
  83.9 0.4 collective-permute-start.10
  84.3 1.3 copy-done
  85.5 4.9 %backward.2.own = f32[1024,512]{1,0:T(8,128)} custom-call(s32[1]{0:T(128)} %bitcast.2.t, bf16[1024,1536]{1,0:T(8,128)(2,1)} %bitcast.26, bf16[512,3072]{1,0:T(8,128)(2,1)} %bitcast.28), custom_call_target="tpu_custom_call" | custom-call | flops 1600000000 | bytes 7340032 | tf_op jit(solution)/shard_map/backward/pallas_call | solution.py:86
  90.5 1.7 copy-done.3
  92.2 10.2 %backward.3 = (bf16[1024,1024]{1,0:T(8,128)(2,1)}, bf16[1024,128]{1,0:T(8,128)(2,1)}, bf16[1024,384]{1,0:T(8,128)(2,1)}, bf16[1024,384]{1,0:T(8,128)(2,1)}, bf16...) custom-call(s32[1]{0:T(128)} %bitcast.2.t, bf16[1024,1536]{1,0:T(8,128)(2,1)} %copy-done.3, f32[1024,512]{1,0:T(8,128)} %backward.2.own, ...), custom_call_target="tpu_custom_call" | custom-call | flops 4800000000 | bytes 25165824 | tf_op jit(solution)/shard_map/backward/pallas_call | solution.py:86
  103.5 7.5 %weights_down.1 = bf16[512,3072]{1,0:T(8,128)(2,1)} custom-call(s32[1]{0:T(128)} %bitcast.2.t, bf16[1024,512]{1,0:T(8,128)(2,1)} %get-tuple-element.35.hidden, bf16[1024,1536]{1,0:T(8,128)(2,1)} %bitcast.27, bf16[1024,1536]{1,0:T(8,128)(2,1)} %copy-done.3), custom_call_target="tpu_custom_call" | custom-call | flops 3300000000 | bytes 10485760 | tf_op jit(solution)/shard_map/weights_down/pallas_call | solution.py:86
  111.1 0.6 copy-done.11
  112.3 0.9 copy-done.8
  113.2 6.6 %sums.1 = (bf16[1024,384]{1,0:T(8,128)(2,1)}, bf16[1024,512]{1,0:T(8,128)(2,1)}, bf16[1024,384]{1,0:T(8,128)(2,1)}) custom-call(s32[1]{0:T(128)} %bitcast.2.t, bf16[1024,1024]{1,0:T(8,128)(2,1)} %get-tuple-element.46.grads, bf16[1024,128]{1,0:T(8,128)(2,1)} %get-tuple-element.37.prob, bf16[1024,128]{1,0:T(8,128)(2,1)} %copy-done.11, ...), custom_call_target="tpu_custom_call" | custom-call | flops 2400000000 | bytes 10485760 | tf_op jit(solution)/shard_map/sums/pallas_call | solution.py:86
  119.8 7.3 %all-to-all-start.3 = ((bf16[16,64,512]{2,1,0:T(8,128)(2,1)}), bf16[16,64,512]{2,1,0:T(8,128)(2,1)S(1)}, u32[]{:S(2)}, u32[]{:S(2)}) async-start(bf16[16,64,512]{2,1,0:T(8,128)(2,1)} %bitcast.33), calls=%async_computation.3 | async-start | bytes 2097152 | tf_op jit(solution)/shard_map/sums/all_to_all | solution.py:363
  127.2 0.8 collective-permute-start.16
  128.0 2.5 %collective-permute-start.17 = (bf16[1024,384]{1,0:T(8,128)(2,1)}, bf16[1024,384]{1,0:T(8,128)(2,1)S(1)}, u32[]{:S(2)}, u32[]{:S(2)}) collective-permute-start(bf16[1024,384]{1,0:T(8,128)(2,1)} %get-tuple-element.43), channel_id=1, source_target_pairs={{0,6},{1,7},{2,0},{3,1},{4,2},{5,3},{6,4},{7,5},{8,14},{9,15},{10,... | collective-permute-start | bytes 2359304 | tf_op jit(solution)/shard_map/sums/ppermute | solution.py:355
  130.5 12.4 %weights_gate_up.1 = (bf16[3072,512]{1,0:T(8,128)(2,1)}, bf16[3072,512]{1,0:T(8,128)(2,1)}) custom-call(s32[1]{0:T(128)} %bitcast.2.t, bf16[1024,1024]{1,0:T(8,128)(2,1)} %get-tuple-element.46.grads, bf16[1024,384]{1,0:T(8,128)(2,1)} %bitcast.39, bf16[1024,384]{1,0:T(8,128)(2,1)} %collective-permute-done.3.refs_1_, ...), custom_call_target="tpu_custom_call" | custom-call | flops 6499999744 | bytes 15728640 | tf_op jit(solution)/shard_map/weights_gate_up/pallas_call | solution.py:456
  142.9 5.7 %collective-permute-done.16.left = bf16[1024,384]{1,0:T(8,128)(2,1)S(1)} collective-permute-done((bf16[1024,384]{1,0:T(8,128)(2,1)}, bf16[1024,384]{1,0:T(8,128)(2,1)S(1)}, u32[]{:S(2)}, u32[]{:S(2)}) %collective-permute-start.16) | collective-permute-done | bytes 786464 | tf_op jit(solution)/shard_map/sums/ppermute | solution.py:355
  148.6 0.9 copy-done.7
  149.5 0.9 copy-done.9
  150.4 4.2 %last_sum.1 = bf16[1024,384]{1,0:T(8,128)(2,1)} custom-call(s32[1]{0:T(128)} %bitcast.2.t, bf16[1024,1024]{1,0:T(8,128)(2,1)} %get-tuple-element.46.grads, bf16[1024,384]{1,0:T(8,128)(2,1)} %copy-done.5, bf16[1024,384]{1,0:T(8,128)(2,1)} %copy-done.7, bf16[1024,384]{1,0:T(8,128)(2,1)} %copy-done.9, bf16[3072,512]{1,0:T(8,128)(2,1)} %bitcast.20, ...), custom_call_target="tpu_custom_call" | custom-call | flops 800000000 | bytes 6291456 | tf_op jit(solution)/shard_map/last_sum/pallas_call | solution.py:86
  154.6 7.2 %all-to-all-start.2 = ((bf16[16,64,384]{2,1,0:T(8,128)(2,1)}), bf16[16,64,384]{2,1,0:T(8,128)(2,1)S(1)}, u32[]{:S(2)}, u32[]{:S(2)}) async-start(bf16[16,64,384]{2,1,0:T(8,128)(2,1)} %bitcast.31), calls=%async_computation.2 | async-start | bytes 1572864 | tf_op jit(solution)/shard_map/last_sum/all_to_all | solution.py:363
  161.8 2.4 %finish.2 = (bf16[128,384]{1,0:T(8,128)(2,1)}, f32[8,128]{1,0:T(8,128)}) custom-call(s32[2,128]{1,0:T(2,128)} %bitcast.42, bf16[1024,512]{1,0:T(8,128)(2,1)} %bitcast.30), custom_call_target="tpu_custom_call" | custom-call | flops 100000000 | bytes 1048576 | tf_op jit(solution)/shard_map/finish/pallas_call | solution.py:479
  164.2 1.2 collective-permute-start.18
  165.4 1.7 collective-permute-start.21
  167.2 0.7 collective-permute-start.20
  167.9 2.5 %collective-permute-start.19 = (f32[8,128]{1,0:T(8,128)}, f32[8,128]{1,0:T(8,128)S(1)}, u32[]{:S(2)}, u32[]{:S(2)}) collective-permute-start(f32[8,128]{1,0:T(8,128)} %get-tuple-element.49.q0), channel_id=1, source_target_pairs={{0,6},{1,7},{2,0},{3,1},{4,2},{5,3},{6,4},{7,5},{8,14},{9,15},{10,... | collective-permute-start | bytes 12296 | tf_op jit(solution)/shard_map/finish/ppermute | solution.py:355
  170.7 1.8 %collective-permute-done.20.q2 = f32[8,128]{1,0:T(8,128)S(1)} collective-permute-done((f32[8,128]{1,0:T(8,128)}, f32[8,128]{1,0:T(8,128)S(1)}, u32[]{:S(2)}, u32[]{:S(2)}) %collective-permute-start.20) | collective-permute-done | bytes 4128 | tf_op jit(solution)/shard_map/finish/ppermute | solution.py:355
  172.5 2.1 %all-to-all-done.2 = bf16[16,64,384]{2,1,0:T(8,128)(2,1)S(1)} async-done(((bf16[16,64,384]{2,1,0:T(8,128)(2,1)}), bf16[16,64,384]{2,1,0:T(8,128)(2,1)S(1)}, u32[]{:S(2)}, u32[]{:S(2)}) %all-to-all-start.2) | async-done | bytes 786464 | tf_op jit(solution)/shard_map/last_sum/all_to_all | solution.py:363
  174.6 0.9 copy-done.2
  175.5 2.3 %finish.3 = (bf16[128,384]{1,0:T(8,128)(2,1)}, f32[2,128]{1,0:T(2,128)}) custom-call(s32[2,128]{1,0:T(2,128)} %bitcast.43, f32[2,128]{1,0:T(2,128)} %convert_bitcast_fusion.probs, bf16[1024,384]{1,0:T(8,128)(2,1)} %bitcast.32, bf16[128,384]{1,0:T(8,128)(2,1)} %copy-done.15, f32[8,128]{1,0:T(8,128)} %get-tuple-element.49.q0, f32[8,128]{1,0:T(8,128)} %copy-done.18, ...), custom_call_target="tpu_custom_call" | custom-call | flops 100000000 | bytes 1048576 | tf_op jit(solution)/shard_map/finish/pallas_call | solution.py:484
  (56 shorter events, 2.1 us)
Async XLA Ops:
  2.8 22.7 %all-to-all-start = ((bf16[16,64,384]{2,1,0:T(8,128)(2,1)}), bf16[16,64,384]{2,1,0:T(8,128)(2,1)S(1)}, u32[]{:S(2)}, u32[]{:S(2)}) async-start(bf16[16,64,384]{2,1,0:T(8,128)(2,1)} %dispatch.3), calls=%async_computation | async-start | bytes 1572864 | tf_op jit(solution)/shard_map/dispatch/all_to_all | solution.py:363
  11.1 7.0 %collective-permute-start.1 = (bf16[128,384]{1,0:T(8,128)(2,1)}, bf16[128,384]{1,0:T(8,128)(2,1)S(1)}, u32[]{:S(2)}, u32[]{:S(2)}) collective-permute-start(bf16[128,384]{1,0:T(8,128)(2,1)} %g0.1), channel_id=1, source_target_pairs={{0,4},{1,5},{2,6},{3,7},{4,0},{5,1},{6,2},{7,3},{8,12},{9,13},{10,... | collective-permute-start | bytes 294920 | tf_op jit(solution)/shard_map/dispatch/ppermute | solution.py:355
  14.3 5.0 %collective-permute-start = (bf16[128,384]{1,0:T(8,128)(2,1)}, bf16[128,384]{1,0:T(8,128)(2,1)S(1)}, u32[]{:S(2)}, u32[]{:S(2)}) collective-permute-start(bf16[128,384]{1,0:T(8,128)(2,1)} %g0.1), channel_id=1, source_target_pairs={{0,6},{1,7},{2,0},{3,1},{4,2},{5,3},{6,4},{7,5},{8,14},{9,15},{10,... | collective-permute-start | bytes 294920 | tf_op jit(solution)/shard_map/dispatch/ppermute | solution.py:355
  15.4 6.0 %collective-permute-start.2 = (bf16[128,384]{1,0:T(8,128)(2,1)}, bf16[128,384]{1,0:T(8,128)(2,1)S(1)}, u32[]{:S(2)}, u32[]{:S(2)}) collective-permute-start(bf16[128,384]{1,0:T(8,128)(2,1)} %g0.1), channel_id=1, source_target_pairs={{0,2},{1,3},{2,4},{3,5},{4,6},{5,7},{6,0},{7,1},{8,10},{9,11},{10,... | collective-permute-start | bytes 294920 | tf_op jit(solution)/shard_map/dispatch/ppermute | solution.py:355
  18.1 3.3 %copy-start.12 = (bf16[128,384]{1,0:T(8,128)(2,1)}, bf16[128,384]{1,0:T(8,128)(2,1)S(1)}, u32[]{:S(2)}) copy-start(bf16[128,384]{1,0:T(8,128)(2,1)S(1)} %collective-permute-done.1.g2) | copy-start | bytes 294916
  19.3 2.1 %copy-start.13 = (bf16[128,384]{1,0:T(8,128)(2,1)}, bf16[128,384]{1,0:T(8,128)(2,1)S(1)}, u32[]{:S(2)}) copy-start(bf16[128,384]{1,0:T(8,128)(2,1)S(1)} %collective-permute-done.g1) | copy-start | bytes 294916
  21.4 0.6 copy-start.14
  25.5 1.0 copy-start.10
  26.4 57.5 %all-to-all-start.1 = ((bf16[16,64,1536]{2,1,0:T(8,128)(2,1)}), bf16[16,64,1536]{2,1,0:T(8,128)(2,1)S(1)}, u32[]{:S(2)}, u32[]{:S(2)}) async-start(bf16[16,64,1536]{2,1,0:T(8,128)(2,1)} %dispatch.2), calls=%async_computation.1 | async-start | bytes 6291456 | tf_op jit(solution)/shard_map/gather/all_to_all | solution.py:363
  33.6 21.4 %collective-permute-start.5 = (bf16[1024,384]{1,0:T(8,128)(2,1)}, bf16[1024,384]{1,0:T(8,128)(2,1)}, u32[]{:S(2)}, u32[]{:S(2)}) collective-permute-start(bf16[1024,384]{1,0:T(8,128)(2,1)} %bitcast.34), channel_id=1, source_target_pairs={{0,2},{1,3},{2,4},{3,5},{4,6},{5,7},{6,0},{7,1},{8,10},{9,11},{10,... | collective-permute-start | bytes 2359304 | tf_op jit(solution)/shard_map/gather/ppermute | solution.py:355
  33.6 35.1 %collective-permute-start.4 = (bf16[1024,384]{1,0:T(8,128)(2,1)}, bf16[1024,384]{1,0:T(8,128)(2,1)}, u32[]{:S(2)}, u32[]{:S(2)}) collective-permute-start(bf16[1024,384]{1,0:T(8,128)(2,1)} %bitcast.35), channel_id=1, source_target_pairs={{0,4},{1,5},{2,6},{3,7},{4,0},{5,1},{6,2},{7,3},{8,12},{9,13},{10,... | collective-permute-start | bytes 2359304 | tf_op jit(solution)/shard_map/gather/ppermute | solution.py:355
  36.3 33.1 %collective-permute-start.3 = (bf16[1024,384]{1,0:T(8,128)(2,1)}, bf16[1024,384]{1,0:T(8,128)(2,1)}, u32[]{:S(2)}, u32[]{:S(2)}) collective-permute-start(bf16[1024,384]{1,0:T(8,128)(2,1)} %bitcast.36), channel_id=1, source_target_pairs={{0,6},{1,7},{2,0},{3,1},{4,2},{5,3},{6,4},{7,5},{8,14},{9,15},{10,... | collective-permute-start | bytes 2359304 | tf_op jit(solution)/shard_map/gather/ppermute | solution.py:355
  37.2 32.2 %collective-permute-start.6 = (bf16[1024,384]{1,0:T(8,128)(2,1)}, bf16[1024,384]{1,0:T(8,128)(2,1)}, u32[]{:S(2)}, u32[]{:S(2)}) collective-permute-start(bf16[1024,384]{1,0:T(8,128)(2,1)} %bitcast.37), channel_id=1, source_target_pairs={{0,1},{1,0},{2,3},{3,2},{4,5},{5,4},{6,7},{7,6},{8,9},{9,8},{10,11... | collective-permute-start | bytes 2359304 | tf_op jit(solution)/shard_map/gather/ppermute | solution.py:360
  55.1 14.3 %collective-permute-start.9 = (bf16[1024,384]{1,0:T(8,128)(2,1)}, bf16[1024,384]{1,0:T(8,128)(2,1)}, u32[]{:S(2)}, u32[]{:S(2)}) collective-permute-start(bf16[1024,384]{1,0:T(8,128)(2,1)} %collective-permute-done.5.refs_3_), channel_id=1, source_target_pairs={{0,1},{1,0},{2,3},{3,2},{4,5},{5,4},{6,7},{7,6},{8,9},{9,8},{10,11... | collective-permute-start | bytes 2359304 | tf_op jit(solution)/shard_map/gather/ppermute | solution.py:360
  68.8 2.6 %collective-permute-start.8 = (bf16[1024,384]{1,0:T(8,128)(2,1)}, bf16[1024,384]{1,0:T(8,128)(2,1)}, u32[]{:S(2)}, u32[]{:S(2)}) collective-permute-start(bf16[1024,384]{1,0:T(8,128)(2,1)} %collective-permute-done.4.refs_2_), channel_id=1, source_target_pairs={{0,1},{1,0},{2,3},{3,2},{4,5},{5,4},{6,7},{7,6},{8,9},{9,8},{10,11... | collective-permute-start | bytes 2359304 | tf_op jit(solution)/shard_map/gather/ppermute | solution.py:360
  69.4 3.1 %collective-permute-start.7 = (bf16[1024,384]{1,0:T(8,128)(2,1)}, bf16[1024,384]{1,0:T(8,128)(2,1)}, u32[]{:S(2)}, u32[]{:S(2)}) collective-permute-start(bf16[1024,384]{1,0:T(8,128)(2,1)} %collective-permute-done.3.refs_1_), channel_id=1, source_target_pairs={{0,1},{1,0},{2,3},{3,2},{4,5},{5,4},{6,7},{7,6},{8,9},{9,8},{10,11... | collective-permute-start | bytes 2359304 | tf_op jit(solution)/shard_map/gather/ppermute | solution.py:360
  83.9 1.7 copy-start
  83.9 6.6 %collective-permute-start.10 = (bf16[1024,1536]{1,0:T(8,128)(2,1)S(1)}, bf16[1024,1536]{1,0:T(8,128)(2,1)S(1)}, u32[]{:S(2)}, u32[]{:S(2)}) collective-permute-start(bf16[1024,1536]{1,0:T(8,128)(2,1)S(1)} %bitcast.25), channel_id=1, source_target_pairs={{0,1},{1,0},{2,3},{3,2},{4,5},{5,4},{6,7},{7,6},{8,9},{9,8},{10,11... | collective-permute-start | bytes 9437192 | tf_op jit(solution)/shard_map/forward/ppermute | solution.py:360
  90.5 1.7 copy-start.3
  102.4 8.7 %collective-permute-start.12 = (bf16[1024,384]{1,0:T(8,128)(2,1)}, bf16[1024,384]{1,0:T(8,128)(2,1)S(1)}, u32[]{:S(2)}, u32[]{:S(2)}) collective-permute-start(bf16[1024,384]{1,0:T(8,128)(2,1)} %get-tuple-element.38), channel_id=1, source_target_pairs={{0,1},{1,0},{2,3},{3,2},{4,5},{5,4},{6,7},{7,6},{8,9},{9,8},{10,11... | collective-permute-start | bytes 2359304 | tf_op jit(solution)/shard_map/backward/ppermute | solution.py:360
  102.6 8.5 %collective-permute-start.13 = (bf16[1024,384]{1,0:T(8,128)(2,1)}, bf16[1024,384]{1,0:T(8,128)(2,1)S(1)}, u32[]{:S(2)}, u32[]{:S(2)}) collective-permute-start(bf16[1024,384]{1,0:T(8,128)(2,1)} %get-tuple-element.39), channel_id=1, source_target_pairs={{0,1},{1,0},{2,3},{3,2},{4,5},{5,4},{6,7},{7,6},{8,9},{9,8},{10,11... | collective-permute-start | bytes 2359304 | tf_op jit(solution)/shard_map/backward/ppermute | solution.py:360
  103.0 8.1 %collective-permute-start.14 = (bf16[1024,384]{1,0:T(8,128)(2,1)}, bf16[1024,384]{1,0:T(8,128)(2,1)S(1)}, u32[]{:S(2)}, u32[]{:S(2)}) collective-permute-start(bf16[1024,384]{1,0:T(8,128)(2,1)} %get-tuple-element.40), channel_id=1, source_target_pairs={{0,1},{1,0},{2,3},{3,2},{4,5},{5,4},{6,7},{7,6},{8,9},{9,8},{10,11... | collective-permute-start | bytes 2359304 | tf_op jit(solution)/shard_map/backward/ppermute | solution.py:360
  103.1 8.0 %collective-permute-start.11 = (bf16[1024,128]{1,0:T(8,128)(2,1)}, bf16[1024,128]{1,0:T(8,128)(2,1)S(1)}, u32[]{:S(2)}, u32[]{:S(2)}) collective-permute-start(bf16[1024,128]{1,0:T(8,128)(2,1)} %get-tuple-element.37.prob), channel_id=1, source_target_pairs={{0,1},{1,0},{2,3},{3,2},{4,5},{5,4},{6,7},{7,6},{8,9},{9,8},{10,11... | collective-permute-start | bytes 786440 | tf_op jit(solution)/shard_map/backward/ppermute | solution.py:360
  111.0 16.1 %copy-start.19 = (bf16[1024,384]{1,0:T(8,128)(2,1)S(1)}, bf16[1024,384]{1,0:T(8,128)(2,1)}, u32[]{:S(2)}) copy-start(bf16[1024,384]{1,0:T(8,128)(2,1)} %get-tuple-element.47) | copy-start | bytes 2359300
  111.0 0.7 copy-start.11
  111.1 0.9 copy-start.4
  111.1 1.2 copy-start.6
  112.3 0.9 copy-start.8
  119.8 34.7 %all-to-all-start.3 = ((bf16[16,64,512]{2,1,0:T(8,128)(2,1)}), bf16[16,64,512]{2,1,0:T(8,128)(2,1)S(1)}, u32[]{:S(2)}, u32[]{:S(2)}) async-start(bf16[16,64,512]{2,1,0:T(8,128)(2,1)} %bitcast.33), calls=%async_computation.3 | async-start | bytes 2097152 | tf_op jit(solution)/shard_map/sums/all_to_all | solution.py:363
  127.1 15.8 %collective-permute-start.15 = (bf16[1024,384]{1,0:T(8,128)(2,1)S(1)}, bf16[1024,384]{1,0:T(8,128)(2,1)S(1)}, u32[]{:S(2)}, u32[]{:S(2)}) collective-permute-start(bf16[1024,384]{1,0:T(8,128)(2,1)S(1)} %copy-done.19), channel_id=1, source_target_pairs={{0,1},{1,0},{2,3},{3,2},{4,5},{5,4},{6,7},{7,6},{8,9},{9,8},{10,11... | collective-permute-start | bytes 2359304 | tf_op jit(solution)/shard_map/backward/ppermute | solution.py:360
  127.2 21.4 %collective-permute-start.16 = (bf16[1024,384]{1,0:T(8,128)(2,1)}, bf16[1024,384]{1,0:T(8,128)(2,1)S(1)}, u32[]{:S(2)}, u32[]{:S(2)}) collective-permute-start(bf16[1024,384]{1,0:T(8,128)(2,1)} %get-tuple-element.41), channel_id=1, source_target_pairs={{0,2},{1,3},{2,4},{3,5},{4,6},{5,7},{6,0},{7,1},{8,10},{9,11},{10,... | collective-permute-start | bytes 2359304 | tf_op jit(solution)/shard_map/sums/ppermute | solution.py:355
  128.0 20.6 %collective-permute-start.17 = (bf16[1024,384]{1,0:T(8,128)(2,1)}, bf16[1024,384]{1,0:T(8,128)(2,1)S(1)}, u32[]{:S(2)}, u32[]{:S(2)}) collective-permute-start(bf16[1024,384]{1,0:T(8,128)(2,1)} %get-tuple-element.43), channel_id=1, source_target_pairs={{0,6},{1,7},{2,0},{3,1},{4,2},{5,3},{6,4},{7,5},{8,14},{9,15},{10,... | collective-permute-start | bytes 2359304 | tf_op jit(solution)/shard_map/sums/ppermute | solution.py:355
  142.9 5.7 %copy-start.5 = (bf16[1024,384]{1,0:T(8,128)(2,1)}, bf16[1024,384]{1,0:T(8,128)(2,1)S(1)}, u32[]{:S(2)}) copy-start(bf16[1024,384]{1,0:T(8,128)(2,1)S(1)} %collective-permute-done.15.s0) | copy-start | bytes 2359300
  148.6 0.9 copy-start.7
  149.5 0.9 copy-start.9
  154.6 7.2 %copy-start.1 = (bf16[16,64,512]{2,1,0:T(8,128)(2,1)}, bf16[16,64,512]{2,1,0:T(8,128)(2,1)S(1)}, u32[]{:S(2)}) copy-start(bf16[16,64,512]{2,1,0:T(8,128)(2,1)S(1)} %all-to-all-done.3) | copy-start | bytes 3145732
  154.6 20.0 %all-to-all-start.2 = ((bf16[16,64,384]{2,1,0:T(8,128)(2,1)}), bf16[16,64,384]{2,1,0:T(8,128)(2,1)S(1)}, u32[]{:S(2)}, u32[]{:S(2)}) async-start(bf16[16,64,384]{2,1,0:T(8,128)(2,1)} %bitcast.31), calls=%async_computation.2 | async-start | bytes 1572864 | tf_op jit(solution)/shard_map/last_sum/all_to_all | solution.py:363
  164.2 8.3 %collective-permute-start.18 = (bf16[128,384]{1,0:T(8,128)(2,1)}, bf16[128,384]{1,0:T(8,128)(2,1)S(1)}, u32[]{:S(2)}, u32[]{:S(2)}) collective-permute-start(bf16[128,384]{1,0:T(8,128)(2,1)} %get-tuple-element.48), channel_id=1, source_target_pairs={{0,4},{1,5},{2,6},{3,7},{4,0},{5,1},{6,2},{7,3},{8,12},{9,13},{10,... | collective-permute-start | bytes 294920 | tf_op jit(solution)/shard_map/finish/ppermute | solution.py:355
  165.4 5.2 %collective-permute-start.21 = (f32[8,128]{1,0:T(8,128)}, f32[8,128]{1,0:T(8,128)S(1)}, u32[]{:S(2)}, u32[]{:S(2)}) collective-permute-start(f32[8,128]{1,0:T(8,128)} %get-tuple-element.49.q0), channel_id=1, source_target_pairs={{0,2},{1,3},{2,4},{3,5},{4,6},{5,7},{6,0},{7,1},{8,10},{9,11},{10,... | collective-permute-start | bytes 12296 | tf_op jit(solution)/shard_map/finish/ppermute | solution.py:355
  167.2 5.3 %collective-permute-start.20 = (f32[8,128]{1,0:T(8,128)}, f32[8,128]{1,0:T(8,128)S(1)}, u32[]{:S(2)}, u32[]{:S(2)}) collective-permute-start(f32[8,128]{1,0:T(8,128)} %get-tuple-element.49.q0), channel_id=1, source_target_pairs={{0,4},{1,5},{2,6},{3,7},{4,0},{5,1},{6,2},{7,3},{8,12},{9,13},{10,... | collective-permute-start | bytes 12296 | tf_op jit(solution)/shard_map/finish/ppermute | solution.py:355
  167.9 4.6 %collective-permute-start.19 = (f32[8,128]{1,0:T(8,128)}, f32[8,128]{1,0:T(8,128)S(1)}, u32[]{:S(2)}, u32[]{:S(2)}) collective-permute-start(f32[8,128]{1,0:T(8,128)} %get-tuple-element.49.q0), channel_id=1, source_target_pairs={{0,6},{1,7},{2,0},{3,1},{4,2},{5,3},{6,4},{7,5},{8,14},{9,15},{10,... | collective-permute-start | bytes 12296 | tf_op jit(solution)/shard_map/finish/ppermute | solution.py:355
  170.7 4.0 %copy-start.16 = (f32[8,128]{1,0:T(8,128)}, f32[8,128]{1,0:T(8,128)S(1)}, u32[]{:S(2)}) copy-start(f32[8,128]{1,0:T(8,128)S(1)} %collective-permute-done.21.q3) | copy-start | bytes 12292
  172.5 2.1 %copy-start.17 = (f32[8,128]{1,0:T(8,128)}, f32[8,128]{1,0:T(8,128)S(1)}, u32[]{:S(2)}) copy-start(f32[8,128]{1,0:T(8,128)S(1)} %collective-permute-done.20.q2) | copy-start | bytes 12292
  172.5 2.1 %copy-start.18 = (f32[8,128]{1,0:T(8,128)}, f32[8,128]{1,0:T(8,128)S(1)}, u32[]{:S(2)}) copy-start(f32[8,128]{1,0:T(8,128)S(1)} %collective-permute-done.19.q1) | copy-start | bytes 12292
  172.5 2.1 %copy-start.15 = (bf16[128,384]{1,0:T(8,128)(2,1)}, bf16[128,384]{1,0:T(8,128)(2,1)S(1)}, u32[]{:S(2)}) copy-start(bf16[128,384]{1,0:T(8,128)(2,1)S(1)} %collective-permute-done.18.far) | copy-start | bytes 294916
  174.6 0.9 copy-start.2

commit v2 on v1

v2 whole, which is shorter than its diff:
```python
import jax
import jax.numpy as jnp
from jax import lax
from jax.experimental import pallas as pl
from jax.experimental.pallas import tpu as pltpu
from jax.sharding import PartitionSpec as P

BF = jnp.bfloat16
F32 = jnp.float32
VMEM_LIMIT = 56 * 1024 * 1024
EXPERTS = 8
CAP = 64
EARLY = 32
TOK = 128
COLS = 384
ROWS = 1024
HID = 512
NT = (((1,), (1,)), ((), ()))
TN = (((0,), (0,)), ((), ()))


def dot(a, b, dims=(((1,), (0,)), ((), ()))):
    return lax.dot_general(a, b, dims, preferred_element_type=F32)


def call(body, outs, grid=None, scratch=(), flops=0, nbytes=0, **specs):
    params = dict(vmem_limit_bytes=VMEM_LIMIT)
    return pl.pallas_call(
        body,
        out_shape=outs,
        compiler_params=pltpu.CompilerParams(**params),
        cost_estimate=pl.CostEstimate(flops=flops, bytes_accessed=nbytes, transcendentals=0),
        **specs,
    )


def sds(shape, dtype=BF):
    return jax.ShapeDtypeStruct(shape, dtype)


def slot_masks(routes):
    expert = lax.broadcasted_iota(jnp.int32, (EXPERTS, TOK), 0)
    first = routes[0:1, :] == expert
    second = routes[1:2, :] == expert
    named = jnp.where(first | second, 1.0, 0.0).astype(F32)
    before = lax.broadcasted_iota(jnp.int32, (TOK, TOK), 0)
    after = lax.broadcasted_iota(jnp.int32, (TOK, TOK), 1)
    earlier = jnp.where(before < after, 1.0, 0.0).astype(BF)
    rank = dot(named.astype(BF), earlier)
    slot = jnp.where(named > 0.0, rank, -1.0)
    return first, second, slot


def one_hot(slot, expert):
    place = lax.broadcasted_iota(jnp.int32, (CAP, TOK), 0).astype(F32)
    return jnp.where(slot[expert : expert + 1, :] == place, 1.0, 0.0)


def dispatch_x_body(routes, tokens, out):
    _, _, slot = slot_masks(routes[...])
    select = jnp.concatenate([one_hot(slot, e) for e in range(EXPERTS)], axis=0).astype(BF)
    rows = dot(select, tokens[...]).astype(BF).reshape(EXPERTS, CAP, COLS)
    out[0:EXPERTS] = rows
    out[EXPERTS : 2 * EXPERTS] = rows


def dispatch_g_body(routes, probs, g0, g1, g2, g3, out):
    first, _, slot = slot_masks(routes[...])
    p = probs[...].astype(F32)
    weight = jnp.where(first, p[0:1, :], p[1:2, :])
    select = jnp.concatenate(
        [one_hot(slot, e) * weight[e : e + 1, :] for e in range(EXPERTS)], axis=0
    ).astype(BF)
    for i, g in enumerate((g0, g1, g2, g3)):
        rows = dot(select, g[...]).astype(BF).reshape(EXPERTS, CAP, COLS)
        out[0:EXPERTS, :, i * COLS : (i + 1) * COLS] = rows
        out[EXPERTS : 2 * EXPERTS, :, i * COLS : (i + 1) * COLS] = rows


def slice_of(t, dy, sibling):
    core = t % 2
    core = 1 - core if sibling else core
    return ((t // 2 + dy) % 4) * 2 + core


def plain_call(body, t, ins, outs, scratch, copies, flops, nbytes):
    anywhere = pl.BlockSpec(memory_space=pltpu.HBM)
    return pl.pallas_call(
        body,
        out_shape=outs,
        in_specs=[pl.BlockSpec(memory_space=pltpu.SMEM)] + [anywhere] * len(ins),
        out_specs=[anywhere] * len(outs),
        scratch_shapes=[pltpu.VMEM(shape, dtype) for shape, dtype in scratch]
        + [pltpu.SemaphoreType.DMA((copies,))],
        compiler_params=pltpu.CompilerParams(vmem_limit_bytes=VMEM_LIMIT),
        cost_estimate=pl.CostEstimate(flops=flops, bytes_accessed=nbytes, transcendentals=0),
    )(t, *ins)


class Copies:
    def __init__(self, sems):
        self.sems, self.used = sems, 0

    def start(self, src, dst):
        copy = pltpu.make_async_copy(src, dst, self.sems.at[self.used])
        self.used += 1
        copy.start()
        return copy


def wait_all(copies):
    for copy in copies:
        copy.wait()


def slice_at(t, dy, sibling):
    return pl.ds(pl.multiple_of(slice_of(t[0], dy, sibling) * COLS, COLS), COLS)


def lanes(dy):
    return slice(dy * COLS, (dy + 1) * COLS)


def down_columns(copies, t, wd, into, sibling):
    return [
        copies.start(
            wd.at[:, pl.ds(pl.multiple_of(slice_of(t[0], dy, sibling) * COLS, 128), COLS)],
            into.at[:, lanes(dy)],
        )
        for dy in range(4)
    ]


def gate_up_rows(copies, t, wg, wu, into, steps, sibling):
    started = []
    for i, dy in enumerate(steps):
        at = slice_at(t, dy, sibling)
        started.append(copies.start(wg.at[at, :], into.at[lanes(i), 0:HID]))
        started.append(copies.start(wu.at[at, :], into.at[lanes(i), HID : 2 * HID]))
    return started


def chunks(rows):
    return [slice(r, r + rows) for r in range(0, ROWS, rows)]


def split_lanes(*values):
    lane = lax.broadcasted_iota(jnp.int32, values[0].shape[:-1] + (128,), values[0].ndim - 1)
    total = jnp.zeros(lane.shape, F32)
    for i, value in enumerate(values):
        upper = value.astype(BF).astype(F32)
        total = jnp.where(lane == 2 * i, upper, total)
        total = jnp.where(lane == 2 * i + 1, value - upper, total)
    return total.astype(BF)


def back_body(t, own, sib, act, slope, hidden, wd, wg, wu, grads, prob, *refs):
    parts = refs[:4]
    own_v, sib_v, act_v, slope_v, hidden_v, wd_o, wd_s, w_v, grads_v, prob_v, part_v, sems = refs[4:]
    copies = Copies(sems)
    pairs = ((own, own_v), (sib, sib_v), (act, act_v), (slope, slope_v), (hidden, hidden_v))
    rows = chunks(256)
    wd_in = down_columns(copies, t, wd, wd_o, False)
    ins = [[copies.start(a.at[rows[0]], b.at[rows[0]]) for a, b in pairs]]
    wd_in += down_columns(copies, t, wd, wd_s, True)
    w_in = gate_up_rows(copies, t, wg, wu, w_v, range(4), True)
    ins += [[copies.start(a.at[c], b.at[c]) for a, b in pairs] for c in rows[1:]]
    done = []
    for i, c in enumerate(rows):
        wait_all(ins[i])
        if i == 0:
            wait_all(wd_in[:4])
        back = dot(own_v[c], wd_o[...], NT)
        if i == 0:
            wait_all(wd_in[4:])
        back += dot(sib_v[c], wd_s[...], NT)
        prob_v[c] = split_lanes(
            jnp.sum(hidden_v[c].astype(F32) * back, axis=1, keepdims=True)
        )
        grads_v[c, 0:HID] = (back * slope_v[c]).astype(BF)
        grads_v[c, HID : 2 * HID] = (back * act_v[c]).astype(BF)
        if i == 0:
            wait_all(w_in)
        part_v[c] = dot(grads_v[c], w_v[...], NT).astype(BF)
        done.append(copies.start(grads_v.at[c], grads.at[c]))
        done.append(copies.start(prob_v.at[c], prob.at[c]))
        for dy in range(4):
            done.append(copies.start(part_v.at[c, lanes(dy)], parts[dy].at[c]))
    wait_all(done)


def sums_body(t, grads, prob, prob_sib, s0, s1, s2, s3, wg, wu, early, *refs):
    late, (grads_v, prob_v, sib_v) = refs[:4], refs[4:7]
    s_v, w_v, early_v, late_v, sems = refs[7:]
    copies = Copies(sems)
    w_in = gate_up_rows(copies, t, wg, wu, w_v, range(4), False)
    rows = chunks(256)
    ins = [
        [copies.start(a.at[c], b.at[c]) for a, b in ((grads, grads_v), (prob, prob_v), (prob_sib, sib_v))]
        + [copies.start(s.at[c], s_v.at[dy, c]) for dy, s in enumerate((s0, s1, s2, s3))]
        for c in rows
    ]
    wait_all(w_in)
    done = []
    for i, (c, started) in enumerate(zip(rows, ins)):
        wait_all(started)
        blocks = slice(i * 256 // CAP, (i + 1) * 256 // CAP)
        part = dot(grads_v[c], w_v[...], NT)
        for dy in range(4):
            value = (part[:, lanes(dy)] + s_v[dy, c].astype(F32)).astype(BF)
            value = value.reshape(256 // CAP, CAP, COLS)
            early_v[blocks, :, lanes(dy)] = value[:, 0:EARLY]
            late_v[dy, blocks] = value[:, EARLY:CAP]
        both = prob_v[c].astype(F32) + sib_v[c].astype(F32)
        both = jnp.sum(both, axis=1, keepdims=True).reshape(256 // CAP, CAP, 1)
        early_v[blocks, :, 4 * COLS : 4 * COLS + 128] = split_lanes(
            both[:, 0:EARLY], both[:, EARLY:CAP]
        )
        done.append(copies.start(early_v.at[blocks], early.at[blocks]))
        for dy in range(4):
            done.append(copies.start(late_v.at[dy, blocks], late[dy].at[blocks]))
    wait_all(done)


HALF = ROWS // 2


def part_of(source, c):
    if len(source) == 1:
        return source[0].at[c]
    half = c.start // HALF
    return source[half].at[slice(c.start - half * HALF, c.stop - half * HALF)]


def in_chunks(copies, sources, x_v, c):
    return [copies.start(part_of(x, c), x_v.at[c, lanes(i)]) for i, x in enumerate(sources)]


def near_forward_body(t, *refs):
    xs, wg, wu, out = [(x,) for x in refs[:6]], refs[6], refs[7], refs[8]
    x_v, w_v, out_v, sems = refs[9:]
    copies = Copies(sems)
    w_in = gate_up_rows(copies, t, wg, wu, w_v.at[0 : 3 * COLS], (0, 1, 3), False)
    w_in += gate_up_rows(copies, t, wg, wu, w_v.at[3 * COLS : 6 * COLS], (0, 1, 3), True)
    rows = chunks(256)
    ins = [in_chunks(copies, xs, x_v, c) for c in rows]
    wait_all(w_in)
    done = []
    for i, c in enumerate(rows):
        wait_all(ins[i])
        out_v[c] = dot(x_v[c], w_v[...])
        done.append(copies.start(out_v.at[c], out.at[c]))
    wait_all(done)


def forward_body(t, *refs):
    xs, near, wg, wu = [refs[0:2], refs[2:4]], *refs[4:7]
    act, slope, hidden, x_v, w_v, near_v, act_v, slope_v, hidden_v, sems = refs[7:]
    copies = Copies(sems)
    w_in = gate_up_rows(copies, t, wg, wu, w_v.at[0:COLS], (2,), False)
    w_in += gate_up_rows(copies, t, wg, wu, w_v.at[COLS : 2 * COLS], (2,), True)
    rows = chunks(256)
    ins = [
        in_chunks(copies, xs, x_v, c) + [copies.start(near.at[c], near_v.at[c])] for c in rows
    ]
    wait_all(w_in)
    done = []
    for i, c in enumerate(rows):
        wait_all(ins[i])
        total = near_v[c] + dot(x_v[c], w_v[...])
        gate, up = total[:, 0:HID], total[:, HID : 2 * HID]
        sigma = jax.nn.sigmoid(gate)
        active = gate * sigma
        act_v[c] = active
        slope_v[c] = up * (sigma * (1.0 + gate * (1.0 - sigma)))
        hidden_v[c] = (active * up).astype(BF)
        for a, b in ((act_v, act), (slope_v, slope), (hidden_v, hidden)):
            done.append(copies.start(a.at[c], b.at[c]))
    wait_all(done)


def weights_gate_up_body(t, grads, *refs):
    xs = [(0, 0, refs[0:1]), (1, 0, refs[1:2]), (3, 0, refs[2:3])]
    xs += [(0, 1, refs[3:4]), (1, 1, refs[4:5]), (3, 1, refs[5:6])]
    xs += [(2, 0, refs[6:8]), (2, 1, refs[8:10])]
    out_gate, out_up, grads_v, x_v, gate_v, up_v, sems = refs[10:]
    copies = Copies(sems)

    def load(i):
        parts = xs[i][2]
        rows = ROWS // len(parts)
        return [
            copies.start(p, x_v.at[i, h * rows : (h + 1) * rows]) for h, p in enumerate(parts)
        ]

    ins = [load(0)]
    grads_in = copies.start(grads, grads_v)
    ins += [load(i) for i in range(1, 8)]
    grads_in.wait()
    done = []
    for i, (dy, sibling, _) in enumerate(xs):
        wait_all(ins[i])
        both = dot(x_v[i], grads_v[...], TN).astype(BF)
        gate_v[lanes(i)] = both[:, 0:HID]
        up_v[lanes(i)] = both[:, HID : 2 * HID]
        at = slice_at(t, dy, sibling == 1)
        done.append(copies.start(gate_v.at[lanes(i)], out_gate.at[at]))
        done.append(copies.start(up_v.at[lanes(i)], out_up.at[at]))
    wait_all(done)


def weights_down_body(t, hidden, own, sib, out, h_v, own_v, sib_v, ht_v, out_v, sems):
    copies = Copies(sems)
    h_in = copies.start(hidden, h_v)
    pairs = [(side, half) for side in range(2) for half in range(2)]
    g_in = []
    for side, half in pairs:
        cols = slice(half * 2 * COLS, (half + 1) * 2 * COLS)
        src, dst = ((own, own_v), (sib, sib_v))[side]
        g_in.append(copies.start(src.at[:, cols], dst.at[:, cols]))
    h_in.wait()
    ht_v[...] = h_v[...].T
    done = []
    for (side, half), started in zip(pairs, g_in):
        started.wait()
        cols = slice(half * 2 * COLS, (half + 1) * 2 * COLS)
        part = dot(ht_v[...], (own_v, sib_v)[side][:, cols]).astype(BF)
        for j in range(2):
            dy = half * 2 + j
            place = out_v.at[:, slice((side * 4 + dy) * COLS, (side * 4 + dy + 1) * COLS)]
            place[...] = part[:, lanes(j)]
            at = pl.ds(pl.multiple_of(slice_of(t[0], dy, side == 1) * COLS, 128), COLS)
            done.append(copies.start(place, out.at[:, at]))
    wait_all(done)


def selection(routes):
    first, second, slot = slot_masks(routes)
    hots = [one_hot(slot, e) for e in range(EXPERTS)]
    kinds = [hots]
    for mask in (first, second):
        kinds.append([hots[e] * jnp.where(mask[e : e + 1, :], 1.0, 0.0) for e in range(EXPERTS)])
    return [
        [jnp.concatenate([h[at] for h in kind], axis=0).astype(BF) for kind in kinds]
        for at in (slice(0, EARLY), slice(EARLY, CAP))
    ]


def from_slots(select, rows, cols):
    half = EXPERTS * EARLY
    return dot(select, rows[0:half, cols], TN) + dot(select, rows[half : 2 * half, cols], TN)


def combine_body(routes, rows, own, own_lanes, m1, m2, m3):
    early, late = selection(routes[...])
    total = from_slots(early[0], rows, slice(0, 4 * COLS))
    own[...] = total[:, 0:COLS]
    at = slice(4 * COLS, 4 * COLS + 128)
    probs = []
    for k in (1, 2):
        a, b = from_slots(early[k], rows, at), from_slots(late[k], rows, at)
        probs.append(a[:, 0:1] + a[:, 1:2] + b[:, 2:3] + b[:, 3:4])
    prob_lanes = split_lanes(*probs)
    own_lanes[...] = prob_lanes
    for dy, m in ((1, m1), (2, m2), (3, m3)):
        m[:, 0:COLS] = total[:, lanes(dy)].astype(BF)
        m[:, COLS : COLS + 128] = prob_lanes


def finish_body(routes, probs, rows, own, own_lanes, m1, m2, m3, out, prob_out):
    _, late = selection(routes[...])
    total = from_slots(late[0], rows, slice(0, COLS)) + own[...]
    prob_lanes = own_lanes[...].astype(F32)
    for m in (m1, m2, m3):
        total += m[:, 0:COLS].astype(F32)
        prob_lanes += m[:, COLS : COLS + 128].astype(F32)
    out[...] = total.astype(BF)
    turned = prob_lanes.T
    p = probs[...].astype(F32)
    prob_out[0:1, :] = (turned[0:1, :] + turned[1:2, :]) / p[0:1, :]
    prob_out[1:2, :] = (turned[2:3, :] + turned[3:4, :]) / p[1:2, :]


def on_device(tokens, d_out, routes, probs, w_gate, w_up, w_down):
    wg, wu, wd = w_gate[0], w_up[0], w_down[0]
    t = lax.axis_index("tensor").astype(jnp.int32).reshape(1)
    routes_t = routes.T
    probs_t = probs.T

    def from_y(x, dy):
        return lax.ppermute(
            x, "tensor", [(i, ((i // 2 - dy) % 4) * 2 + i % 2) for i in range(8)]
        )

    def from_sibling(x):
        return lax.ppermute(x, "tensor", [(i, i ^ 1) for i in range(8)])

    def exchange(x):
        got = lax.all_to_all(x, ("dp", "ctx"), split_axis=0, concat_axis=0, tiled=True)
        return got.reshape(16 * x.shape[1], x.shape[2])

    def after(x, *others):
        return lax.optimization_barrier((x,) + others)[0]

    MB = 1 << 20
    wide = 4 * COLS
    with jax.named_scope("dispatch"):
        gs = [d_out] + [from_y(d_out, dy) for dy in (1, 2, 3)]
        send_x = call(dispatch_x_body, sds((16, CAP, COLS)), flops=10**8, nbytes=MB)(routes_t, tokens)
        x0 = exchange(send_x)
        send_g = call(dispatch_g_body, sds((16, CAP, wide)), flops=2 * 10**8, nbytes=4 * MB)(
            routes_t, probs_t, *gs
        )
    with jax.named_scope("gather"):
        up1, down1 = from_y(x0, 1), from_y(x0, 3)
        near_xs = [x0, up1, down1]
        near_xs += [from_sibling(x) for x in near_xs]
        far_xs = [from_y(down1[:HALF], 3), from_y(up1[HALF:], 1)]
        g_got = exchange(after(send_g, x0))
    with jax.named_scope("forward"):
        (near,) = plain_call(
            near_forward_body,
            t,
            near_xs + [wg, wu],
            [sds((ROWS, 2 * HID), F32)],
            [((ROWS, 6 * COLS), BF), ((6 * COLS, 2 * HID), BF), ((ROWS, 2 * HID), F32)],
            40,
            1,
            1,
        )
        far_xs += [from_sibling(after(x, near)) for x in far_xs]
        g_own = after(g_got, *far_xs)
        g_sib = from_sibling(g_own)
        act, slope, hidden = plain_call(
            forward_body,
            t,
            far_xs + [near, wg, wu],
            [sds((ROWS, HID), F32), sds((ROWS, HID), F32), sds((ROWS, HID))],
            [((ROWS, 2 * COLS), BF), ((2 * COLS, 2 * HID), BF), ((ROWS, 2 * HID), F32)]
            + [((ROWS, HID), F32), ((ROWS, HID), F32), ((ROWS, HID), BF)],
            28,
            1,
            1,
        )
    with jax.named_scope("backward"):
        got = plain_call(
            back_body,
            t,
            [g_own, g_sib, act, slope, hidden, wd, wg, wu],
            [sds((ROWS, 2 * HID)), sds((ROWS, 128))] + [sds((ROWS, COLS))] * 4,
            [((ROWS, wide), BF)] * 2
            + [((ROWS, HID), F32)] * 2
            + [((ROWS, HID), BF), ((HID, wide), BF), ((HID, wide), BF), ((wide, 2 * HID), BF)]
            + [((ROWS, 2 * HID), BF), ((ROWS, 128), BF), ((ROWS, wide), BF)],
            60,
            1,
            1,
        )
        grads, prob = got[:2]
        prob_sib = from_sibling(prob)
        part_sib = [from_sibling(p) for p in got[2:]]
    with jax.named_scope("sums"):
        sums = plain_call(
            sums_body,
            t,
            [grads, prob, prob_sib] + part_sib + [wg, wu],
            [sds((16, EARLY, wide + 128))] + [sds((16, CAP - EARLY, COLS))] * 4,
            [((ROWS, 2 * HID), BF), ((ROWS, 128), BF), ((ROWS, 128), BF)]
            + [((4, ROWS, COLS), BF), ((wide, 2 * HID), BF), ((16, EARLY, wide + 128), BF)]
            + [((4, 16, CAP - EARLY, COLS), BF)],
            56,
            1,
            1,
        )
        early, late = sums[0], sums[1:]
        arrived = [from_y(late[dy], 4 - dy) for dy in (1, 2, 3)]
        early_rows = exchange(early)
    with jax.named_scope("weights_gate_up"):
        grad_gate, grad_up = plain_call(
            weights_gate_up_body,
            t,
            [after(grads, early)] + near_xs + far_xs,
            [sds((8 * COLS, HID))] * 2,
            [((ROWS, 2 * HID), BF), ((8, ROWS, COLS), BF)] + [((8 * COLS, HID), BF)] * 2,
            27,
            1,
            1,
        )
    with jax.named_scope("weights_down"):
        (grad_down,) = plain_call(
            weights_down_body,
            t,
            [after(hidden, grad_gate), g_own, g_sib],
            [sds((HID, 8 * COLS))],
            [((ROWS, HID), BF), ((ROWS, wide), BF), ((ROWS, wide), BF)]
            + [((HID, ROWS), BF), ((HID, 8 * COLS), BF)],
            13,
            1,
            1,
        )
    with jax.named_scope("late_sum"):
        mine = after(late[0], grad_down)
        late_sum = sum((x.astype(F32) for x in arrived), mine.astype(F32)).astype(BF)
        late_rows = exchange(late_sum)
    with jax.named_scope("finish"):
        own, own_lanes, m1, m2, m3 = call(
            combine_body,
            [sds((TOK, COLS), F32), sds((TOK, 128))] + [sds((TOK, COLS + 128))] * 3,
            flops=1,
            nbytes=1,
        )(routes_t, early_rows)
        d_tokens, d_probs = call(
            finish_body, [sds((TOK, COLS)), sds((2, TOK), F32)], flops=1, nbytes=1
        )(
            routes_t,
            probs_t,
            late_rows,
            own,
            own_lanes,
            from_y(m1, 3),
            from_y(m2, 2),
            from_y(m3, 1),
        )
    return d_tokens, d_probs.T, grad_gate[None], grad_up[None], grad_down[None]


def solution(mesh):
    in_specs = (
        P(("dp", "ctx"), "tensor"),
        P(("dp", "ctx"), "tensor"),
        P(("dp", "ctx"), None),
        P(("dp", "ctx"), None),
        P("ctx", None, ("dp", "tensor")),
        P("ctx", None, ("dp", "tensor")),
        P("ctx", ("dp", "tensor"), None),
    )
    out_specs = (
        P(("dp", "ctx"), "tensor"),
        P(("dp", "ctx"), None),
        P("ctx", None, ("dp", "tensor")),
        P("ctx", None, ("dp", "tensor")),
        P("ctx", ("dp", "tensor"), None),
    )
    return jax.shard_map(
        on_device, mesh=mesh, in_specs=in_specs, out_specs=out_specs, check_vma=False
    )
```

time: 179 us -> 167 us (0.933)
  waiting for transfers between devices: 49.1 us -> 36.7 us
  starting transfers between devices: 49.9 us -> 52.6 us
  Pallas kernels: 67.5 us -> 65.7 us
    ppermute x12 -> x13, waiting for transfers between devices: 43.8 us -> 28 us  [from_y(): lax.ppermute(x, 'tensor', [(i, (i // 2 - dy) % 4 * 2 + i % 2) for i in ra...]
    pallas_call x3 -> x2, Pallas kernels: 17.1 us -> 5.41 us  [the longest x1 3.08 us: on_device(): call(combine_body, [sds((TOK, COLS), F32), sds((TOK, 128))] + [sds((TOK,...]
    pallas_call x6, Pallas kernels: 44.9 us -> 54.7 us  [plain_call(): pl.pallas_call(body, out_shape=outs, in_specs=[pl.BlockSpec(memory_space=...]
    ppermute x10 -> x11, waiting for transfers between devices: 3.14 us -> 7.1 us  [from_sibling(): return lax.ppermute(x, 'tensor', [(i, i ^ 1) for i in range(8)])]
    slice x0 -> x2, local copies, waits for them, and re-layouts: none -> 3.56 us  [on_device(): far_xs = [from_y(down1[:HALF], 3), from_y(up1[HALF:], 1)]]
    unnamed x40 -> x44, local copies, waits for them, and re-layouts: 9.27 us -> 6.28 us
    all_to_all x4, starting transfers between devices: 30 us -> 32.2 us  [exchange(): lax.all_to_all(x, ('dp', 'ctx'), split_axis=0, concat_axis=0, tiled=True)]
    ppermute x12 -> x13, starting transfers between devices: 18.2 us -> 18.6 us  [from_y(): lax.ppermute(x, 'tensor', [(i, (i // 2 - dy) % 4 * 2 + i % 2) for i in ra...]
  transfers between devices with their start and end apart: 26 -> 28, of which waited for: 12 -> 14; matrix products, arithmetic and copies ran while one was open for 1% -> 3% of each run, Pallas kernels for 26% -> 25%
where the time goes in v2:
time: 167 us
  Pallas kernels  65.7 us (39%)
  starting transfers between devices  52.6 us (31%)
  waiting for transfers between devices  36.7 us (22%)
  local copies, waits for them, and re-layouts  9.84 us (6%)
    pallas_call x6, Pallas kernels, plain_call(): pl.pallas_call(body, out_shape=outs, in_specs=[pl.BlockSpec(memory_space=...  54.7 us
    all_to_all x4, starting transfers between devices, exchange(): lax.all_to_all(x, ('dp', 'ctx'), split_axis=0, concat_axis=0, tiled=True)  32.2 us
    ppermute x13, waiting for transfers between devices, from_y(): lax.ppermute(x, 'tensor', [(i, (i // 2 - dy) % 4 * 2 + i % 2) for i in ra...  28 us
    ppermute x13, starting transfers between devices, from_y(): lax.ppermute(x, 'tensor', [(i, (i // 2 - dy) % 4 * 2 + i % 2) for i in ra...  18.6 us
    ppermute x11, waiting for transfers between devices, from_sibling(): return lax.ppermute(x, 'tensor', [(i, i ^ 1) for i in range(8)])  7.1 us
    unnamed x44, local copies, waits for them, and re-layouts  6.28 us
    slice x2, local copies, waits for them, and re-layouts, on_device(): far_xs = [from_y(down1[:HALF], 3), from_y(up1[HALF:], 1)]  3.56 us
    pallas_call x1, Pallas kernels, on_device(): call(dispatch_g_body, sds((16, CAP, wide)), flops=2 * 10 ** 8, nbytes=4 *...  3.41 us
  transfers between devices with their start and end apart: 28, of which 14 were waited for; matrix products, arithmetic and copies ran while one was open for 3% of the time, Pallas kernels for 25%

profile of v2, /device:TPU:2, one launch (start us, length us, event | category | flops | bytes accessed | tf_op | source)
XLA Modules:
  0.0 166.7 jit_solution(2316065747121926070)
XLA Ops:
  0.6 2.2 %dispatch.3 = bf16[16,64,384]{2,1,0:T(8,128)(2,1)} custom-call(s32[2,128]{1,0:T(2,128)} %bitcast.34, bf16[128,384]{1,0:T(8,128)(2,1)} %tokens.1), custom_call_target="tpu_custom_call" | custom-call | flops 100000000 | bytes 1048576 | tf_op jit(solution)/shard_map/dispatch/pallas_call | solution.py:409
  2.8 8.3 %all-to-all-start = ((bf16[16,64,384]{2,1,0:T(8,128)(2,1)}), bf16[16,64,384]{2,1,0:T(8,128)(2,1)S(1)}, u32[]{:S(2)}, u32[]{:S(2)}) async-start(bf16[16,64,384]{2,1,0:T(8,128)(2,1)} %dispatch.3), calls=%async_computation | async-start | bytes 1572864 | tf_op jit(solution)/shard_map/dispatch/all_to_all | solution.py:399
  11.1 3.2 %collective-permute-start.1 = (bf16[128,384]{1,0:T(8,128)(2,1)}, bf16[128,384]{1,0:T(8,128)(2,1)S(1)}, u32[]{:S(2)}, u32[]{:S(2)}) collective-permute-start(bf16[128,384]{1,0:T(8,128)(2,1)} %g0.1), channel_id=1, source_target_pairs={{0,4},{1,5},{2,6},{3,7},{4,0},{5,1},{6,2},{7,3},{8,12},{9,13},{10,... | collective-permute-start | bytes 294920 | tf_op jit(solution)/shard_map/dispatch/ppermute | solution.py:391
  14.3 1.1 collective-permute-start
  15.4 1.0 collective-permute-start.2
  16.3 1.8 %collective-permute-done.1.g2 = bf16[128,384]{1,0:T(8,128)(2,1)S(1)} collective-permute-done((bf16[128,384]{1,0:T(8,128)(2,1)}, bf16[128,384]{1,0:T(8,128)(2,1)S(1)}, u32[]{:S(2)}, u32[]{:S(2)}) %collective-permute-start.1) | collective-permute-done | bytes 98336 | tf_op jit(solution)/shard_map/dispatch/ppermute | solution.py:391
  18.1 1.2 collective-permute-done.g1
  19.3 2.1 %collective-permute-done.2.g3 = bf16[128,384]{1,0:T(8,128)(2,1)S(1)} collective-permute-done((bf16[128,384]{1,0:T(8,128)(2,1)}, bf16[128,384]{1,0:T(8,128)(2,1)S(1)}, u32[]{:S(2)}, u32[]{:S(2)}) %collective-permute-start.2) | collective-permute-done | bytes 98336 | tf_op jit(solution)/shard_map/dispatch/ppermute | solution.py:391
  21.4 0.6 copy-done.18
  22.0 3.4 %dispatch.2 = bf16[16,64,1536]{2,1,0:T(8,128)(2,1)} custom-call(s32[2,128]{1,0:T(2,128)} %bitcast.35, bf16[2,128]{1,0:T(2,128)(2,1)} %bitcast.38, bf16[128,384]{1,0:T(8,128)(2,1)} %g0.1, bf16[128,384]{1,0:T(8,128)(2,1)} %copy-done.17, bf16[128,384]{1,0:T(8,128)(2,1)} %copy-done.16, bf16[128,384]{1,0:T(8,128)(2,1)} %copy-done.18), custom_call_target="tpu_custom_call" | custom-call | flops 200000000 | bytes 4194304 | tf_op jit(solution)/shard_map/dispatch/pallas_call | solution.py:411
  25.5 0.9 copy-done.2
  26.4 7.2 %all-to-all-start.1 = ((bf16[16,64,1536]{2,1,0:T(8,128)(2,1)}), bf16[16,64,1536]{2,1,0:T(8,128)(2,1)S(1)}, u32[]{:S(2)}, u32[]{:S(2)}) async-start(bf16[16,64,1536]{2,1,0:T(8,128)(2,1)} %dispatch.2), calls=%async_computation.1 | async-start | bytes 6291456 | tf_op jit(solution)/shard_map/gather/all_to_all | solution.py:399
  33.6 0.6 collective-permute-start.5
  34.2 1.5 collective-permute-start.3
  35.6 15.0 %collective-permute-done.5.refs_1_ = bf16[1024,384]{1,0:T(8,128)(2,1)} collective-permute-done((bf16[1024,384]{1,0:T(8,128)(2,1)}, bf16[1024,384]{1,0:T(8,128)(2,1)}, u32[]{:S(2)}, u32[]{:S(2)}) %collective-permute-start.5) | collective-permute-done | bytes 786464 | tf_op jit(solution)/shard_map/gather/ppermute | solution.py:391
  50.7 2.6 %collective-permute-done.3.refs_2_ = bf16[1024,384]{1,0:T(8,128)(2,1)} collective-permute-done((bf16[1024,384]{1,0:T(8,128)(2,1)}, bf16[1024,384]{1,0:T(8,128)(2,1)}, u32[]{:S(2)}, u32[]{:S(2)}) %collective-permute-start.3) | collective-permute-done | bytes 786464 | tf_op jit(solution)/shard_map/gather/ppermute | solution.py:391
  53.3 1.8 %slice.9 = bf16[512,384]{1,0:T(8,128)(2,1)} slice(bf16[1024,384]{1,0:T(8,128)(2,1)} %collective-permute-done.5.refs_1_), slice={[512:1024], [0:384]} | slice | bytes 786432 | tf_op jit(solution)/shard_map/gather/slice | solution.py:418
  55.1 0.8 collective-permute-start.6
  55.8 1.8 %slice.8 = bf16[512,384]{1,0:T(8,128)(2,1)} slice(bf16[1024,384]{1,0:T(8,128)(2,1)} %collective-permute-done.3.refs_2_), slice={[0:512], [0:384]} | slice | bytes 786432 | tf_op jit(solution)/shard_map/gather/slice | solution.py:418
  57.6 1.2 collective-permute-start.4
  58.9 9.5 %forward.2.refs_4_ = f32[1024,1024]{1,0:T(8,128)} custom-call(s32[1]{0:T(128)} %bitcast.2.t, bf16[1024,384]{1,0:T(8,128)(2,1)} %bitcast.28, bf16[1024,384]{1,0:T(8,128)(2,1)} %collective-permute-done.5.refs_1_, bf16[1024,384]{1,0:T(8,128)(2,1)} %collective-permute-done.3.refs_2_, bf16[1024,384]{1,0:T(8,128)(2,1)} %collective-permute-done.7.refs_3_, ...), custom_call_target="tpu_custom_call" | custom-call | flops 1 | bytes 1 | tf_op jit(solution)/shard_map/forward/pallas_call | solution.py:88
  68.4 1.5 collective-permute-done.4.refs_0_.refs_6_
  69.9 0.5 collective-permute-start.11
  70.4 1.9 %collective-permute-done.10.refs_2_.refs_8_ = bf16[512,384]{1,0:T(8,128)(2,1)S(1)} collective-permute-done((bf16[512,384]{1,0:T(8,128)(2,1)}, bf16[512,384]{1,0:T(8,128)(2,1)S(1)}, u32[]{:S(2)}, u32[]{:S(2)}) %collective-permute-start.10) | collective-permute-done | bytes 393248 | tf_op jit(solution)/shard_map/forward/ppermute | solution.py:396
  72.4 0.7 copy-done.5
  73.5 6.9 %forward.3 = (f32[1024,512]{1,0:T(8,128)}, f32[1024,512]{1,0:T(8,128)}, bf16[1024,512]{1,0:T(8,128)(2,1)}) custom-call(s32[1]{0:T(128)} %bitcast.2.t, bf16[512,384]{1,0:T(8,128)(2,1)} %collective-permute-done.4.refs_0_.refs_6_, bf16[512,384]{1,0:T(8,128)(2,1)} %copy-done.4, bf16[512,384]{1,0:T(8,128)(2,1)} %copy-done.5, ...), custom_call_target="tpu_custom_call" | custom-call | flops 1 | bytes 1 | tf_op jit(solution)/shard_map/forward/pallas_call | solution.py:88
  80.4 1.6 copy-done.1
  82.0 12.1 %backward.1 = (bf16[1024,1024]{1,0:T(8,128)(2,1)}, bf16[1024,128]{1,0:T(8,128)(2,1)}, bf16[1024,384]{1,0:T(8,128)(2,1)}, bf16[1024,384]{1,0:T(8,128)(2,1)}, bf16...) custom-call(s32[1]{0:T(128)} %bitcast.2.t, bf16[1024,1536]{1,0:T(8,128)(2,1)} %bitcast.23, bf16[1024,1536]{1,0:T(8,128)(2,1)} %copy-done.1, ...), custom_call_target="tpu_custom_call" | custom-call | flops 1 | bytes 1 | tf_op jit(solution)/shard_map/backward/pallas_call | solution.py:88
  94.2 0.5 collective-permute-start.15
  95.3 5.1 %collective-permute-done.13.prob_sib = bf16[1024,128]{1,0:T(8,128)(2,1)S(1)} collective-permute-done((bf16[1024,128]{1,0:T(8,128)(2,1)}, bf16[1024,128]{1,0:T(8,128)(2,1)S(1)}, u32[]{:S(2)}, u32[]{:S(2)}) %collective-permute-start.13) | collective-permute-done | bytes 262176 | tf_op jit(solution)/shard_map/backward/ppermute | solution.py:396
  100.5 0.6 copy-done.12
  102.2 7.8 %sums.1 = (bf16[16,32,1664]{2,1,0:T(8,128)(2,1)}, bf16[16,32,384]{2,1,0:T(8,128)(2,1)}, bf16[16,32,384]{2,1,0:T(8,128)(2,1)}, bf16[16,32,384]{2,1,0:T(8,128)(2,1)}, bf16[16,32,384]{2,1,0:T(8,128)(2,1)}) custom-call(s32[1]{0:T(128)} %bitcast.2.t, bf16[1024,1024]{1,0:T(8,128)(2,1)} %get-tuple-element.50.grads, bf16[1024,128]{1,0:T(8,128)(2,1)} %get-tuple-element.43.prob, ...), custom_call_target="tpu_custom_call" | custom-call | flops 1 | bytes 1 | tf_op jit(solution)/shard_map/sums/pallas_call | solution.py:88
  110.0 10.3 %all-to-all-start.3 = ((bf16[16,32,1664]{2,1,0:T(8,128)(2,1)}), bf16[16,32,1664]{2,1,0:T(8,128)(2,1)S(1)}, u32[]{:S(2)}, u32[]{:S(2)}) async-start(bf16[16,32,1664]{2,1,0:T(8,128)(2,1)} %get-tuple-element.49), calls=%async_computation.3 | async-start | bytes 3407872 | tf_op jit(solution)/shard_map/sums/all_to_all | solution.py:399
  120.3 0.9 collective-permute-start.18
  121.2 2.5 %collective-permute-start.19 = (bf16[16,32,384]{2,1,0:T(8,128)(2,1)S(1)}, bf16[16,32,384]{2,1,0:T(8,128)(2,1)S(1)}, u32[]{:S(2)}, u32[]{:S(2)}) collective-permute-start(bf16[16,32,384]{2,1,0:T(8,128)(2,1)S(1)} %copy-done.20), channel_id=1, source_target_pairs={{0,4},{1,5},{2,6},{3,7},{4,0},{5,1},{6,2},{7,3},{8,12},{9,13},{10,... | collective-permute-start | bytes 1179656 | tf_op jit(solution)/shard_map/sums/ppermute | solution.py:391
  123.7 1.3 collective-permute-start.20
  125.0 10.9 %weights_gate_up.1 = (bf16[3072,512]{1,0:T(8,128)(2,1)}, bf16[3072,512]{1,0:T(8,128)(2,1)}) custom-call(s32[1]{0:T(128)} %bitcast.2.t, bf16[1024,1024]{1,0:T(8,128)(2,1)} %get-tuple-element.50.grads, bf16[1024,384]{1,0:T(8,128)(2,1)} %bitcast.29, bf16[1024,384]{1,0:T(8,128)(2,1)} %collective-permute-done.5.refs_1_, ...), custom_call_target="tpu_custom_call" | custom-call | flops 1 | bytes 1 | tf_op jit(solution)/shard_map/weights_gate_up/pallas_call | solution.py:88
  135.9 7.6 %weights_down.1 = bf16[512,3072]{1,0:T(8,128)(2,1)} custom-call(s32[1]{0:T(128)} %bitcast.2.t, bf16[1024,512]{1,0:T(8,128)(2,1)} %get-tuple-element.52.hidden, bf16[1024,1536]{1,0:T(8,128)(2,1)} %bitcast.24, bf16[1024,1536]{1,0:T(8,128)(2,1)} %copy-done.1), custom_call_target="tpu_custom_call" | custom-call | flops 1 | bytes 1 | tf_op jit(solution)/shard_map/weights_down/pallas_call | solution.py:88
  143.5 1.0 add_convert_fusion
  144.5 0.9 all-to-all-done.3
  145.4 6.4 %all-to-all-start.2 = ((bf16[16,32,384]{2,1,0:T(8,128)(2,1)}), bf16[16,32,384]{2,1,0:T(8,128)(2,1)S(1)}, u32[]{:S(2)}, u32[]{:S(2)}) async-start(bf16[16,32,384]{2,1,0:T(8,128)(2,1)} %add_convert_fusion), calls=%async_computation.2 | async-start | bytes 786432 | tf_op jit(solution)/shard_map/late_sum/all_to_all | solution.py:399
  151.8 3.1 %finish.2 = (f32[128,384]{1,0:T(8,128)}, bf16[128,128]{1,0:T(8,128)(2,1)}, bf16[128,512]{1,0:T(8,128)(2,1)}, bf16[128,512]{1,0:T(8,128)(2,1)}, bf16[128,512]{1,0:T(8,128)(2,1)}) custom-call(s32[2,128]{1,0:T(2,128)} %bitcast.36, bf16[512,1664]{1,0:T(8,128)(2,1)} %bitcast.30), custom_call_target="tpu_custom_call" | custom-call | flops 1 | bytes 1 | tf_op jit(solution)/shard_map/finish/pallas_call | solution.py:506
  154.9 0.8 collective-permute-start.21
  155.7 2.5 %collective-permute-start.22 = (bf16[128,512]{1,0:T(8,128)(2,1)}, bf16[128,512]{1,0:T(8,128)(2,1)S(1)}, u32[]{:S(2)}, u32[]{:S(2)}) collective-permute-start(bf16[128,512]{1,0:T(8,128)(2,1)} %get-tuple-element.60), channel_id=1, source_target_pairs={{0,4},{1,5},{2,6},{3,7},{4,0},{5,1},{6,2},{7,3},{8,12},{9,13},{10,... | collective-permute-start | bytes 393224 | tf_op jit(solution)/shard_map/finish/ppermute | solution.py:391
  158.2 1.3 collective-permute-start.23
  159.9 1.9 %collective-permute-done.21.m1 = bf16[128,512]{1,0:T(8,128)(2,1)S(1)} collective-permute-done((bf16[128,512]{1,0:T(8,128)(2,1)}, bf16[128,512]{1,0:T(8,128)(2,1)S(1)}, u32[]{:S(2)}, u32[]{:S(2)}) %collective-permute-start.21) | collective-permute-done | bytes 131104 | tf_op jit(solution)/shard_map/finish/ppermute | solution.py:391
  161.8 1.4 collective-permute-done.22.m2
  164.3 2.3 %finish.3 = (bf16[128,384]{1,0:T(8,128)(2,1)}, f32[2,128]{1,0:T(2,128)}) custom-call(s32[2,128]{1,0:T(2,128)} %bitcast.37, bf16[2,128]{1,0:T(2,128)(2,1)} %bitcast.39, bf16[512,384]{1,0:T(8,128)(2,1)} %bitcast.33, f32[128,384]{1,0:T(8,128)} %get-tuple-element.57.own, bf16[128,128]{1,0:T(8,128)(2,1)} %get-tuple-element.58.own_lanes, ...), custom_call_target="tpu_custom_call" | custom-call | flops 1 | bytes 1 | tf_op jit(solution)/shard_map/finish/pallas_call | solution.py:512
  (65 shorter events, 3.7 us)
Async XLA Ops:
  2.8 22.7 %all-to-all-start = ((bf16[16,64,384]{2,1,0:T(8,128)(2,1)}), bf16[16,64,384]{2,1,0:T(8,128)(2,1)S(1)}, u32[]{:S(2)}, u32[]{:S(2)}) async-start(bf16[16,64,384]{2,1,0:T(8,128)(2,1)} %dispatch.3), calls=%async_computation | async-start | bytes 1572864 | tf_op jit(solution)/shard_map/dispatch/all_to_all | solution.py:399
  11.1 7.0 %collective-permute-start.1 = (bf16[128,384]{1,0:T(8,128)(2,1)}, bf16[128,384]{1,0:T(8,128)(2,1)S(1)}, u32[]{:S(2)}, u32[]{:S(2)}) collective-permute-start(bf16[128,384]{1,0:T(8,128)(2,1)} %g0.1), channel_id=1, source_target_pairs={{0,4},{1,5},{2,6},{3,7},{4,0},{5,1},{6,2},{7,3},{8,12},{9,13},{10,... | collective-permute-start | bytes 294920 | tf_op jit(solution)/shard_map/dispatch/ppermute | solution.py:391
  14.3 5.0 %collective-permute-start = (bf16[128,384]{1,0:T(8,128)(2,1)}, bf16[128,384]{1,0:T(8,128)(2,1)S(1)}, u32[]{:S(2)}, u32[]{:S(2)}) collective-permute-start(bf16[128,384]{1,0:T(8,128)(2,1)} %g0.1), channel_id=1, source_target_pairs={{0,6},{1,7},{2,0},{3,1},{4,2},{5,3},{6,4},{7,5},{8,14},{9,15},{10,... | collective-permute-start | bytes 294920 | tf_op jit(solution)/shard_map/dispatch/ppermute | solution.py:391
  15.4 6.0 %collective-permute-start.2 = (bf16[128,384]{1,0:T(8,128)(2,1)}, bf16[128,384]{1,0:T(8,128)(2,1)S(1)}, u32[]{:S(2)}, u32[]{:S(2)}) collective-permute-start(bf16[128,384]{1,0:T(8,128)(2,1)} %g0.1), channel_id=1, source_target_pairs={{0,2},{1,3},{2,4},{3,5},{4,6},{5,7},{6,0},{7,1},{8,10},{9,11},{10,... | collective-permute-start | bytes 294920 | tf_op jit(solution)/shard_map/dispatch/ppermute | solution.py:391
  18.1 3.3 %copy-start.16 = (bf16[128,384]{1,0:T(8,128)(2,1)}, bf16[128,384]{1,0:T(8,128)(2,1)S(1)}, u32[]{:S(2)}) copy-start(bf16[128,384]{1,0:T(8,128)(2,1)S(1)} %collective-permute-done.1.g2) | copy-start | bytes 294916
  19.3 2.1 %copy-start.17 = (bf16[128,384]{1,0:T(8,128)(2,1)}, bf16[128,384]{1,0:T(8,128)(2,1)S(1)}, u32[]{:S(2)}) copy-start(bf16[128,384]{1,0:T(8,128)(2,1)S(1)} %collective-permute-done.g1) | copy-start | bytes 294916
  25.5 0.9 copy-start.2
  26.4 47.1 %all-to-all-start.1 = ((bf16[16,64,1536]{2,1,0:T(8,128)(2,1)}), bf16[16,64,1536]{2,1,0:T(8,128)(2,1)S(1)}, u32[]{:S(2)}, u32[]{:S(2)}) async-start(bf16[16,64,1536]{2,1,0:T(8,128)(2,1)} %dispatch.2), calls=%async_computation.1 | async-start | bytes 6291456 | tf_op jit(solution)/shard_map/gather/all_to_all | solution.py:399
  33.6 17.1 %collective-permute-start.5 = (bf16[1024,384]{1,0:T(8,128)(2,1)}, bf16[1024,384]{1,0:T(8,128)(2,1)}, u32[]{:S(2)}, u32[]{:S(2)}) collective-permute-start(bf16[1024,384]{1,0:T(8,128)(2,1)} %bitcast.25), channel_id=1, source_target_pairs={{0,6},{1,7},{2,0},{3,1},{4,2},{5,3},{6,4},{7,5},{8,14},{9,15},{10,... | collective-permute-start | bytes 2359304 | tf_op jit(solution)/shard_map/gather/ppermute | solution.py:391
  34.2 19.1 %collective-permute-start.3 = (bf16[1024,384]{1,0:T(8,128)(2,1)}, bf16[1024,384]{1,0:T(8,128)(2,1)}, u32[]{:S(2)}, u32[]{:S(2)}) collective-permute-start(bf16[1024,384]{1,0:T(8,128)(2,1)} %bitcast.26), channel_id=1, source_target_pairs={{0,2},{1,3},{2,4},{3,5},{4,6},{5,7},{6,0},{7,1},{8,10},{9,11},{10,... | collective-permute-start | bytes 2359304 | tf_op jit(solution)/shard_map/gather/ppermute | solution.py:391
  35.6 23.2 %collective-permute-start.7 = (bf16[1024,384]{1,0:T(8,128)(2,1)}, bf16[1024,384]{1,0:T(8,128)(2,1)}, u32[]{:S(2)}, u32[]{:S(2)}) collective-permute-start(bf16[1024,384]{1,0:T(8,128)(2,1)} %bitcast.27), channel_id=1, source_target_pairs={{0,1},{1,0},{2,3},{3,2},{4,5},{5,4},{6,7},{7,6},{8,9},{9,8},{10,11... | collective-permute-start | bytes 2359304 | tf_op jit(solution)/shard_map/gather/ppermute | solution.py:396
  50.7 8.2 %collective-permute-start.8 = (bf16[1024,384]{1,0:T(8,128)(2,1)}, bf16[1024,384]{1,0:T(8,128)(2,1)}, u32[]{:S(2)}, u32[]{:S(2)}) collective-permute-start(bf16[1024,384]{1,0:T(8,128)(2,1)} %collective-permute-done.5.refs_1_), channel_id=1, source_target_pairs={{0,1},{1,0},{2,3},{3,2},{4,5},{5,4},{6,7},{7,6},{8,9},{9,8},{10,11... | collective-permute-start | bytes 2359304 | tf_op jit(solution)/shard_map/gather/ppermute | solution.py:396
  53.3 5.6 %collective-permute-start.9 = (bf16[1024,384]{1,0:T(8,128)(2,1)}, bf16[1024,384]{1,0:T(8,128)(2,1)}, u32[]{:S(2)}, u32[]{:S(2)}) collective-permute-start(bf16[1024,384]{1,0:T(8,128)(2,1)} %collective-permute-done.3.refs_2_), channel_id=1, source_target_pairs={{0,1},{1,0},{2,3},{3,2},{4,5},{5,4},{6,7},{7,6},{8,9},{9,8},{10,11... | collective-permute-start | bytes 2359304 | tf_op jit(solution)/shard_map/gather/ppermute | solution.py:396
  55.1 13.4 %collective-permute-start.6 = (bf16[512,384]{1,0:T(8,128)(2,1)}, bf16[512,384]{1,0:T(8,128)(2,1)S(1)}, u32[]{:S(2)}, u32[]{:S(2)}) collective-permute-start(bf16[512,384]{1,0:T(8,128)(2,1)} %slice.9), channel_id=1, source_target_pairs={{0,6},{1,7},{2,0},{3,1},{4,2},{5,3},{6,4},{7,5},{8,14},{9,15},{10,... | collective-permute-start | bytes 1179656 | tf_op jit(solution)/shard_map/gather/ppermute | solution.py:391
  57.6 12.3 %collective-permute-start.4 = (bf16[512,384]{1,0:T(8,128)(2,1)}, bf16[512,384]{1,0:T(8,128)(2,1)}, u32[]{:S(2)}, u32[]{:S(2)}) collective-permute-start(bf16[512,384]{1,0:T(8,128)(2,1)} %slice.8), channel_id=1, source_target_pairs={{0,2},{1,3},{2,4},{3,5},{4,6},{5,7},{6,0},{7,1},{8,10},{9,11},{10,... | collective-permute-start | bytes 1179656 | tf_op jit(solution)/shard_map/gather/ppermute | solution.py:391
  68.4 5.1 %copy-start.4 = (bf16[512,384]{1,0:T(8,128)(2,1)}, bf16[512,384]{1,0:T(8,128)(2,1)S(1)}, u32[]{:S(2)}) copy-start(bf16[512,384]{1,0:T(8,128)(2,1)S(1)} %collective-permute-done.6.refs_1_.refs_7_) | copy-start | bytes 1179652
  69.9 2.5 %collective-permute-start.10 = (bf16[512,384]{1,0:T(8,128)(2,1)}, bf16[512,384]{1,0:T(8,128)(2,1)S(1)}, u32[]{:S(2)}, u32[]{:S(2)}) collective-permute-start(bf16[512,384]{1,0:T(8,128)(2,1)} %collective-permute-done.4.refs_0_.refs_6_), channel_id=1, source_target_pairs={{0,1},{1,0},{2,3},{3,2},{4,5},{5,4},{6,7},{7,6},{8,9},{9,8},{10,11... | collective-permute-start | bytes 1179656 | tf_op jit(solution)/shard_map/forward/ppermute | solution.py:396
  69.9 3.2 %collective-permute-start.11 = (bf16[512,384]{1,0:T(8,128)(2,1)S(1)}, bf16[512,384]{1,0:T(8,128)(2,1)}, u32[]{:S(2)}, u32[]{:S(2)}) collective-permute-start(bf16[512,384]{1,0:T(8,128)(2,1)S(1)} %collective-permute-done.6.refs_1_.refs_7_), channel_id=1, source_target_pairs={{0,1},{1,0},{2,3},{3,2},{4,5},{5,4},{6,7},{7,6},{8,9},{9,8},{10,11... | collective-permute-start | bytes 1179656 | tf_op jit(solution)/shard_map/forward/ppermute | solution.py:396
  72.4 0.7 copy-start.5
  73.4 6.9 %copy-start = (bf16[16,64,1536]{2,1,0:T(8,128)(2,1)}, bf16[16,64,1536]{2,1,0:T(8,128)(2,1)S(1)}, u32[]{:S(2)}) copy-start(bf16[16,64,1536]{2,1,0:T(8,128)(2,1)S(1)} %all-to-all-done.1) | copy-start | bytes 9437188
  73.4 7.0 %collective-permute-start.12 = (bf16[1024,1536]{1,0:T(8,128)(2,1)S(1)}, bf16[1024,1536]{1,0:T(8,128)(2,1)S(1)}, u32[]{:S(2)}, u32[]{:S(2)}) collective-permute-start(bf16[1024,1536]{1,0:T(8,128)(2,1)S(1)} %bitcast.22), channel_id=1, source_target_pairs={{0,1},{1,0},{2,3},{3,2},{4,5},{5,4},{6,7},{7,6},{8,9},{9,8},{10,11... | collective-permute-start | bytes 9437192 | tf_op jit(solution)/shard_map/forward/ppermute | solution.py:396
  80.4 1.6 copy-start.1
  94.1 6.3 %collective-permute-start.14 = (bf16[1024,384]{1,0:T(8,128)(2,1)}, bf16[1024,384]{1,0:T(8,128)(2,1)S(1)}, u32[]{:S(2)}, u32[]{:S(2)}) collective-permute-start(bf16[1024,384]{1,0:T(8,128)(2,1)} %get-tuple-element.44), channel_id=1, source_target_pairs={{0,1},{1,0},{2,3},{3,2},{4,5},{5,4},{6,7},{7,6},{8,9},{9,8},{10,11... | collective-permute-start | bytes 2359304 | tf_op jit(solution)/shard_map/backward/ppermute | solution.py:396
  94.2 6.2 %collective-permute-start.15 = (bf16[1024,384]{1,0:T(8,128)(2,1)}, bf16[1024,384]{1,0:T(8,128)(2,1)S(1)}, u32[]{:S(2)}, u32[]{:S(2)}) collective-permute-start(bf16[1024,384]{1,0:T(8,128)(2,1)} %get-tuple-element.45), channel_id=1, source_target_pairs={{0,1},{1,0},{2,3},{3,2},{4,5},{5,4},{6,7},{7,6},{8,9},{9,8},{10,11... | collective-permute-start | bytes 2359304 | tf_op jit(solution)/shard_map/backward/ppermute | solution.py:396
  94.7 5.8 %collective-permute-start.16 = (bf16[1024,384]{1,0:T(8,128)(2,1)}, bf16[1024,384]{1,0:T(8,128)(2,1)S(1)}, u32[]{:S(2)}, u32[]{:S(2)}) collective-permute-start(bf16[1024,384]{1,0:T(8,128)(2,1)} %get-tuple-element.46), channel_id=1, source_target_pairs={{0,1},{1,0},{2,3},{3,2},{4,5},{5,4},{6,7},{7,6},{8,9},{9,8},{10,11... | collective-permute-start | bytes 2359304 | tf_op jit(solution)/shard_map/backward/ppermute | solution.py:396
  94.8 5.7 %collective-permute-start.17 = (bf16[1024,384]{1,0:T(8,128)(2,1)}, bf16[1024,384]{1,0:T(8,128)(2,1)S(1)}, u32[]{:S(2)}, u32[]{:S(2)}) collective-permute-start(bf16[1024,384]{1,0:T(8,128)(2,1)} %get-tuple-element.47), channel_id=1, source_target_pairs={{0,1},{1,0},{2,3},{3,2},{4,5},{5,4},{6,7},{7,6},{8,9},{9,8},{10,11... | collective-permute-start | bytes 2359304 | tf_op jit(solution)/shard_map/backward/ppermute | solution.py:396
  95.2 5.2 %collective-permute-start.13 = (bf16[1024,128]{1,0:T(8,128)(2,1)}, bf16[1024,128]{1,0:T(8,128)(2,1)S(1)}, u32[]{:S(2)}, u32[]{:S(2)}) collective-permute-start(bf16[1024,128]{1,0:T(8,128)(2,1)} %get-tuple-element.43.prob), channel_id=1, source_target_pairs={{0,1},{1,0},{2,3},{3,2},{4,5},{5,4},{6,7},{7,6},{8,9},{9,8},{10,11... | collective-permute-start | bytes 786440 | tf_op jit(solution)/shard_map/backward/ppermute | solution.py:396
  100.5 0.7 copy-start.12
  100.5 1.0 copy-start.7
  100.5 1.2 copy-start.8
  100.5 1.4 copy-start.9
  100.5 1.7 %copy-start.10 = (bf16[1024,384]{1,0:T(8,128)(2,1)}, bf16[1024,384]{1,0:T(8,128)(2,1)S(1)}, u32[]{:S(2)}) copy-start(bf16[1024,384]{1,0:T(8,128)(2,1)S(1)} %collective-permute-done.17.s3) | copy-start | bytes 2359300
  110.0 10.3 %copy-start.21 = (bf16[16,32,384]{2,1,0:T(8,128)(2,1)S(1)}, bf16[16,32,384]{2,1,0:T(8,128)(2,1)}, u32[]{:S(2)}) copy-start(bf16[16,32,384]{2,1,0:T(8,128)(2,1)} %get-tuple-element.54) | copy-start | bytes 1179652
  110.0 11.2 %copy-start.20 = (bf16[16,32,384]{2,1,0:T(8,128)(2,1)S(1)}, bf16[16,32,384]{2,1,0:T(8,128)(2,1)}, u32[]{:S(2)}) copy-start(bf16[16,32,384]{2,1,0:T(8,128)(2,1)} %get-tuple-element.55) | copy-start | bytes 1179652
  110.0 13.7 %copy-start.19 = (bf16[16,32,384]{2,1,0:T(8,128)(2,1)S(1)}, bf16[16,32,384]{2,1,0:T(8,128)(2,1)}, u32[]{:S(2)}) copy-start(bf16[16,32,384]{2,1,0:T(8,128)(2,1)} %get-tuple-element.56) | copy-start | bytes 1179652
  110.0 35.4 %all-to-all-start.3 = ((bf16[16,32,1664]{2,1,0:T(8,128)(2,1)}), bf16[16,32,1664]{2,1,0:T(8,128)(2,1)S(1)}, u32[]{:S(2)}, u32[]{:S(2)}) async-start(bf16[16,32,1664]{2,1,0:T(8,128)(2,1)} %get-tuple-element.49), calls=%async_computation.3 | async-start | bytes 3407872 | tf_op jit(solution)/shard_map/sums/all_to_all | solution.py:399
  120.3 23.2 %collective-permute-start.18 = (bf16[16,32,384]{2,1,0:T(8,128)(2,1)S(1)}, bf16[16,32,384]{2,1,0:T(8,128)(2,1)S(1)}, u32[]{:S(2)}, u32[]{:S(2)}) collective-permute-start(bf16[16,32,384]{2,1,0:T(8,128)(2,1)S(1)} %copy-done.21), channel_id=1, source_target_pairs={{0,2},{1,3},{2,4},{3,5},{4,6},{5,7},{6,0},{7,1},{8,10},{9,11},{10,... | collective-permute-start | bytes 1179656 | tf_op jit(solution)/shard_map/sums/ppermute | solution.py:391
  121.2 22.3 %collective-permute-start.19 = (bf16[16,32,384]{2,1,0:T(8,128)(2,1)S(1)}, bf16[16,32,384]{2,1,0:T(8,128)(2,1)S(1)}, u32[]{:S(2)}, u32[]{:S(2)}) collective-permute-start(bf16[16,32,384]{2,1,0:T(8,128)(2,1)S(1)} %copy-done.20), channel_id=1, source_target_pairs={{0,4},{1,5},{2,6},{3,7},{4,0},{5,1},{6,2},{7,3},{8,12},{9,13},{10,... | collective-permute-start | bytes 1179656 | tf_op jit(solution)/shard_map/sums/ppermute | solution.py:391
  123.7 19.8 %collective-permute-start.20 = (bf16[16,32,384]{2,1,0:T(8,128)(2,1)S(1)}, bf16[16,32,384]{2,1,0:T(8,128)(2,1)S(1)}, u32[]{:S(2)}, u32[]{:S(2)}) collective-permute-start(bf16[16,32,384]{2,1,0:T(8,128)(2,1)S(1)} %copy-done.19), channel_id=1, source_target_pairs={{0,6},{1,7},{2,0},{3,1},{4,2},{5,3},{6,4},{7,5},{8,14},{9,15},{10,... | collective-permute-start | bytes 1179656 | tf_op jit(solution)/shard_map/sums/ppermute | solution.py:391
  135.9 7.6 %copy-start.11 = (bf16[16,32,384]{2,1,0:T(8,128)(2,1)S(1)}, bf16[16,32,384]{2,1,0:T(8,128)(2,1)}, u32[]{:S(2)}) copy-start(bf16[16,32,384]{2,1,0:T(8,128)(2,1)} %get-tuple-element.53) | copy-start | bytes 1179652
  145.4 6.4 %copy-start.3 = (bf16[16,32,1664]{2,1,0:T(8,128)(2,1)}, bf16[16,32,1664]{2,1,0:T(8,128)(2,1)S(1)}, u32[]{:S(2)}) copy-start(bf16[16,32,1664]{2,1,0:T(8,128)(2,1)S(1)} %all-to-all-done.3) | copy-start | bytes 5111812
  145.4 14.5 %all-to-all-start.2 = ((bf16[16,32,384]{2,1,0:T(8,128)(2,1)}), bf16[16,32,384]{2,1,0:T(8,128)(2,1)S(1)}, u32[]{:S(2)}, u32[]{:S(2)}) async-start(bf16[16,32,384]{2,1,0:T(8,128)(2,1)} %add_convert_fusion), calls=%async_computation.2 | async-start | bytes 786432 | tf_op jit(solution)/shard_map/late_sum/all_to_all | solution.py:399
  154.9 6.9 %collective-permute-start.21 = (bf16[128,512]{1,0:T(8,128)(2,1)}, bf16[128,512]{1,0:T(8,128)(2,1)S(1)}, u32[]{:S(2)}, u32[]{:S(2)}) collective-permute-start(bf16[128,512]{1,0:T(8,128)(2,1)} %get-tuple-element.59), channel_id=1, source_target_pairs={{0,2},{1,3},{2,4},{3,5},{4,6},{5,7},{6,0},{7,1},{8,10},{9,11},{10,... | collective-permute-start | bytes 393224 | tf_op jit(solution)/shard_map/finish/ppermute | solution.py:391
  155.7 7.5 %collective-permute-start.22 = (bf16[128,512]{1,0:T(8,128)(2,1)}, bf16[128,512]{1,0:T(8,128)(2,1)S(1)}, u32[]{:S(2)}, u32[]{:S(2)}) collective-permute-start(bf16[128,512]{1,0:T(8,128)(2,1)} %get-tuple-element.60), channel_id=1, source_target_pairs={{0,4},{1,5},{2,6},{3,7},{4,0},{5,1},{6,2},{7,3},{8,12},{9,13},{10,... | collective-permute-start | bytes 393224 | tf_op jit(solution)/shard_map/finish/ppermute | solution.py:391
  158.2 5.4 %collective-permute-start.23 = (bf16[128,512]{1,0:T(8,128)(2,1)}, bf16[128,512]{1,0:T(8,128)(2,1)S(1)}, u32[]{:S(2)}, u32[]{:S(2)}) collective-permute-start(bf16[128,512]{1,0:T(8,128)(2,1)} %get-tuple-element.61), channel_id=1, source_target_pairs={{0,6},{1,7},{2,0},{3,1},{4,2},{5,3},{6,4},{7,5},{8,14},{9,15},{10,... | collective-permute-start | bytes 393224 | tf_op jit(solution)/shard_map/finish/ppermute | solution.py:391
  159.9 3.8 %copy-start.6 = (bf16[16,32,384]{2,1,0:T(8,128)(2,1)}, bf16[16,32,384]{2,1,0:T(8,128)(2,1)S(1)}, u32[]{:S(2)}) copy-start(bf16[16,32,384]{2,1,0:T(8,128)(2,1)S(1)} %all-to-all-done.2) | copy-start | bytes 1179652
  161.8 1.9 %copy-start.13 = (bf16[128,512]{1,0:T(8,128)(2,1)}, bf16[128,512]{1,0:T(8,128)(2,1)S(1)}, u32[]{:S(2)}) copy-start(bf16[128,512]{1,0:T(8,128)(2,1)S(1)} %collective-permute-done.21.m1) | copy-start | bytes 393220
  163.7 0.6 copy-start.15
  (2 other events, 1.3 us)

commit v3 on v2

--- a/solution.py
+++ b/solution.py
@@ -7,7 +7,7 @@
 
 BF = jnp.bfloat16
 F32 = jnp.float32
-VMEM_LIMIT = 56 * 1024 * 1024
+VMEM_LIMIT = 62 * 1024 * 1024
 EXPERTS = 8
 CAP = 64
 EARLY = 32
@@ -154,16 +154,14 @@
     return total.astype(BF)
 
 
-def back_body(t, own, sib, act, slope, hidden, wd, wg, wu, grads, prob, *refs):
-    parts = refs[:4]
-    own_v, sib_v, act_v, slope_v, hidden_v, wd_o, wd_s, w_v, grads_v, prob_v, part_v, sems = refs[4:]
+def back_body(t, own, sib, act, slope, hidden, wd, grads, prob, *refs):
+    own_v, sib_v, act_v, slope_v, hidden_v, wd_o, wd_s, grads_v, prob_v, sems = refs
     copies = Copies(sems)
     pairs = ((own, own_v), (sib, sib_v), (act, act_v), (slope, slope_v), (hidden, hidden_v))
     rows = chunks(256)
     wd_in = down_columns(copies, t, wd, wd_o, False)
     ins = [[copies.start(a.at[rows[0]], b.at[rows[0]]) for a, b in pairs]]
     wd_in += down_columns(copies, t, wd, wd_s, True)
-    w_in = gate_up_rows(copies, t, wg, wu, w_v, range(4), True)
     ins += [[copies.start(a.at[c], b.at[c]) for a, b in pairs] for c in rows[1:]]
     done = []
     for i, c in enumerate(rows):
@@ -179,46 +177,59 @@
         )
         grads_v[c, 0:HID] = (back * slope_v[c]).astype(BF)
         grads_v[c, HID : 2 * HID] = (back * act_v[c]).astype(BF)
-        if i == 0:
-            wait_all(w_in)
-        part_v[c] = dot(grads_v[c], w_v[...], NT).astype(BF)
         done.append(copies.start(grads_v.at[c], grads.at[c]))
         done.append(copies.start(prob_v.at[c], prob.at[c]))
+    wait_all(done)
+
+
+STEP = 4
+
+
+def own_part_body(t, grads, wg, wu, out, g_v, w_v, out_v, sems):
+    copies = Copies(sems)
+    rows = chunks(256)
+    ins = [copies.start(grads.at[rows[0]], g_v.at[rows[0]])]
+    w_in = gate_up_rows(copies, t, wg, wu, w_v, range(4), False)
+    ins += [copies.start(grads.at[c], g_v.at[c]) for c in rows[1:]]
+    wait_all(w_in)
+    done = []
+    for c, started in zip(rows, ins):
+        started.wait()
+        out_v[c] = dot(g_v[c], w_v[...], NT).astype(BF)
+        done.append(copies.start(out_v.at[c], out.at[c]))
+    wait_all(done)
+
+
+def sums_body(t, own, grads_sib, prob, prob_sib, sib_wg, sib_wu, early, *refs):
+    late, (own_v, g_v, p_v, q_v, w_v, early_v, late_v, sems) = refs[:4], refs[4:]
+    copies = Copies(sems)
+    blocks = [slice(i, i + STEP) for i in range(0, 16, STEP)]
+    pairs = ((grads_sib, g_v), (own, own_v), (prob, p_v), (prob_sib, q_v))
+    ins = [[copies.start(x.at[blocks[0]], v.at[blocks[0]]) for x, v in pairs]]
+    w_in = []
+    for dy in range(4):
+        y = (t[0] // 2 + dy) % 4
+        w_in.append(copies.start(sib_wg.at[y], w_v.at[lanes(dy), 0:HID]))
+        w_in.append(copies.start(sib_wu.at[y], w_v.at[lanes(dy), HID : 2 * HID]))
+    ins += [[copies.start(x.at[b], v.at[b]) for x, v in pairs] for b in blocks[1:]]
+    wait_all(w_in)
+    done = []
+    for b, started in zip(blocks, ins):
+        wait_all(started)
+        part = dot(g_v[b].reshape(STEP * CAP, 2 * HID), w_v[...], NT)
         for dy in range(4):
-            done.append(copies.start(part_v.at[c, lanes(dy)], parts[dy].at[c]))
-    wait_all(done)
-
-
-def sums_body(t, grads, prob, prob_sib, s0, s1, s2, s3, wg, wu, early, *refs):
-    late, (grads_v, prob_v, sib_v) = refs[:4], refs[4:7]
-    s_v, w_v, early_v, late_v, sems = refs[7:]
-    copies = Copies(sems)
-    w_in = gate_up_rows(copies, t, wg, wu, w_v, range(4), False)
-    rows = chunks(256)
-    ins = [
-        [copies.start(a.at[c], b.at[c]) for a, b in ((grads, grads_v), (prob, prob_v), (prob_sib, sib_v))]
-        + [copies.start(s.at[c], s_v.at[dy, c]) for dy, s in enumerate((s0, s1, s2, s3))]
-        for c in rows
-    ]
-    wait_all(w_in)
-    done = []
-    for i, (c, started) in enumerate(zip(rows, ins)):
-        wait_all(started)
-        blocks = slice(i * 256 // CAP, (i + 1) * 256 // CAP)
-        part = dot(grads_v[c], w_v[...], NT)
+            value = part[:, lanes(dy)].reshape(STEP, CAP, COLS)
+            value = (value + own_v[b, :, lanes(dy)].astype(F32)).astype(BF)
+            early_v[b, :, lanes(dy)] = value[:, 0:EARLY]
+            late_v[dy, b] = value[:, EARLY:CAP]
+        both = p_v[b].astype(F32) + q_v[b].astype(F32)
+        both = jnp.sum(both, axis=2, keepdims=True)
+        early_v[b, :, 4 * COLS : 4 * COLS + 128] = split_lanes(
+            both[:, 0:EARLY], both[:, EARLY:CAP]
+        )
+        done.append(copies.start(early_v.at[b], early.at[b]))
         for dy in range(4):
-            value = (part[:, lanes(dy)] + s_v[dy, c].astype(F32)).astype(BF)
-            value = value.reshape(256 // CAP, CAP, COLS)
-            early_v[blocks, :, lanes(dy)] = value[:, 0:EARLY]
-            late_v[dy, blocks] = value[:, EARLY:CAP]
-        both = prob_v[c].astype(F32) + sib_v[c].astype(F32)
-        both = jnp.sum(both, axis=1, keepdims=True).reshape(256 // CAP, CAP, 1)
-        early_v[blocks, :, 4 * COLS : 4 * COLS + 128] = split_lanes(
-            both[:, 0:EARLY], both[:, EARLY:CAP]
-        )
-        done.append(copies.start(early_v.at[blocks], early.at[blocks]))
-        for dy in range(4):
-            done.append(copies.start(late_v.at[dy, blocks], late[dy].at[blocks]))
+            done.append(copies.start(late_v.at[dy, b], late[dy].at[b]))
     wait_all(done)
 
 
@@ -334,16 +345,16 @@
     wait_all(done)
 
 
-def selection(routes):
-    first, second, slot = slot_masks(routes)
+def selection(masks, at, choice=None):
+    first, second, slot = masks
     hots = [one_hot(slot, e) for e in range(EXPERTS)]
-    kinds = [hots]
-    for mask in (first, second):
-        kinds.append([hots[e] * jnp.where(mask[e : e + 1, :], 1.0, 0.0) for e in range(EXPERTS)])
-    return [
-        [jnp.concatenate([h[at] for h in kind], axis=0).astype(BF) for kind in kinds]
-        for at in (slice(0, EARLY), slice(EARLY, CAP))
-    ]
+    if choice is not None:
+        mask = (first, second)[choice]
+        hots = [hots[e] * jnp.where(mask[e : e + 1, :], 1.0, 0.0) for e in range(EXPERTS)]
+    return jnp.concatenate([h[at] for h in hots], axis=0).astype(BF)
+
+
+EARLY_SLOTS, LATE_SLOTS = slice(0, EARLY), slice(EARLY, CAP)
 
 
 def from_slots(select, rows, cols):
@@ -352,13 +363,14 @@
 
 
 def combine_body(routes, rows, own, own_lanes, m1, m2, m3):
-    early, late = selection(routes[...])
-    total = from_slots(early[0], rows, slice(0, 4 * COLS))
+    masks = slot_masks(routes[...])
+    total = from_slots(selection(masks, EARLY_SLOTS), rows, slice(0, 4 * COLS))
     own[...] = total[:, 0:COLS]
     at = slice(4 * COLS, 4 * COLS + 128)
     probs = []
-    for k in (1, 2):
-        a, b = from_slots(early[k], rows, at), from_slots(late[k], rows, at)
+    for k in range(2):
+        a = from_slots(selection(masks, EARLY_SLOTS, k), rows, at)
+        b = from_slots(selection(masks, LATE_SLOTS, k), rows, at)
         probs.append(a[:, 0:1] + a[:, 1:2] + b[:, 2:3] + b[:, 3:4])
     prob_lanes = split_lanes(*probs)
     own_lanes[...] = prob_lanes
@@ -368,8 +380,8 @@
 
 
 def finish_body(routes, probs, rows, own, own_lanes, m1, m2, m3, out, prob_out):
-    _, late = selection(routes[...])
-    total = from_slots(late[0], rows, slice(0, COLS)) + own[...]
+    late = selection(slot_masks(routes[...]), LATE_SLOTS)
+    total = from_slots(late, rows, slice(0, COLS)) + own[...]
     prob_lanes = own_lanes[...].astype(F32)
     for m in (m1, m2, m3):
         total += m[:, 0:COLS].astype(F32)
@@ -417,6 +429,13 @@
         near_xs += [from_sibling(x) for x in near_xs]
         far_xs = [from_y(down1[:HALF], 3), from_y(up1[HALF:], 1)]
         g_got = exchange(after(send_g, x0))
+        core = t[0] % 2
+
+        def sibling_rows(w):
+            its = lax.dynamic_index_in_dim(w.reshape(4, 2, COLS, HID), 1 - core, 1, False)
+            return from_sibling(after(its, x0))
+
+        sib_wg, sib_wu = sibling_rows(wg), sibling_rows(wu)
     with jax.named_scope("forward"):
         (near,) = plain_call(
             near_forward_body,
@@ -429,7 +448,7 @@
             1,
         )
         far_xs += [from_sibling(after(x, near)) for x in far_xs]
-        g_own = after(g_got, *far_xs)
+        g_own = after(g_got, sib_wg, sib_wu, *far_xs)
         g_sib = from_sibling(g_own)
         act, slope, hidden = plain_call(
             forward_body,
@@ -443,43 +462,55 @@
             1,
         )
     with jax.named_scope("backward"):
-        got = plain_call(
+        grads, prob = plain_call(
             back_body,
             t,
-            [g_own, g_sib, act, slope, hidden, wd, wg, wu],
-            [sds((ROWS, 2 * HID)), sds((ROWS, 128))] + [sds((ROWS, COLS))] * 4,
+            [g_own, g_sib, act, slope, hidden, wd],
+            [sds((ROWS, 2 * HID)), sds((ROWS, 128))],
             [((ROWS, wide), BF)] * 2
             + [((ROWS, HID), F32)] * 2
-            + [((ROWS, HID), BF), ((HID, wide), BF), ((HID, wide), BF), ((wide, 2 * HID), BF)]
-            + [((ROWS, 2 * HID), BF), ((ROWS, 128), BF), ((ROWS, wide), BF)],
-            60,
-            1,
-            1,
-        )
-        grads, prob = got[:2]
-        prob_sib = from_sibling(prob)
-        part_sib = [from_sibling(p) for p in got[2:]]
+            + [((ROWS, HID), BF), ((HID, wide), BF), ((HID, wide), BF)]
+            + [((ROWS, 2 * HID), BF), ((ROWS, 128), BF)],
+            36,
+            1,
+            1,
+        )
+        grads_sib, prob_sib = from_sibling(grads), from_sibling(prob)
+
+    def blocks(x):
+        return x.reshape(16, CAP, x.shape[1])
+
     with jax.named_scope("sums"):
-        sums = plain_call(
+        (own_part,) = plain_call(
+            own_part_body,
+            t,
+            [grads, wg, wu],
+            [sds((ROWS, wide))],
+            [((ROWS, 2 * HID), BF), ((wide, 2 * HID), BF), ((ROWS, wide), BF)],
+            16,
+            1,
+            1,
+        )
+        early, *late = plain_call(
             sums_body,
             t,
-            [grads, prob, prob_sib] + part_sib + [wg, wu],
+            [blocks(x) for x in (own_part, grads_sib, prob, prob_sib)] + [sib_wg, sib_wu],
             [sds((16, EARLY, wide + 128))] + [sds((16, CAP - EARLY, COLS))] * 4,
-            [((ROWS, 2 * HID), BF), ((ROWS, 128), BF), ((ROWS, 128), BF)]
-            + [((4, ROWS, COLS), BF), ((wide, 2 * HID), BF), ((16, EARLY, wide + 128), BF)]
+            [((16, CAP, wide), BF), ((16, CAP, 2 * HID), BF)]
+            + [((16, CAP, 128), BF), ((16, CAP, 128), BF)]
+            + [((wide, 2 * HID), BF), ((16, EARLY, wide + 128), BF)]
             + [((4, 16, CAP - EARLY, COLS), BF)],
-            56,
-            1,
-            1,
-        )
-        early, late = sums[0], sums[1:]
+            44,
+            1,
+            1,
+        )
+        early_rows = exchange(early)
         arrived = [from_y(late[dy], 4 - dy) for dy in (1, 2, 3)]
-        early_rows = exchange(early)
     with jax.named_scope("weights_gate_up"):
         grad_gate, grad_up = plain_call(
             weights_gate_up_body,
             t,
-            [after(grads, early)] + near_xs + far_xs,
+            [after(grads, late[0])] + near_xs + far_xs,
             [sds((8 * COLS, HID))] * 2,
             [((ROWS, 2 * HID), BF), ((8, ROWS, COLS), BF)] + [((8 * COLS, HID), BF)] * 2,
             27,

time: 167 us -> 162 us (0.970)
  waiting for transfers between devices: 36.7 us -> 27.6 us
  Pallas kernels: 65.7 us -> 67.7 us
    ppermute x11 -> x10, waiting for transfers between devices: 7.1 us -> 1.99 us  [from_sibling(): return lax.ppermute(x, 'tensor', [(i, i ^ 1) for i in range(8)])]
    ppermute x13, waiting for transfers between devices: 28 us -> 24.2 us  [from_y(): lax.ppermute(x, 'tensor', [(i, (i // 2 - dy) % 4 * 2 + i % 2) for i in ra...]
    squeeze x0 -> x1, local copies, waits for them, and re-layouts: none -> 3.43 us  [sibling_rows(): lax.dynamic_index_in_dim(w.reshape(4, 2, COLS, HID), 1 - core, 1, False)]
    unnamed x44 -> x32, local copies, waits for them, and re-layouts: 6.28 us -> 3.35 us
    pallas_call x6 -> x7, Pallas kernels: 54.7 us -> 56.7 us  [plain_call(): pl.pallas_call(body, out_shape=outs, in_specs=[pl.BlockSpec(memory_space=...]
  transfers between devices with their start and end apart: 28 -> 27, of which waited for: 14 -> 11; matrix products, arithmetic and copies ran while one was open for 3% -> 6% of each run, Pallas kernels for 25% -> 29%
where the time goes in v3:
time: 162 us
  Pallas kernels  67.7 us (42%)
  starting transfers between devices  53 us (33%)
  waiting for transfers between devices  27.6 us (17%)
  local copies, waits for them, and re-layouts  10.4 us (6%)
  other arithmetic  2.3 us (1%)
    pallas_call x7, Pallas kernels, plain_call(): pl.pallas_call(body, out_shape=outs, in_specs=[pl.BlockSpec(memory_space=...  56.7 us
    all_to_all x4, starting transfers between devices, exchange(): lax.all_to_all(x, ('dp', 'ctx'), split_axis=0, concat_axis=0, tiled=True)  33.3 us
    ppermute x13, waiting for transfers between devices, from_y(): lax.ppermute(x, 'tensor', [(i, (i // 2 - dy) % 4 * 2 + i % 2) for i in ra...  24.2 us
    ppermute x13, starting transfers between devices, from_y(): lax.ppermute(x, 'tensor', [(i, (i // 2 - dy) % 4 * 2 + i % 2) for i in ra...  18.1 us
    slice x2, local copies, waits for them, and re-layouts, on_device(): far_xs = [from_y(down1[:HALF], 3), from_y(up1[HALF:], 1)]  3.57 us
    squeeze x1, local copies, waits for them, and re-layouts, sibling_rows(): lax.dynamic_index_in_dim(w.reshape(4, 2, COLS, HID), 1 - core, 1, False)  3.43 us
    pallas_call x1, Pallas kernels, on_device(): call(dispatch_g_body, sds((16, CAP, wide)), flops=2 * 10 ** 8, nbytes=4 *...  3.41 us
    unnamed x32, local copies, waits for them, and re-layouts  3.35 us
  transfers between devices with their start and end apart: 27, of which 11 were waited for; matrix products, arithmetic and copies ran while one was open for 6% of the time, Pallas kernels for 29%

profile of v3, /device:TPU:2, one launch (start us, length us, event | category | flops | bytes accessed | tf_op | source)
XLA Modules:
  0.0 161.7 jit_solution(12484669420372664478)
XLA Ops:
  0.6 2.2 %dispatch.3 = bf16[16,64,384]{2,1,0:T(8,128)(2,1)} custom-call(s32[2,128]{1,0:T(2,128)} %bitcast.47, bf16[128,384]{1,0:T(8,128)(2,1)} %tokens.1), custom_call_target="tpu_custom_call" | custom-call | flops 100000000 | bytes 1048576 | tf_op jit(solution)/shard_map/dispatch/pallas_call | solution.py:421
  2.8 8.3 %all-to-all-start = ((bf16[16,64,384]{2,1,0:T(8,128)(2,1)}), bf16[16,64,384]{2,1,0:T(8,128)(2,1)S(1)}, u32[]{:S(2)}, u32[]{:S(2)}) async-start(bf16[16,64,384]{2,1,0:T(8,128)(2,1)} %dispatch.3), calls=%async_computation | async-start | bytes 1572864 | tf_op jit(solution)/shard_map/dispatch/all_to_all | solution.py:411
  11.1 3.2 %collective-permute-start.1 = (bf16[128,384]{1,0:T(8,128)(2,1)}, bf16[128,384]{1,0:T(8,128)(2,1)S(1)}, u32[]{:S(2)}, u32[]{:S(2)}) collective-permute-start(bf16[128,384]{1,0:T(8,128)(2,1)} %g0.1), channel_id=1, source_target_pairs={{0,4},{1,5},{2,6},{3,7},{4,0},{5,1},{6,2},{7,3},{8,12},{9,13},{10,... | collective-permute-start | bytes 294920 | tf_op jit(solution)/shard_map/dispatch/ppermute | solution.py:403
  14.3 1.1 collective-permute-start
  15.4 1.0 collective-permute-start.2
  16.3 1.8 %collective-permute-done.1.g2 = bf16[128,384]{1,0:T(8,128)(2,1)S(1)} collective-permute-done((bf16[128,384]{1,0:T(8,128)(2,1)}, bf16[128,384]{1,0:T(8,128)(2,1)S(1)}, u32[]{:S(2)}, u32[]{:S(2)}) %collective-permute-start.1) | collective-permute-done | bytes 98336 | tf_op jit(solution)/shard_map/dispatch/ppermute | solution.py:403
  18.1 1.2 collective-permute-done.g1
  19.3 2.1 %collective-permute-done.2.g3 = bf16[128,384]{1,0:T(8,128)(2,1)S(1)} collective-permute-done((bf16[128,384]{1,0:T(8,128)(2,1)}, bf16[128,384]{1,0:T(8,128)(2,1)S(1)}, u32[]{:S(2)}, u32[]{:S(2)}) %collective-permute-start.2) | collective-permute-done | bytes 98336 | tf_op jit(solution)/shard_map/dispatch/ppermute | solution.py:403
  21.4 0.6 copy-done.15
  22.0 3.4 %dispatch.2 = bf16[16,64,1536]{2,1,0:T(8,128)(2,1)} custom-call(s32[2,128]{1,0:T(2,128)} %bitcast.48, bf16[2,128]{1,0:T(2,128)(2,1)} %bitcast.51, bf16[128,384]{1,0:T(8,128)(2,1)} %g0.1, bf16[128,384]{1,0:T(8,128)(2,1)} %copy-done.14, bf16[128,384]{1,0:T(8,128)(2,1)} %copy-done.13, bf16[128,384]{1,0:T(8,128)(2,1)} %copy-done.15), custom_call_target="tpu_custom_call" | custom-call | flops 200000000 | bytes 4194304 | tf_op jit(solution)/shard_map/dispatch/pallas_call | solution.py:423
  25.4 0.9 copy-done.1
  26.3 7.5 %all-to-all-start.1 = ((bf16[16,64,1536]{2,1,0:T(8,128)(2,1)}), bf16[16,64,1536]{2,1,0:T(8,128)(2,1)}, u32[]{:S(2)}, u32[]{:S(2)}) async-start(bf16[16,64,1536]{2,1,0:T(8,128)(2,1)} %dispatch.2), calls=%async_computation.1 | async-start | bytes 6291456 | tf_op jit(solution)/shard_map/gather/all_to_all | solution.py:411
  33.8 0.6 collective-permute-start.7
  34.4 1.5 collective-permute-start.5
  35.9 3.4 %dynamic-slice_bitcast_fusion = (bf16[4,384,512]{2,1,0:T(8,128)(2,1)}, bf16[4,384,512]{2,1,0:T(8,128)(2,1)}) fusion(bf16[4,2,384,512]{3,2,1,0:T(8,128)(2,1)} %bitcast.32, s32[]{:T(128)S(6)} %select_n.13, bf16[4,2,384,512]{3,2,1,0:T(8,128)(2,1)S(1)} %bitcast.31), kind=kLoop, calls=%fused_computation | loop fusion | bytes 6291460 | tf_op jit(solution)/shard_map/gather/jit(dynamic_index_in_dim)/squeeze | solution.py:435
  39.3 11.6 %collective-permute-done.7.refs_1_ = bf16[1024,384]{1,0:T(8,128)(2,1)} collective-permute-done((bf16[1024,384]{1,0:T(8,128)(2,1)}, bf16[1024,384]{1,0:T(8,128)(2,1)}, u32[]{:S(2)}, u32[]{:S(2)}) %collective-permute-start.7) | collective-permute-done | bytes 786464 | tf_op jit(solution)/shard_map/gather/ppermute | solution.py:403
  50.9 0.5 collective-permute-start.3
  51.4 2.1 %collective-permute-done.5.refs_2_ = bf16[1024,384]{1,0:T(8,128)(2,1)} collective-permute-done((bf16[1024,384]{1,0:T(8,128)(2,1)}, bf16[1024,384]{1,0:T(8,128)(2,1)}, u32[]{:S(2)}, u32[]{:S(2)}) %collective-permute-start.5) | collective-permute-done | bytes 786464 | tf_op jit(solution)/shard_map/gather/ppermute | solution.py:403
  53.5 1.8 %slice.9 = bf16[512,384]{1,0:T(8,128)(2,1)} slice(bf16[1024,384]{1,0:T(8,128)(2,1)} %collective-permute-done.7.refs_1_), slice={[512:1024], [0:384]} | slice | bytes 786432 | tf_op jit(solution)/shard_map/gather/slice | solution.py:430
  55.3 1.3 collective-permute-start.8
  56.6 1.8 %slice.8 = bf16[512,384]{1,0:T(8,128)(2,1)} slice(bf16[1024,384]{1,0:T(8,128)(2,1)} %collective-permute-done.5.refs_2_), slice={[0:512], [0:384]} | slice | bytes 786432 | tf_op jit(solution)/shard_map/gather/slice | solution.py:430
  58.4 0.7 collective-permute-start.6
  59.3 9.5 %forward.2.refs_4_ = f32[1024,1024]{1,0:T(8,128)} custom-call(s32[1]{0:T(128)} %bitcast.2.t, bf16[1024,384]{1,0:T(8,128)(2,1)} %bitcast.39, bf16[1024,384]{1,0:T(8,128)(2,1)} %collective-permute-done.7.refs_1_, bf16[1024,384]{1,0:T(8,128)(2,1)} %collective-permute-done.5.refs_2_, bf16[1024,384]{1,0:T(8,128)(2,1)} %copy-done.4, bf16[1024,384]{1,0:T(8,128)(2,1)} %copy-done.5, ...), custom_call_target="tpu_custom_call" | custom-call | flops 1 | bytes 1 | tf_op jit(solution)/shard_map/forward/pallas_call | solution.py:88
  68.8 1.8 %collective-permute-done.6.refs_0_.refs_6_ = bf16[512,384]{1,0:T(8,128)(2,1)} collective-permute-done((bf16[512,384]{1,0:T(8,128)(2,1)}, bf16[512,384]{1,0:T(8,128)(2,1)}, u32[]{:S(2)}, u32[]{:S(2)}) %collective-permute-start.6) | collective-permute-done | bytes 393248 | tf_op jit(solution)/shard_map/gather/ppermute | solution.py:403
  70.7 0.5 collective-permute-start.13
  71.2 1.9 %collective-permute-done.12.refs_2_.refs_8_ = bf16[512,384]{1,0:T(8,128)(2,1)S(1)} collective-permute-done((bf16[512,384]{1,0:T(8,128)(2,1)}, bf16[512,384]{1,0:T(8,128)(2,1)S(1)}, u32[]{:S(2)}, u32[]{:S(2)}) %collective-permute-start.12) | collective-permute-done | bytes 393248 | tf_op jit(solution)/shard_map/forward/ppermute | solution.py:408
  73.1 0.5 all-to-all-done.1
  74.0 5.8 %forward.3 = (f32[1024,512]{1,0:T(8,128)}, f32[1024,512]{1,0:T(8,128)}, bf16[1024,512]{1,0:T(8,128)(2,1)}) custom-call(s32[1]{0:T(128)} %bitcast.2.t, bf16[512,384]{1,0:T(8,128)(2,1)} %collective-permute-done.6.refs_0_.refs_6_, bf16[512,384]{1,0:T(8,128)(2,1)} %copy-done.6, bf16[512,384]{1,0:T(8,128)(2,1)} %copy-done.7, bf16[512,384]{1,0:T(8,128)(2,1)} %copy-done.8, ...), custom_call_target="tpu_custom_call" | custom-call | flops 1 | bytes 1 | tf_op jit(solution)/shard_map/forward/pallas_call | solution.py:88
  79.8 8.3 %backward.1 = (bf16[1024,1024]{1,0:T(8,128)(2,1)}, bf16[1024,128]{1,0:T(8,128)(2,1)}) custom-call(s32[1]{0:T(128)} %bitcast.2.t, bf16[1024,1536]{1,0:T(8,128)(2,1)} %bitcast.4.own, bf16[1024,1536]{1,0:T(8,128)(2,1)} %collective-permute-done.14.sib, f32[1024,512]{1,0:T(8,128)} %get-tuple-element.39.act, f32[1024,512]{1,0:T(8,128)} %get-tuple-element.40.slope, ...), custom_call_target="tpu_custom_call" | custom-call | flops 1 | bytes 1 | tf_op jit(solution)/shard_map/backward/pallas_call | solution.py:88
  88.7 7.1 %sums.2 = bf16[1024,1536]{1,0:T(8,128)(2,1)} custom-call(s32[1]{0:T(128)} %bitcast.2.t, bf16[1024,1024]{1,0:T(8,128)(2,1)} %get-tuple-element.45.grads, bf16[3072,512]{1,0:T(8,128)(2,1)} %bitcast.30, bf16[3072,512]{1,0:T(8,128)(2,1)} %bitcast.35), custom_call_target="tpu_custom_call" | custom-call | flops 1 | bytes 1 | tf_op jit(solution)/shard_map/sums/pallas_call | solution.py:88
  95.7 0.7 copy-done.9
  96.4 7.6 %sums.3 = (bf16[16,32,1664]{2,1,0:T(8,128)(2,1)}, bf16[16,32,384]{2,1,0:T(8,128)(2,1)}, bf16[16,32,384]{2,1,0:T(8,128)(2,1)}, bf16[16,32,384]{2,1,0:T(8,128)(2,1)}, bf16[16,32,384]{2,1,0:T(8,128)(2,1)}) custom-call(s32[1]{0:T(128)} %bitcast.2.t, bf16[16,64,1536]{2,1,0:T(8,128)(2,1)} %bitcast.36, bf16[16,64,1024]{2,1,0:T(8,128)(2,1)} %bitcast.13.grads_sib, ...), custom_call_target="tpu_custom_call" | custom-call | flops 1 | bytes 1 | tf_op jit(solution)/shard_map/sums/pallas_call | solution.py:88
  104.1 10.3 %all-to-all-start.3 = ((bf16[16,32,1664]{2,1,0:T(8,128)(2,1)}), bf16[16,32,1664]{2,1,0:T(8,128)(2,1)S(1)}, u32[]{:S(2)}, u32[]{:S(2)}) async-start(bf16[16,32,1664]{2,1,0:T(8,128)(2,1)} %get-tuple-element.52), calls=%async_computation.3 | async-start | bytes 3407872 | tf_op jit(solution)/shard_map/sums/all_to_all | solution.py:411
  114.3 0.8 collective-permute-start.17
  115.2 2.5 %collective-permute-start.18 = (bf16[16,32,384]{2,1,0:T(8,128)(2,1)}, bf16[16,32,384]{2,1,0:T(8,128)(2,1)}, u32[]{:S(2)}, u32[]{:S(2)}) collective-permute-start(bf16[16,32,384]{2,1,0:T(8,128)(2,1)} %get-tuple-element.50), channel_id=1, source_target_pairs={{0,4},{1,5},{2,6},{3,7},{4,0},{5,1},{6,2},{7,3},{8,12},{9,13},{10,... | collective-permute-start | bytes 1179656 | tf_op jit(solution)/shard_map/sums/ppermute | solution.py:403
  117.7 1.3 collective-permute-start.19
  119.0 10.9 %weights_gate_up.1 = (bf16[3072,512]{1,0:T(8,128)(2,1)}, bf16[3072,512]{1,0:T(8,128)(2,1)}) custom-call(s32[1]{0:T(128)} %bitcast.2.t, bf16[1024,1024]{1,0:T(8,128)(2,1)} %get-tuple-element.45.grads, bf16[1024,384]{1,0:T(8,128)(2,1)} %bitcast.40, bf16[1024,384]{1,0:T(8,128)(2,1)} %collective-permute-done.7.refs_1_, ...), custom_call_target="tpu_custom_call" | custom-call | flops 1 | bytes 1 | tf_op jit(solution)/shard_map/weights_gate_up/pallas_call | solution.py:88
  129.9 7.5 %weights_down.1 = bf16[512,3072]{1,0:T(8,128)(2,1)} custom-call(s32[1]{0:T(128)} %bitcast.2.t, bf16[1024,512]{1,0:T(8,128)(2,1)} %get-tuple-element.47.hidden, bf16[1024,1536]{1,0:T(8,128)(2,1)} %bitcast.4.own, bf16[1024,1536]{1,0:T(8,128)(2,1)} %collective-permute-done.14.sib), custom_call_target="tpu_custom_call" | custom-call | flops 1 | bytes 1 | tf_op jit(solution)/shard_map/weights_down/pallas_call | solution.py:88
  137.5 2.3 %add_convert_fusion = bf16[16,32,384]{2,1,0:T(8,128)(2,1)} fusion(bf16[16,32,384]{2,1,0:T(8,128)(2,1)} %collective-permute-done.19, bf16[16,32,384]{2,1,0:T(8,128)(2,1)} %collective-permute-done.18, bf16[16,32,384]{2,1,0:T(8,128)(2,1)} %collective-permute-done.17, bf16[16,32,384]{2,1,0:T(8,128)(2,1)} %get-tuple-element.48), kind=kLoop, calls=%fused_computation.2 | loop fusion | flops 1572864 | bytes 1966080 | tf_op jit(solution)/shard_map/late_sum/convert_element_type | solution.py:534
  139.8 7.2 %all-to-all-start.2 = ((bf16[16,32,384]{2,1,0:T(8,128)(2,1)}), bf16[16,32,384]{2,1,0:T(8,128)(2,1)}, u32[]{:S(2)}, u32[]{:S(2)}) async-start(bf16[16,32,384]{2,1,0:T(8,128)(2,1)} %add_convert_fusion), calls=%async_computation.2 | async-start | bytes 786432 | tf_op jit(solution)/shard_map/late_sum/all_to_all | solution.py:411
  147.0 3.1 %finish.2 = (f32[128,384]{1,0:T(8,128)}, bf16[128,128]{1,0:T(8,128)(2,1)}, bf16[128,512]{1,0:T(8,128)(2,1)}, bf16[128,512]{1,0:T(8,128)(2,1)}, bf16[128,512]{1,0:T(8,128)(2,1)}) custom-call(s32[2,128]{1,0:T(2,128)} %bitcast.49, bf16[512,1664]{1,0:T(8,128)(2,1)} %bitcast.42), custom_call_target="tpu_custom_call" | custom-call | flops 1 | bytes 1 | tf_op jit(solution)/shard_map/finish/pallas_call | solution.py:537
  150.1 0.7 collective-permute-start.20
  150.8 1.7 %collective-permute-start.21 = (bf16[128,512]{1,0:T(8,128)(2,1)}, bf16[128,512]{1,0:T(8,128)(2,1)S(1)}, u32[]{:S(2)}, u32[]{:S(2)}) collective-permute-start(bf16[128,512]{1,0:T(8,128)(2,1)} %get-tuple-element.56), channel_id=1, source_target_pairs={{0,4},{1,5},{2,6},{3,7},{4,0},{5,1},{6,2},{7,3},{8,12},{9,13},{10,... | collective-permute-start | bytes 393224 | tf_op jit(solution)/shard_map/finish/ppermute | solution.py:403
  152.5 1.8 %collective-permute-start.22 = (bf16[128,512]{1,0:T(8,128)(2,1)}, bf16[128,512]{1,0:T(8,128)(2,1)S(1)}, u32[]{:S(2)}, u32[]{:S(2)}) collective-permute-start(bf16[128,512]{1,0:T(8,128)(2,1)} %get-tuple-element.57), channel_id=1, source_target_pairs={{0,6},{1,7},{2,0},{3,1},{4,2},{5,3},{6,4},{7,5},{8,14},{9,15},{10,... | collective-permute-start | bytes 393224 | tf_op jit(solution)/shard_map/finish/ppermute | solution.py:403
  154.2 0.9 all-to-all-done.2
  155.1 3.4 %collective-permute-done.20.m1 = bf16[128,512]{1,0:T(8,128)(2,1)S(1)} collective-permute-done((bf16[128,512]{1,0:T(8,128)(2,1)}, bf16[128,512]{1,0:T(8,128)(2,1)S(1)}, u32[]{:S(2)}, u32[]{:S(2)}) %collective-permute-start.20) | collective-permute-done | bytes 131104 | tf_op jit(solution)/shard_map/finish/ppermute | solution.py:403
  158.7 0.4 copy-done.10
  159.4 2.3 %finish.3 = (bf16[128,384]{1,0:T(8,128)(2,1)}, f32[2,128]{1,0:T(2,128)}) custom-call(s32[2,128]{1,0:T(2,128)} %bitcast.50, bf16[2,128]{1,0:T(2,128)(2,1)} %bitcast.52, bf16[512,384]{1,0:T(8,128)(2,1)} %bitcast.16.rows, f32[128,384]{1,0:T(8,128)} %get-tuple-element.53.own, bf16[128,128]{1,0:T(8,128)(2,1)} %get-tuple-element.54.own_lanes, ...), custom_call_target="tpu_custom_call" | custom-call | flops 1 | bytes 1 | tf_op jit(solution)/shard_map/finish/pallas_call | solution.py:543
  (53 shorter events, 1.6 us)
Async XLA Ops:
  2.8 22.6 %all-to-all-start = ((bf16[16,64,384]{2,1,0:T(8,128)(2,1)}), bf16[16,64,384]{2,1,0:T(8,128)(2,1)S(1)}, u32[]{:S(2)}, u32[]{:S(2)}) async-start(bf16[16,64,384]{2,1,0:T(8,128)(2,1)} %dispatch.3), calls=%async_computation | async-start | bytes 1572864 | tf_op jit(solution)/shard_map/dispatch/all_to_all | solution.py:411
  11.1 7.0 %collective-permute-start.1 = (bf16[128,384]{1,0:T(8,128)(2,1)}, bf16[128,384]{1,0:T(8,128)(2,1)S(1)}, u32[]{:S(2)}, u32[]{:S(2)}) collective-permute-start(bf16[128,384]{1,0:T(8,128)(2,1)} %g0.1), channel_id=1, source_target_pairs={{0,4},{1,5},{2,6},{3,7},{4,0},{5,1},{6,2},{7,3},{8,12},{9,13},{10,... | collective-permute-start | bytes 294920 | tf_op jit(solution)/shard_map/dispatch/ppermute | solution.py:403
  14.3 5.0 %collective-permute-start = (bf16[128,384]{1,0:T(8,128)(2,1)}, bf16[128,384]{1,0:T(8,128)(2,1)S(1)}, u32[]{:S(2)}, u32[]{:S(2)}) collective-permute-start(bf16[128,384]{1,0:T(8,128)(2,1)} %g0.1), channel_id=1, source_target_pairs={{0,6},{1,7},{2,0},{3,1},{4,2},{5,3},{6,4},{7,5},{8,14},{9,15},{10,... | collective-permute-start | bytes 294920 | tf_op jit(solution)/shard_map/dispatch/ppermute | solution.py:403
  15.4 6.0 %collective-permute-start.2 = (bf16[128,384]{1,0:T(8,128)(2,1)}, bf16[128,384]{1,0:T(8,128)(2,1)S(1)}, u32[]{:S(2)}, u32[]{:S(2)}) collective-permute-start(bf16[128,384]{1,0:T(8,128)(2,1)} %g0.1), channel_id=1, source_target_pairs={{0,2},{1,3},{2,4},{3,5},{4,6},{5,7},{6,0},{7,1},{8,10},{9,11},{10,... | collective-permute-start | bytes 294920 | tf_op jit(solution)/shard_map/dispatch/ppermute | solution.py:403
  18.1 3.3 %copy-start.13 = (bf16[128,384]{1,0:T(8,128)(2,1)}, bf16[128,384]{1,0:T(8,128)(2,1)S(1)}, u32[]{:S(2)}) copy-start(bf16[128,384]{1,0:T(8,128)(2,1)S(1)} %collective-permute-done.1.g2) | copy-start | bytes 294916
  19.3 2.1 %copy-start.14 = (bf16[128,384]{1,0:T(8,128)(2,1)}, bf16[128,384]{1,0:T(8,128)(2,1)S(1)}, u32[]{:S(2)}) copy-start(bf16[128,384]{1,0:T(8,128)(2,1)S(1)} %collective-permute-done.g1) | copy-start | bytes 294916
  21.4 0.6 copy-start.15
  25.4 0.9 copy-start.1
  26.3 9.5 %copy-start = (bf16[1,3072,512]{2,1,0:T(8,128)(2,1)S(1)}, bf16[1,3072,512]{2,1,0:T(8,128)(2,1)}, u32[]{:S(2)}) copy-start(bf16[1,3072,512]{2,1,0:T(8,128)(2,1)} %param.11) | copy-start | bytes 9437188
  26.3 47.3 %all-to-all-start.1 = ((bf16[16,64,1536]{2,1,0:T(8,128)(2,1)}), bf16[16,64,1536]{2,1,0:T(8,128)(2,1)}, u32[]{:S(2)}, u32[]{:S(2)}) async-start(bf16[16,64,1536]{2,1,0:T(8,128)(2,1)} %dispatch.2), calls=%async_computation.1 | async-start | bytes 6291456 | tf_op jit(solution)/shard_map/gather/all_to_all | solution.py:411
  33.8 17.1 %collective-permute-start.7 = (bf16[1024,384]{1,0:T(8,128)(2,1)}, bf16[1024,384]{1,0:T(8,128)(2,1)}, u32[]{:S(2)}, u32[]{:S(2)}) collective-permute-start(bf16[1024,384]{1,0:T(8,128)(2,1)} %bitcast.37), channel_id=1, source_target_pairs={{0,6},{1,7},{2,0},{3,1},{4,2},{5,3},{6,4},{7,5},{8,14},{9,15},{10,... | collective-permute-start | bytes 2359304 | tf_op jit(solution)/shard_map/gather/ppermute | solution.py:403
  34.4 19.1 %collective-permute-start.5 = (bf16[1024,384]{1,0:T(8,128)(2,1)}, bf16[1024,384]{1,0:T(8,128)(2,1)}, u32[]{:S(2)}, u32[]{:S(2)}) collective-permute-start(bf16[1024,384]{1,0:T(8,128)(2,1)} %bitcast.38), channel_id=1, source_target_pairs={{0,2},{1,3},{2,4},{3,5},{4,6},{5,7},{6,0},{7,1},{8,10},{9,11},{10,... | collective-permute-start | bytes 2359304 | tf_op jit(solution)/shard_map/gather/ppermute | solution.py:403
  35.9 3.4 %copy-start.2 = (bf16[16,64,384]{2,1,0:T(8,128)(2,1)S(1)}, bf16[16,64,384]{2,1,0:T(8,128)(2,1)}, u32[]{:S(2)}) copy-start(bf16[16,64,384]{2,1,0:T(8,128)(2,1)} %copy-done.1) | copy-start | bytes 2359300
  39.3 16.0 %collective-permute-start.9 = (bf16[1024,384]{1,0:T(8,128)(2,1)S(1)}, bf16[1024,384]{1,0:T(8,128)(2,1)S(1)}, u32[]{:S(2)}, u32[]{:S(2)}) collective-permute-start(bf16[1024,384]{1,0:T(8,128)(2,1)S(1)} %bitcast.41), channel_id=1, source_target_pairs={{0,1},{1,0},{2,3},{3,2},{4,5},{5,4},{6,7},{7,6},{8,9},{9,8},{10,11... | collective-permute-start | bytes 2359304 | tf_op jit(solution)/shard_map/gather/ppermute | solution.py:408
  50.9 7.5 %collective-permute-start.10 = (bf16[1024,384]{1,0:T(8,128)(2,1)}, bf16[1024,384]{1,0:T(8,128)(2,1)S(1)}, u32[]{:S(2)}, u32[]{:S(2)}) collective-permute-start(bf16[1024,384]{1,0:T(8,128)(2,1)} %collective-permute-done.7.refs_1_), channel_id=1, source_target_pairs={{0,1},{1,0},{2,3},{3,2},{4,5},{5,4},{6,7},{7,6},{8,9},{9,8},{10,11... | collective-permute-start | bytes 2359304 | tf_op jit(solution)/shard_map/gather/ppermute | solution.py:408
  50.9 20.3 %collective-permute-start.3 = (bf16[4,384,512]{2,1,0:T(8,128)(2,1)}, bf16[4,384,512]{2,1,0:T(8,128)(2,1)}, u32[]{:S(2)}, u32[]{:S(2)}) collective-permute-start(bf16[4,384,512]{2,1,0:T(8,128)(2,1)} %get-tuple-element.34), channel_id=1, source_target_pairs={{0,1},{1,0},{2,3},{3,2},{4,5},{5,4},{6,7},{7,6},{8,9},{9,8},{10,11... | collective-permute-start | bytes 4718600 | tf_op jit(solution)/shard_map/gather/ppermute | solution.py:408
  51.4 19.8 %collective-permute-start.4 = (bf16[4,384,512]{2,1,0:T(8,128)(2,1)}, bf16[4,384,512]{2,1,0:T(8,128)(2,1)}, u32[]{:S(2)}, u32[]{:S(2)}) collective-permute-start(bf16[4,384,512]{2,1,0:T(8,128)(2,1)} %get-tuple-element.35), channel_id=1, source_target_pairs={{0,1},{1,0},{2,3},{3,2},{4,5},{5,4},{6,7},{7,6},{8,9},{9,8},{10,11... | collective-permute-start | bytes 4718600 | tf_op jit(solution)/shard_map/gather/ppermute | solution.py:408
  53.5 5.6 %collective-permute-start.11 = (bf16[1024,384]{1,0:T(8,128)(2,1)}, bf16[1024,384]{1,0:T(8,128)(2,1)}, u32[]{:S(2)}, u32[]{:S(2)}) collective-permute-start(bf16[1024,384]{1,0:T(8,128)(2,1)} %collective-permute-done.5.refs_2_), channel_id=1, source_target_pairs={{0,1},{1,0},{2,3},{3,2},{4,5},{5,4},{6,7},{7,6},{8,9},{9,8},{10,11... | collective-permute-start | bytes 2359304 | tf_op jit(solution)/shard_map/gather/ppermute | solution.py:408
  55.3 3.8 %copy-start.4 = (bf16[1024,384]{1,0:T(8,128)(2,1)}, bf16[1024,384]{1,0:T(8,128)(2,1)S(1)}, u32[]{:S(2)}) copy-start(bf16[1024,384]{1,0:T(8,128)(2,1)S(1)} %collective-permute-done.9.refs_3_) | copy-start | bytes 2359300
  55.3 13.5 %collective-permute-start.8 = (bf16[512,384]{1,0:T(8,128)(2,1)}, bf16[512,384]{1,0:T(8,128)(2,1)S(1)}, u32[]{:S(2)}, u32[]{:S(2)}) collective-permute-start(bf16[512,384]{1,0:T(8,128)(2,1)} %slice.9), channel_id=1, source_target_pairs={{0,6},{1,7},{2,0},{3,1},{4,2},{5,3},{6,4},{7,5},{8,14},{9,15},{10,... | collective-permute-start | bytes 1179656 | tf_op jit(solution)/shard_map/gather/ppermute | solution.py:403
  58.4 0.9 copy-start.5
  58.4 12.3 %collective-permute-start.6 = (bf16[512,384]{1,0:T(8,128)(2,1)}, bf16[512,384]{1,0:T(8,128)(2,1)}, u32[]{:S(2)}, u32[]{:S(2)}) collective-permute-start(bf16[512,384]{1,0:T(8,128)(2,1)} %slice.8), channel_id=1, source_target_pairs={{0,2},{1,3},{2,4},{3,5},{4,6},{5,7},{6,0},{7,1},{8,10},{9,11},{10,... | collective-permute-start | bytes 1179656 | tf_op jit(solution)/shard_map/gather/ppermute | solution.py:403
  68.8 4.8 %copy-start.6 = (bf16[512,384]{1,0:T(8,128)(2,1)}, bf16[512,384]{1,0:T(8,128)(2,1)S(1)}, u32[]{:S(2)}) copy-start(bf16[512,384]{1,0:T(8,128)(2,1)S(1)} %collective-permute-done.8.refs_1_.refs_7_) | copy-start | bytes 1179652
  70.7 2.5 %collective-permute-start.12 = (bf16[512,384]{1,0:T(8,128)(2,1)}, bf16[512,384]{1,0:T(8,128)(2,1)S(1)}, u32[]{:S(2)}, u32[]{:S(2)}) collective-permute-start(bf16[512,384]{1,0:T(8,128)(2,1)} %collective-permute-done.6.refs_0_.refs_6_), channel_id=1, source_target_pairs={{0,1},{1,0},{2,3},{3,2},{4,5},{5,4},{6,7},{7,6},{8,9},{9,8},{10,11... | collective-permute-start | bytes 1179656 | tf_op jit(solution)/shard_map/forward/ppermute | solution.py:408
  70.7 2.5 %collective-permute-start.13 = (bf16[512,384]{1,0:T(8,128)(2,1)S(1)}, bf16[512,384]{1,0:T(8,128)(2,1)S(1)}, u32[]{:S(2)}, u32[]{:S(2)}) collective-permute-start(bf16[512,384]{1,0:T(8,128)(2,1)S(1)} %collective-permute-done.8.refs_1_.refs_7_), channel_id=1, source_target_pairs={{0,1},{1,0},{2,3},{3,2},{4,5},{5,4},{6,7},{7,6},{8,9},{9,8},{10,11... | collective-permute-start | bytes 1179656 | tf_op jit(solution)/shard_map/forward/ppermute | solution.py:408
  73.1 0.7 copy-start.7
  73.1 0.9 copy-start.8
  73.7 6.1 %collective-permute-start.14 = (bf16[1024,1536]{1,0:T(8,128)(2,1)}, bf16[1024,1536]{1,0:T(8,128)(2,1)}, u32[]{:S(2)}, u32[]{:S(2)}) collective-permute-start(bf16[1024,1536]{1,0:T(8,128)(2,1)} %bitcast.4.own), channel_id=1, source_target_pairs={{0,1},{1,0},{2,3},{3,2},{4,5},{5,4},{6,7},{7,6},{8,9},{9,8},{10,11... | collective-permute-start | bytes 9437192 | tf_op jit(solution)/shard_map/forward/ppermute | solution.py:408
  88.1 7.7 %collective-permute-start.15 = (bf16[1024,1024]{1,0:T(8,128)(2,1)}, bf16[1024,1024]{1,0:T(8,128)(2,1)}, u32[]{:S(2)}, u32[]{:S(2)}) collective-permute-start(bf16[1024,1024]{1,0:T(8,128)(2,1)} %get-tuple-element.45.grads), channel_id=1, source_target_pairs={{0,1},{1,0},{2,3},{3,2},{4,5},{5,4},{6,7},{7,6},{8,9},{9,8},{10,11... | collective-permute-start | bytes 6291464 | tf_op jit(solution)/shard_map/backward/ppermute | solution.py:408
  88.3 7.4 %collective-permute-start.16 = (bf16[1024,128]{1,0:T(8,128)(2,1)}, bf16[1024,128]{1,0:T(8,128)(2,1)S(1)}, u32[]{:S(2)}, u32[]{:S(2)}) collective-permute-start(bf16[1024,128]{1,0:T(8,128)(2,1)} %get-tuple-element.43), channel_id=1, source_target_pairs={{0,1},{1,0},{2,3},{3,2},{4,5},{5,4},{6,7},{7,6},{8,9},{9,8},{10,11... | collective-permute-start | bytes 786440 | tf_op jit(solution)/shard_map/backward/ppermute | solution.py:408
  95.7 0.7 copy-start.9
  104.1 35.7 %all-to-all-start.3 = ((bf16[16,32,1664]{2,1,0:T(8,128)(2,1)}), bf16[16,32,1664]{2,1,0:T(8,128)(2,1)S(1)}, u32[]{:S(2)}, u32[]{:S(2)}) async-start(bf16[16,32,1664]{2,1,0:T(8,128)(2,1)} %get-tuple-element.52), calls=%async_computation.3 | async-start | bytes 3407872 | tf_op jit(solution)/shard_map/sums/all_to_all | solution.py:411
  114.3 23.1 %collective-permute-start.17 = (bf16[16,32,384]{2,1,0:T(8,128)(2,1)}, bf16[16,32,384]{2,1,0:T(8,128)(2,1)}, u32[]{:S(2)}, u32[]{:S(2)}) collective-permute-start(bf16[16,32,384]{2,1,0:T(8,128)(2,1)} %get-tuple-element.49), channel_id=1, source_target_pairs={{0,2},{1,3},{2,4},{3,5},{4,6},{5,7},{6,0},{7,1},{8,10},{9,11},{10,... | collective-permute-start | bytes 1179656 | tf_op jit(solution)/shard_map/sums/ppermute | solution.py:403
  115.2 22.3 %collective-permute-start.18 = (bf16[16,32,384]{2,1,0:T(8,128)(2,1)}, bf16[16,32,384]{2,1,0:T(8,128)(2,1)}, u32[]{:S(2)}, u32[]{:S(2)}) collective-permute-start(bf16[16,32,384]{2,1,0:T(8,128)(2,1)} %get-tuple-element.50), channel_id=1, source_target_pairs={{0,4},{1,5},{2,6},{3,7},{4,0},{5,1},{6,2},{7,3},{8,12},{9,13},{10,... | collective-permute-start | bytes 1179656 | tf_op jit(solution)/shard_map/sums/ppermute | solution.py:403
  117.7 19.8 %collective-permute-start.19 = (bf16[16,32,384]{2,1,0:T(8,128)(2,1)}, bf16[16,32,384]{2,1,0:T(8,128)(2,1)}, u32[]{:S(2)}, u32[]{:S(2)}) collective-permute-start(bf16[16,32,384]{2,1,0:T(8,128)(2,1)} %get-tuple-element.51), channel_id=1, source_target_pairs={{0,6},{1,7},{2,0},{3,1},{4,2},{5,3},{6,4},{7,5},{8,14},{9,15},{10,... | collective-permute-start | bytes 1179656 | tf_op jit(solution)/shard_map/sums/ppermute | solution.py:403
  139.8 7.2 %copy-start.3 = (bf16[16,32,1664]{2,1,0:T(8,128)(2,1)}, bf16[16,32,1664]{2,1,0:T(8,128)(2,1)S(1)}, u32[]{:S(2)}) copy-start(bf16[16,32,1664]{2,1,0:T(8,128)(2,1)S(1)} %all-to-all-done.3) | copy-start | bytes 5111812
  139.8 15.4 %all-to-all-start.2 = ((bf16[16,32,384]{2,1,0:T(8,128)(2,1)}), bf16[16,32,384]{2,1,0:T(8,128)(2,1)}, u32[]{:S(2)}, u32[]{:S(2)}) async-start(bf16[16,32,384]{2,1,0:T(8,128)(2,1)} %add_convert_fusion), calls=%async_computation.2 | async-start | bytes 786432 | tf_op jit(solution)/shard_map/late_sum/all_to_all | solution.py:411
  150.1 8.4 %collective-permute-start.20 = (bf16[128,512]{1,0:T(8,128)(2,1)}, bf16[128,512]{1,0:T(8,128)(2,1)S(1)}, u32[]{:S(2)}, u32[]{:S(2)}) collective-permute-start(bf16[128,512]{1,0:T(8,128)(2,1)} %get-tuple-element.55), channel_id=1, source_target_pairs={{0,2},{1,3},{2,4},{3,5},{4,6},{5,7},{6,0},{7,1},{8,10},{9,11},{10,... | collective-permute-start | bytes 393224 | tf_op jit(solution)/shard_map/finish/ppermute | solution.py:403
  150.8 7.7 %collective-permute-start.21 = (bf16[128,512]{1,0:T(8,128)(2,1)}, bf16[128,512]{1,0:T(8,128)(2,1)S(1)}, u32[]{:S(2)}, u32[]{:S(2)}) collective-permute-start(bf16[128,512]{1,0:T(8,128)(2,1)} %get-tuple-element.56), channel_id=1, source_target_pairs={{0,4},{1,5},{2,6},{3,7},{4,0},{5,1},{6,2},{7,3},{8,12},{9,13},{10,... | collective-permute-start | bytes 393224 | tf_op jit(solution)/shard_map/finish/ppermute | solution.py:403
  152.5 6.2 %collective-permute-start.22 = (bf16[128,512]{1,0:T(8,128)(2,1)}, bf16[128,512]{1,0:T(8,128)(2,1)S(1)}, u32[]{:S(2)}, u32[]{:S(2)}) collective-permute-start(bf16[128,512]{1,0:T(8,128)(2,1)} %get-tuple-element.57), channel_id=1, source_target_pairs={{0,6},{1,7},{2,0},{3,1},{4,2},{5,3},{6,4},{7,5},{8,14},{9,15},{10,... | collective-permute-start | bytes 393224 | tf_op jit(solution)/shard_map/finish/ppermute | solution.py:403
  158.5 0.7 copy-start.10
  158.5 0.7 copy-start.11
  158.7 0.6 copy-start.12

commit v4 on v3

--- a/solution.py
+++ b/solution.py
@@ -8,6 +8,7 @@
 BF = jnp.bfloat16
 F32 = jnp.float32
 VMEM_LIMIT = 62 * 1024 * 1024
+SMALL_LIMIT = 16 * 1024 * 1024
 EXPERTS = 8
 CAP = 64
 EARLY = 32
@@ -23,14 +24,12 @@
     return lax.dot_general(a, b, dims, preferred_element_type=F32)
 
 
-def call(body, outs, grid=None, scratch=(), flops=0, nbytes=0, **specs):
-    params = dict(vmem_limit_bytes=VMEM_LIMIT)
+def call(body, outs, limit, flops=0, nbytes=0):
     return pl.pallas_call(
         body,
         out_shape=outs,
-        compiler_params=pltpu.CompilerParams(**params),
+        compiler_params=pltpu.CompilerParams(vmem_limit_bytes=limit),
         cost_estimate=pl.CostEstimate(flops=flops, bytes_accessed=nbytes, transcendentals=0),
-        **specs,
     )
 
 
@@ -418,9 +417,9 @@
     wide = 4 * COLS
     with jax.named_scope("dispatch"):
         gs = [d_out] + [from_y(d_out, dy) for dy in (1, 2, 3)]
-        send_x = call(dispatch_x_body, sds((16, CAP, COLS)), flops=10**8, nbytes=MB)(routes_t, tokens)
+        send_x = call(dispatch_x_body, sds((16, CAP, COLS)), VMEM_LIMIT, flops=10**8, nbytes=MB)(routes_t, tokens)
         x0 = exchange(send_x)
-        send_g = call(dispatch_g_body, sds((16, CAP, wide)), flops=2 * 10**8, nbytes=4 * MB)(
+        send_g = call(dispatch_g_body, sds((16, CAP, wide)), VMEM_LIMIT, flops=2 * 10**8, nbytes=4 * MB)(
             routes_t, probs_t, *gs
         )
     with jax.named_scope("gather"):
@@ -537,11 +536,12 @@
         own, own_lanes, m1, m2, m3 = call(
             combine_body,
             [sds((TOK, COLS), F32), sds((TOK, 128))] + [sds((TOK, COLS + 128))] * 3,
+            SMALL_LIMIT,
             flops=1,
             nbytes=1,
         )(routes_t, early_rows)
         d_tokens, d_probs = call(
-            finish_body, [sds((TOK, COLS)), sds((2, TOK), F32)], flops=1, nbytes=1
+            finish_body, [sds((TOK, COLS)), sds((2, TOK), F32)], SMALL_LIMIT, flops=1, nbytes=1
         )(
             routes_t,
             probs_t,

time: 162 us -> 158 us (0.975)
  Pallas kernels: 67.7 us -> 64.1 us
    ppermute x13, waiting for transfers between devices: 24.2 us -> 21.9 us  [from_y(): lax.ppermute(x, 'tensor', [(i, (i // 2 - dy) % 4 * 2 + i % 2) for i in ra...]
    pallas_call x1, Pallas kernels: 3.07 us -> 0.84 us  [on_device(): call(combine_body, [sds((TOK, COLS), F32), sds((TOK, 128))] + [sds((TOK,...]
    all_to_all x4, waiting for transfers between devices: 1.44 us -> 3.48 us  [exchange(): lax.all_to_all(x, ('dp', 'ctx'), split_axis=0, concat_axis=0, tiled=True)]
    unnamed x32 -> x28, local copies, waits for them, and re-layouts: 3.35 us -> 2.73 us
where the time goes in v4:
time: 158 us; the launch traced here: 157 us
  Pallas kernels  64.1 us (41%)
  starting transfers between devices  53.1 us (34%)
  waiting for transfers between devices  27.4 us (17%)
  local copies, waits for them, and re-layouts  9.75 us (6%)
  other arithmetic  2.3 us (1%)
    pallas_call x7, Pallas kernels, plain_call(): pl.pallas_call(body, out_shape=outs, in_specs=[pl.BlockSpec(memory_space=...  56.7 us
    all_to_all x4, starting transfers between devices, exchange(): lax.all_to_all(x, ('dp', 'ctx'), split_axis=0, concat_axis=0, tiled=True)  33.3 us
    ppermute x13, waiting for transfers between devices, from_y(): lax.ppermute(x, 'tensor', [(i, (i // 2 - dy) % 4 * 2 + i % 2) for i in ra...  21.9 us
    ppermute x13, starting transfers between devices, from_y(): lax.ppermute(x, 'tensor', [(i, (i // 2 - dy) % 4 * 2 + i % 2) for i in ra...  18.1 us
    slice x2, local copies, waits for them, and re-layouts, on_device(): far_xs = [from_y(down1[:HALF], 3), from_y(up1[HALF:], 1)]  3.59 us
    all_to_all x4, waiting for transfers between devices, exchange(): lax.all_to_all(x, ('dp', 'ctx'), split_axis=0, concat_axis=0, tiled=True)  3.48 us
    squeeze x1, local copies, waits for them, and re-layouts, sibling_rows(): lax.dynamic_index_in_dim(w.reshape(4, 2, COLS, HID), 1 - core, 1, False)  3.43 us
    pallas_call x1, Pallas kernels, on_device(): call(dispatch_g_body, sds((16, CAP, wide)), VMEM_LIMIT, flops=2 * 10 ** 8...  3.41 us
  transfers between devices with their start and end apart: 27, of which 11 were waited for; matrix products, arithmetic and copies ran while one was open for 6% of the time, Pallas kernels for 29%

profile of v4, /device:TPU:2, one launch (start us, length us, event | category | flops | bytes accessed | tf_op | source)
XLA Modules:
  0.0 157.4 jit_solution(11167239997598117687)
XLA Ops:
  0.6 2.2 %dispatch.3 = bf16[16,64,384]{2,1,0:T(8,128)(2,1)} custom-call(s32[2,128]{1,0:T(2,128)} %bitcast.30, bf16[128,384]{1,0:T(8,128)(2,1)} %tokens.1), custom_call_target="tpu_custom_call" | custom-call | flops 100000000 | bytes 1048576 | tf_op jit(solution)/shard_map/dispatch/pallas_call | solution.py:420
  2.8 8.3 %all-to-all-start = ((bf16[16,64,384]{2,1,0:T(8,128)(2,1)}), bf16[16,64,384]{2,1,0:T(8,128)(2,1)S(1)}, u32[]{:S(2)}, u32[]{:S(2)}) async-start(bf16[16,64,384]{2,1,0:T(8,128)(2,1)} %dispatch.3), calls=%async_computation | async-start | bytes 1572864 | tf_op jit(solution)/shard_map/dispatch/all_to_all | solution.py:410
  11.1 3.2 %collective-permute-start.1 = (bf16[128,384]{1,0:T(8,128)(2,1)}, bf16[128,384]{1,0:T(8,128)(2,1)S(1)}, u32[]{:S(2)}, u32[]{:S(2)}) collective-permute-start(bf16[128,384]{1,0:T(8,128)(2,1)} %g0.1), channel_id=1, source_target_pairs={{0,4},{1,5},{2,6},{3,7},{4,0},{5,1},{6,2},{7,3},{8,12},{9,13},{10,... | collective-permute-start | bytes 294920 | tf_op jit(solution)/shard_map/dispatch/ppermute | solution.py:402
  14.3 1.1 collective-permute-start
  15.4 1.0 collective-permute-start.2
  16.3 1.8 %collective-permute-done.1.g2 = bf16[128,384]{1,0:T(8,128)(2,1)S(1)} collective-permute-done((bf16[128,384]{1,0:T(8,128)(2,1)}, bf16[128,384]{1,0:T(8,128)(2,1)S(1)}, u32[]{:S(2)}, u32[]{:S(2)}) %collective-permute-start.1) | collective-permute-done | bytes 98336 | tf_op jit(solution)/shard_map/dispatch/ppermute | solution.py:402
  18.1 1.2 collective-permute-done.g1
  19.3 2.1 %collective-permute-done.2.g3 = bf16[128,384]{1,0:T(8,128)(2,1)S(1)} collective-permute-done((bf16[128,384]{1,0:T(8,128)(2,1)}, bf16[128,384]{1,0:T(8,128)(2,1)S(1)}, u32[]{:S(2)}, u32[]{:S(2)}) %collective-permute-start.2) | collective-permute-done | bytes 98336 | tf_op jit(solution)/shard_map/dispatch/ppermute | solution.py:402
  21.4 0.6 copy-done.13
  22.0 3.4 %dispatch.2 = bf16[16,64,1536]{2,1,0:T(8,128)(2,1)} custom-call(s32[2,128]{1,0:T(2,128)} %bitcast.31, bf16[2,128]{1,0:T(2,128)(2,1)} %bitcast.34, bf16[128,384]{1,0:T(8,128)(2,1)} %g0.1, bf16[128,384]{1,0:T(8,128)(2,1)} %copy-done.12, bf16[128,384]{1,0:T(8,128)(2,1)} %copy-done.11, bf16[128,384]{1,0:T(8,128)(2,1)} %copy-done.13), custom_call_target="tpu_custom_call" | custom-call | flops 200000000 | bytes 4194304 | tf_op jit(solution)/shard_map/dispatch/pallas_call | solution.py:422
  25.4 0.9 copy-done.3
  26.3 7.5 %all-to-all-start.1 = ((bf16[16,64,1536]{2,1,0:T(8,128)(2,1)}), bf16[16,64,1536]{2,1,0:T(8,128)(2,1)}, u32[]{:S(2)}, u32[]{:S(2)}) async-start(bf16[16,64,1536]{2,1,0:T(8,128)(2,1)} %dispatch.2), calls=%async_computation.1 | async-start | bytes 6291456 | tf_op jit(solution)/shard_map/gather/all_to_all | solution.py:410
  33.8 0.6 collective-permute-start.7
  34.4 1.5 collective-permute-start.5
  35.9 3.4 %dynamic-slice_bitcast_fusion = (bf16[4,384,512]{2,1,0:T(8,128)(2,1)}, bf16[4,384,512]{2,1,0:T(8,128)(2,1)}) fusion(bf16[4,2,384,512]{3,2,1,0:T(8,128)(2,1)} %bitcast.40, s32[]{:T(128)S(6)} %select_n.13, bf16[4,2,384,512]{3,2,1,0:T(8,128)(2,1)S(1)} %bitcast.39), kind=kLoop, calls=%fused_computation | loop fusion | bytes 6291460 | tf_op jit(solution)/shard_map/gather/jit(dynamic_index_in_dim)/squeeze | solution.py:434
  39.3 11.6 %collective-permute-done.7.refs_1_ = bf16[1024,384]{1,0:T(8,128)(2,1)} collective-permute-done((bf16[1024,384]{1,0:T(8,128)(2,1)}, bf16[1024,384]{1,0:T(8,128)(2,1)}, u32[]{:S(2)}, u32[]{:S(2)}) %collective-permute-start.7) | collective-permute-done | bytes 786464 | tf_op jit(solution)/shard_map/gather/ppermute | solution.py:402
  50.9 0.5 collective-permute-start.3
  51.4 2.1 %collective-permute-done.5.refs_2_ = bf16[1024,384]{1,0:T(8,128)(2,1)} collective-permute-done((bf16[1024,384]{1,0:T(8,128)(2,1)}, bf16[1024,384]{1,0:T(8,128)(2,1)}, u32[]{:S(2)}, u32[]{:S(2)}) %collective-permute-start.5) | collective-permute-done | bytes 786464 | tf_op jit(solution)/shard_map/gather/ppermute | solution.py:402
  53.5 1.8 %slice.9 = bf16[512,384]{1,0:T(8,128)(2,1)} slice(bf16[1024,384]{1,0:T(8,128)(2,1)} %collective-permute-done.7.refs_1_), slice={[512:1024], [0:384]} | slice | bytes 786432 | tf_op jit(solution)/shard_map/gather/slice | solution.py:429
  55.3 1.3 collective-permute-start.8
  56.6 1.8 %slice.8 = bf16[512,384]{1,0:T(8,128)(2,1)} slice(bf16[1024,384]{1,0:T(8,128)(2,1)} %collective-permute-done.5.refs_2_), slice={[0:512], [0:384]} | slice | bytes 786432 | tf_op jit(solution)/shard_map/gather/slice | solution.py:429
  58.4 0.7 collective-permute-start.6
  59.3 9.5 %forward.2.refs_4_ = f32[1024,1024]{1,0:T(8,128)} custom-call(s32[1]{0:T(128)} %bitcast.2.t, bf16[1024,384]{1,0:T(8,128)(2,1)} %bitcast.47, bf16[1024,384]{1,0:T(8,128)(2,1)} %collective-permute-done.7.refs_1_, bf16[1024,384]{1,0:T(8,128)(2,1)} %collective-permute-done.5.refs_2_, bf16[1024,384]{1,0:T(8,128)(2,1)} %copy-done.5, bf16[1024,384]{1,0:T(8,128)(2,1)} %copy-done.6, ...), custom_call_target="tpu_custom_call" | custom-call | flops 1 | bytes 1 | tf_op jit(solution)/shard_map/forward/pallas_call | solution.py:87
  68.8 1.8 %collective-permute-done.6.refs_0_.refs_6_ = bf16[512,384]{1,0:T(8,128)(2,1)} collective-permute-done((bf16[512,384]{1,0:T(8,128)(2,1)}, bf16[512,384]{1,0:T(8,128)(2,1)}, u32[]{:S(2)}, u32[]{:S(2)}) %collective-permute-start.6) | collective-permute-done | bytes 393248 | tf_op jit(solution)/shard_map/gather/ppermute | solution.py:402
  70.7 0.5 collective-permute-start.13
  71.2 1.9 %collective-permute-done.12.refs_2_.refs_8_ = bf16[512,384]{1,0:T(8,128)(2,1)S(1)} collective-permute-done((bf16[512,384]{1,0:T(8,128)(2,1)}, bf16[512,384]{1,0:T(8,128)(2,1)S(1)}, u32[]{:S(2)}, u32[]{:S(2)}) %collective-permute-start.12) | collective-permute-done | bytes 393248 | tf_op jit(solution)/shard_map/forward/ppermute | solution.py:407
  73.2 0.5 all-to-all-done.1
  74.0 5.8 %forward.3 = (f32[1024,512]{1,0:T(8,128)}, f32[1024,512]{1,0:T(8,128)}, bf16[1024,512]{1,0:T(8,128)(2,1)}) custom-call(s32[1]{0:T(128)} %bitcast.2.t, bf16[512,384]{1,0:T(8,128)(2,1)} %collective-permute-done.6.refs_0_.refs_6_, bf16[512,384]{1,0:T(8,128)(2,1)} %copy-done.7, bf16[512,384]{1,0:T(8,128)(2,1)} %copy-done.8, bf16[512,384]{1,0:T(8,128)(2,1)} %copy-done.9, ...), custom_call_target="tpu_custom_call" | custom-call | flops 1 | bytes 1 | tf_op jit(solution)/shard_map/forward/pallas_call | solution.py:87
  79.8 8.3 %backward.1 = (bf16[1024,1024]{1,0:T(8,128)(2,1)}, bf16[1024,128]{1,0:T(8,128)(2,1)}) custom-call(s32[1]{0:T(128)} %bitcast.2.t, bf16[1024,1536]{1,0:T(8,128)(2,1)} %bitcast.4.own, bf16[1024,1536]{1,0:T(8,128)(2,1)} %collective-permute-done.14.sib, f32[1024,512]{1,0:T(8,128)} %get-tuple-element.39.act, f32[1024,512]{1,0:T(8,128)} %get-tuple-element.40.slope, ...), custom_call_target="tpu_custom_call" | custom-call | flops 1 | bytes 1 | tf_op jit(solution)/shard_map/backward/pallas_call | solution.py:87
  88.3 0.3 collective-permute-start.16
  88.7 7.1 %sums.2 = bf16[1024,1536]{1,0:T(8,128)(2,1)} custom-call(s32[1]{0:T(128)} %bitcast.2.t, bf16[1024,1024]{1,0:T(8,128)(2,1)} %get-tuple-element.45.grads, bf16[3072,512]{1,0:T(8,128)(2,1)} %bitcast.38, bf16[3072,512]{1,0:T(8,128)(2,1)} %bitcast.43), custom_call_target="tpu_custom_call" | custom-call | flops 1 | bytes 1 | tf_op jit(solution)/shard_map/sums/pallas_call | solution.py:87
  95.8 0.7 copy-done.10
  96.5 7.6 %sums.3 = (bf16[16,32,1664]{2,1,0:T(8,128)(2,1)}, bf16[16,32,384]{2,1,0:T(8,128)(2,1)}, bf16[16,32,384]{2,1,0:T(8,128)(2,1)}, bf16[16,32,384]{2,1,0:T(8,128)(2,1)}, bf16[16,32,384]{2,1,0:T(8,128)(2,1)}) custom-call(s32[1]{0:T(128)} %bitcast.2.t, bf16[16,64,1536]{2,1,0:T(8,128)(2,1)} %bitcast.44, bf16[16,64,1024]{2,1,0:T(8,128)(2,1)} %bitcast.13.grads_sib, ...), custom_call_target="tpu_custom_call" | custom-call | flops 1 | bytes 1 | tf_op jit(solution)/shard_map/sums/pallas_call | solution.py:87
  104.1 10.3 %all-to-all-start.3 = ((bf16[16,32,1664]{2,1,0:T(8,128)(2,1)}), bf16[16,32,1664]{2,1,0:T(8,128)(2,1)S(1)}, u32[]{:S(2)}, u32[]{:S(2)}) async-start(bf16[16,32,1664]{2,1,0:T(8,128)(2,1)} %get-tuple-element.52), calls=%async_computation.3 | async-start | bytes 3407872 | tf_op jit(solution)/shard_map/sums/all_to_all | solution.py:410
  114.3 0.8 collective-permute-start.17
  115.2 2.5 %collective-permute-start.18 = (bf16[16,32,384]{2,1,0:T(8,128)(2,1)}, bf16[16,32,384]{2,1,0:T(8,128)(2,1)}, u32[]{:S(2)}, u32[]{:S(2)}) collective-permute-start(bf16[16,32,384]{2,1,0:T(8,128)(2,1)} %get-tuple-element.50), channel_id=1, source_target_pairs={{0,4},{1,5},{2,6},{3,7},{4,0},{5,1},{6,2},{7,3},{8,12},{9,13},{10,... | collective-permute-start | bytes 1179656 | tf_op jit(solution)/shard_map/sums/ppermute | solution.py:402
  117.7 1.3 collective-permute-start.19
  119.0 10.9 %weights_gate_up.1 = (bf16[3072,512]{1,0:T(8,128)(2,1)}, bf16[3072,512]{1,0:T(8,128)(2,1)}) custom-call(s32[1]{0:T(128)} %bitcast.2.t, bf16[1024,1024]{1,0:T(8,128)(2,1)} %get-tuple-element.45.grads, bf16[1024,384]{1,0:T(8,128)(2,1)} %bitcast.48, bf16[1024,384]{1,0:T(8,128)(2,1)} %collective-permute-done.7.refs_1_, ...), custom_call_target="tpu_custom_call" | custom-call | flops 1 | bytes 1 | tf_op jit(solution)/shard_map/weights_gate_up/pallas_call | solution.py:87
  129.9 7.5 %weights_down.1 = bf16[512,3072]{1,0:T(8,128)(2,1)} custom-call(s32[1]{0:T(128)} %bitcast.2.t, bf16[1024,512]{1,0:T(8,128)(2,1)} %get-tuple-element.47.hidden, bf16[1024,1536]{1,0:T(8,128)(2,1)} %bitcast.4.own, bf16[1024,1536]{1,0:T(8,128)(2,1)} %collective-permute-done.14.sib), custom_call_target="tpu_custom_call" | custom-call | flops 1 | bytes 1 | tf_op jit(solution)/shard_map/weights_down/pallas_call | solution.py:87
  137.5 2.3 %add_convert_fusion = bf16[16,32,384]{2,1,0:T(8,128)(2,1)} fusion(bf16[16,32,384]{2,1,0:T(8,128)(2,1)} %collective-permute-done.19, bf16[16,32,384]{2,1,0:T(8,128)(2,1)} %collective-permute-done.18, bf16[16,32,384]{2,1,0:T(8,128)(2,1)} %collective-permute-done.17, bf16[16,32,384]{2,1,0:T(8,128)(2,1)} %get-tuple-element.48), kind=kLoop, calls=%fused_computation.2 | loop fusion | flops 1572864 | bytes 1966080 | tf_op jit(solution)/shard_map/late_sum/convert_element_type | solution.py:533
  139.8 7.2 %all-to-all-start.2 = ((bf16[16,32,384]{2,1,0:T(8,128)(2,1)}), bf16[16,32,384]{2,1,0:T(8,128)(2,1)S(1)}, u32[]{:S(2)}, u32[]{:S(2)}) async-start(bf16[16,32,384]{2,1,0:T(8,128)(2,1)} %add_convert_fusion), calls=%async_computation.2 | async-start | bytes 786432 | tf_op jit(solution)/shard_map/late_sum/all_to_all | solution.py:410
  147.0 0.8 finish.2
  147.9 0.8 collective-permute-start.20
  148.7 1.6 %collective-permute-start.21 = (bf16[128,512]{1,0:T(8,128)(2,1)S(1)}, bf16[128,512]{1,0:T(8,128)(2,1)S(1)}, u32[]{:S(2)}, u32[]{:S(2)}) collective-permute-start(bf16[128,512]{1,0:T(8,128)(2,1)S(1)} %get-tuple-element.56), channel_id=1, source_target_pairs={{0,4},{1,5},{2,6},{3,7},{4,0},{5,1},{6,2},{7,3},{8,12},{9,13},{10,... | collective-permute-start | bytes 393224 | tf_op jit(solution)/shard_map/finish/ppermute | solution.py:402
  150.3 1.8 %collective-permute-start.22 = (bf16[128,512]{1,0:T(8,128)(2,1)S(1)}, bf16[128,512]{1,0:T(8,128)(2,1)S(1)}, u32[]{:S(2)}, u32[]{:S(2)}) collective-permute-start(bf16[128,512]{1,0:T(8,128)(2,1)S(1)} %get-tuple-element.57), channel_id=1, source_target_pairs={{0,6},{1,7},{2,0},{3,1},{4,2},{5,3},{6,4},{7,5},{8,14},{9,15},{10,... | collective-permute-start | bytes 393224 | tf_op jit(solution)/shard_map/finish/ppermute | solution.py:402
  152.1 2.9 %all-to-all-done.2 = bf16[16,32,384]{2,1,0:T(8,128)(2,1)S(1)} async-done(((bf16[16,32,384]{2,1,0:T(8,128)(2,1)}), bf16[16,32,384]{2,1,0:T(8,128)(2,1)S(1)}, u32[]{:S(2)}, u32[]{:S(2)}) %all-to-all-start.2) | async-done | bytes 393248 | tf_op jit(solution)/shard_map/late_sum/all_to_all | solution.py:410
  155.0 1.1 collective-permute-done.20.m1
  156.4 1.1 finish.3
  (49 shorter events, 1.1 us)
Async XLA Ops:
  2.8 22.6 %all-to-all-start = ((bf16[16,64,384]{2,1,0:T(8,128)(2,1)}), bf16[16,64,384]{2,1,0:T(8,128)(2,1)S(1)}, u32[]{:S(2)}, u32[]{:S(2)}) async-start(bf16[16,64,384]{2,1,0:T(8,128)(2,1)} %dispatch.3), calls=%async_computation | async-start | bytes 1572864 | tf_op jit(solution)/shard_map/dispatch/all_to_all | solution.py:410
  11.1 7.0 %collective-permute-start.1 = (bf16[128,384]{1,0:T(8,128)(2,1)}, bf16[128,384]{1,0:T(8,128)(2,1)S(1)}, u32[]{:S(2)}, u32[]{:S(2)}) collective-permute-start(bf16[128,384]{1,0:T(8,128)(2,1)} %g0.1), channel_id=1, source_target_pairs={{0,4},{1,5},{2,6},{3,7},{4,0},{5,1},{6,2},{7,3},{8,12},{9,13},{10,... | collective-permute-start | bytes 294920 | tf_op jit(solution)/shard_map/dispatch/ppermute | solution.py:402
  14.3 5.0 %collective-permute-start = (bf16[128,384]{1,0:T(8,128)(2,1)}, bf16[128,384]{1,0:T(8,128)(2,1)S(1)}, u32[]{:S(2)}, u32[]{:S(2)}) collective-permute-start(bf16[128,384]{1,0:T(8,128)(2,1)} %g0.1), channel_id=1, source_target_pairs={{0,6},{1,7},{2,0},{3,1},{4,2},{5,3},{6,4},{7,5},{8,14},{9,15},{10,... | collective-permute-start | bytes 294920 | tf_op jit(solution)/shard_map/dispatch/ppermute | solution.py:402
  15.4 6.0 %collective-permute-start.2 = (bf16[128,384]{1,0:T(8,128)(2,1)}, bf16[128,384]{1,0:T(8,128)(2,1)S(1)}, u32[]{:S(2)}, u32[]{:S(2)}) collective-permute-start(bf16[128,384]{1,0:T(8,128)(2,1)} %g0.1), channel_id=1, source_target_pairs={{0,2},{1,3},{2,4},{3,5},{4,6},{5,7},{6,0},{7,1},{8,10},{9,11},{10,... | collective-permute-start | bytes 294920 | tf_op jit(solution)/shard_map/dispatch/ppermute | solution.py:402
  18.1 3.3 %copy-start.11 = (bf16[128,384]{1,0:T(8,128)(2,1)}, bf16[128,384]{1,0:T(8,128)(2,1)S(1)}, u32[]{:S(2)}) copy-start(bf16[128,384]{1,0:T(8,128)(2,1)S(1)} %collective-permute-done.1.g2) | copy-start | bytes 294916
  19.3 2.1 %copy-start.12 = (bf16[128,384]{1,0:T(8,128)(2,1)}, bf16[128,384]{1,0:T(8,128)(2,1)S(1)}, u32[]{:S(2)}) copy-start(bf16[128,384]{1,0:T(8,128)(2,1)S(1)} %collective-permute-done.g1) | copy-start | bytes 294916
  21.4 0.6 copy-start.13
  25.4 0.9 copy-start.3
  26.3 9.5 %copy-start.2 = (bf16[1,3072,512]{2,1,0:T(8,128)(2,1)S(1)}, bf16[1,3072,512]{2,1,0:T(8,128)(2,1)}, u32[]{:S(2)}) copy-start(bf16[1,3072,512]{2,1,0:T(8,128)(2,1)} %param.11) | copy-start | bytes 9437188
  26.3 47.3 %all-to-all-start.1 = ((bf16[16,64,1536]{2,1,0:T(8,128)(2,1)}), bf16[16,64,1536]{2,1,0:T(8,128)(2,1)}, u32[]{:S(2)}, u32[]{:S(2)}) async-start(bf16[16,64,1536]{2,1,0:T(8,128)(2,1)} %dispatch.2), calls=%async_computation.1 | async-start | bytes 6291456 | tf_op jit(solution)/shard_map/gather/all_to_all | solution.py:410
  33.8 17.1 %collective-permute-start.7 = (bf16[1024,384]{1,0:T(8,128)(2,1)}, bf16[1024,384]{1,0:T(8,128)(2,1)}, u32[]{:S(2)}, u32[]{:S(2)}) collective-permute-start(bf16[1024,384]{1,0:T(8,128)(2,1)} %bitcast.45), channel_id=1, source_target_pairs={{0,6},{1,7},{2,0},{3,1},{4,2},{5,3},{6,4},{7,5},{8,14},{9,15},{10,... | collective-permute-start | bytes 2359304 | tf_op jit(solution)/shard_map/gather/ppermute | solution.py:402
  34.4 19.1 %collective-permute-start.5 = (bf16[1024,384]{1,0:T(8,128)(2,1)}, bf16[1024,384]{1,0:T(8,128)(2,1)}, u32[]{:S(2)}, u32[]{:S(2)}) collective-permute-start(bf16[1024,384]{1,0:T(8,128)(2,1)} %bitcast.46), channel_id=1, source_target_pairs={{0,2},{1,3},{2,4},{3,5},{4,6},{5,7},{6,0},{7,1},{8,10},{9,11},{10,... | collective-permute-start | bytes 2359304 | tf_op jit(solution)/shard_map/gather/ppermute | solution.py:402
  35.9 3.4 %copy-start.4 = (bf16[16,64,384]{2,1,0:T(8,128)(2,1)S(1)}, bf16[16,64,384]{2,1,0:T(8,128)(2,1)}, u32[]{:S(2)}) copy-start(bf16[16,64,384]{2,1,0:T(8,128)(2,1)} %copy-done.3) | copy-start | bytes 2359300
  39.3 16.0 %collective-permute-start.9 = (bf16[1024,384]{1,0:T(8,128)(2,1)S(1)}, bf16[1024,384]{1,0:T(8,128)(2,1)S(1)}, u32[]{:S(2)}, u32[]{:S(2)}) collective-permute-start(bf16[1024,384]{1,0:T(8,128)(2,1)S(1)} %bitcast.49), channel_id=1, source_target_pairs={{0,1},{1,0},{2,3},{3,2},{4,5},{5,4},{6,7},{7,6},{8,9},{9,8},{10,11... | collective-permute-start | bytes 2359304 | tf_op jit(solution)/shard_map/gather/ppermute | solution.py:407
  50.9 7.5 %collective-permute-start.10 = (bf16[1024,384]{1,0:T(8,128)(2,1)}, bf16[1024,384]{1,0:T(8,128)(2,1)S(1)}, u32[]{:S(2)}, u32[]{:S(2)}) collective-permute-start(bf16[1024,384]{1,0:T(8,128)(2,1)} %collective-permute-done.7.refs_1_), channel_id=1, source_target_pairs={{0,1},{1,0},{2,3},{3,2},{4,5},{5,4},{6,7},{7,6},{8,9},{9,8},{10,11... | collective-permute-start | bytes 2359304 | tf_op jit(solution)/shard_map/gather/ppermute | solution.py:407
  50.9 20.3 %collective-permute-start.3 = (bf16[4,384,512]{2,1,0:T(8,128)(2,1)}, bf16[4,384,512]{2,1,0:T(8,128)(2,1)}, u32[]{:S(2)}, u32[]{:S(2)}) collective-permute-start(bf16[4,384,512]{2,1,0:T(8,128)(2,1)} %get-tuple-element.34), channel_id=1, source_target_pairs={{0,1},{1,0},{2,3},{3,2},{4,5},{5,4},{6,7},{7,6},{8,9},{9,8},{10,11... | collective-permute-start | bytes 4718600 | tf_op jit(solution)/shard_map/gather/ppermute | solution.py:407
  51.4 19.8 %collective-permute-start.4 = (bf16[4,384,512]{2,1,0:T(8,128)(2,1)}, bf16[4,384,512]{2,1,0:T(8,128)(2,1)}, u32[]{:S(2)}, u32[]{:S(2)}) collective-permute-start(bf16[4,384,512]{2,1,0:T(8,128)(2,1)} %get-tuple-element.35), channel_id=1, source_target_pairs={{0,1},{1,0},{2,3},{3,2},{4,5},{5,4},{6,7},{7,6},{8,9},{9,8},{10,11... | collective-permute-start | bytes 4718600 | tf_op jit(solution)/shard_map/gather/ppermute | solution.py:407
  53.5 5.6 %collective-permute-start.11 = (bf16[1024,384]{1,0:T(8,128)(2,1)}, bf16[1024,384]{1,0:T(8,128)(2,1)}, u32[]{:S(2)}, u32[]{:S(2)}) collective-permute-start(bf16[1024,384]{1,0:T(8,128)(2,1)} %collective-permute-done.5.refs_2_), channel_id=1, source_target_pairs={{0,1},{1,0},{2,3},{3,2},{4,5},{5,4},{6,7},{7,6},{8,9},{9,8},{10,11... | collective-permute-start | bytes 2359304 | tf_op jit(solution)/shard_map/gather/ppermute | solution.py:407
  55.3 3.8 %copy-start.5 = (bf16[1024,384]{1,0:T(8,128)(2,1)}, bf16[1024,384]{1,0:T(8,128)(2,1)S(1)}, u32[]{:S(2)}) copy-start(bf16[1024,384]{1,0:T(8,128)(2,1)S(1)} %collective-permute-done.9.refs_3_) | copy-start | bytes 2359300
  55.3 13.5 %collective-permute-start.8 = (bf16[512,384]{1,0:T(8,128)(2,1)}, bf16[512,384]{1,0:T(8,128)(2,1)S(1)}, u32[]{:S(2)}, u32[]{:S(2)}) collective-permute-start(bf16[512,384]{1,0:T(8,128)(2,1)} %slice.9), channel_id=1, source_target_pairs={{0,6},{1,7},{2,0},{3,1},{4,2},{5,3},{6,4},{7,5},{8,14},{9,15},{10,... | collective-permute-start | bytes 1179656 | tf_op jit(solution)/shard_map/gather/ppermute | solution.py:402
  58.4 0.9 copy-start.6
  58.4 12.3 %collective-permute-start.6 = (bf16[512,384]{1,0:T(8,128)(2,1)}, bf16[512,384]{1,0:T(8,128)(2,1)}, u32[]{:S(2)}, u32[]{:S(2)}) collective-permute-start(bf16[512,384]{1,0:T(8,128)(2,1)} %slice.8), channel_id=1, source_target_pairs={{0,2},{1,3},{2,4},{3,5},{4,6},{5,7},{6,0},{7,1},{8,10},{9,11},{10,... | collective-permute-start | bytes 1179656 | tf_op jit(solution)/shard_map/gather/ppermute | solution.py:402
  68.8 4.8 %copy-start.7 = (bf16[512,384]{1,0:T(8,128)(2,1)}, bf16[512,384]{1,0:T(8,128)(2,1)S(1)}, u32[]{:S(2)}) copy-start(bf16[512,384]{1,0:T(8,128)(2,1)S(1)} %collective-permute-done.8.refs_1_.refs_7_) | copy-start | bytes 1179652
  70.7 2.5 %collective-permute-start.12 = (bf16[512,384]{1,0:T(8,128)(2,1)}, bf16[512,384]{1,0:T(8,128)(2,1)S(1)}, u32[]{:S(2)}, u32[]{:S(2)}) collective-permute-start(bf16[512,384]{1,0:T(8,128)(2,1)} %collective-permute-done.6.refs_0_.refs_6_), channel_id=1, source_target_pairs={{0,1},{1,0},{2,3},{3,2},{4,5},{5,4},{6,7},{7,6},{8,9},{9,8},{10,11... | collective-permute-start | bytes 1179656 | tf_op jit(solution)/shard_map/forward/ppermute | solution.py:407
  70.7 2.5 %collective-permute-start.13 = (bf16[512,384]{1,0:T(8,128)(2,1)S(1)}, bf16[512,384]{1,0:T(8,128)(2,1)S(1)}, u32[]{:S(2)}, u32[]{:S(2)}) collective-permute-start(bf16[512,384]{1,0:T(8,128)(2,1)S(1)} %collective-permute-done.8.refs_1_.refs_7_), channel_id=1, source_target_pairs={{0,1},{1,0},{2,3},{3,2},{4,5},{5,4},{6,7},{7,6},{8,9},{9,8},{10,11... | collective-permute-start | bytes 1179656 | tf_op jit(solution)/shard_map/forward/ppermute | solution.py:407
  73.1 0.7 copy-start.8
  73.1 0.9 copy-start.9
  73.7 6.1 %collective-permute-start.14 = (bf16[1024,1536]{1,0:T(8,128)(2,1)}, bf16[1024,1536]{1,0:T(8,128)(2,1)}, u32[]{:S(2)}, u32[]{:S(2)}) collective-permute-start(bf16[1024,1536]{1,0:T(8,128)(2,1)} %bitcast.4.own), channel_id=1, source_target_pairs={{0,1},{1,0},{2,3},{3,2},{4,5},{5,4},{6,7},{7,6},{8,9},{9,8},{10,11... | collective-permute-start | bytes 9437192 | tf_op jit(solution)/shard_map/forward/ppermute | solution.py:407
  88.1 7.7 %collective-permute-start.15 = (bf16[1024,1024]{1,0:T(8,128)(2,1)}, bf16[1024,1024]{1,0:T(8,128)(2,1)}, u32[]{:S(2)}, u32[]{:S(2)}) collective-permute-start(bf16[1024,1024]{1,0:T(8,128)(2,1)} %get-tuple-element.45.grads), channel_id=1, source_target_pairs={{0,1},{1,0},{2,3},{3,2},{4,5},{5,4},{6,7},{7,6},{8,9},{9,8},{10,11... | collective-permute-start | bytes 6291464 | tf_op jit(solution)/shard_map/backward/ppermute | solution.py:407
  88.3 7.4 %collective-permute-start.16 = (bf16[1024,128]{1,0:T(8,128)(2,1)}, bf16[1024,128]{1,0:T(8,128)(2,1)S(1)}, u32[]{:S(2)}, u32[]{:S(2)}) collective-permute-start(bf16[1024,128]{1,0:T(8,128)(2,1)} %get-tuple-element.43), channel_id=1, source_target_pairs={{0,1},{1,0},{2,3},{3,2},{4,5},{5,4},{6,7},{7,6},{8,9},{9,8},{10,11... | collective-permute-start | bytes 786440 | tf_op jit(solution)/shard_map/backward/ppermute | solution.py:407
  95.7 0.7 copy-start.10
  104.1 35.7 %all-to-all-start.3 = ((bf16[16,32,1664]{2,1,0:T(8,128)(2,1)}), bf16[16,32,1664]{2,1,0:T(8,128)(2,1)S(1)}, u32[]{:S(2)}, u32[]{:S(2)}) async-start(bf16[16,32,1664]{2,1,0:T(8,128)(2,1)} %get-tuple-element.52), calls=%async_computation.3 | async-start | bytes 3407872 | tf_op jit(solution)/shard_map/sums/all_to_all | solution.py:410
  114.3 23.1 %collective-permute-start.17 = (bf16[16,32,384]{2,1,0:T(8,128)(2,1)}, bf16[16,32,384]{2,1,0:T(8,128)(2,1)}, u32[]{:S(2)}, u32[]{:S(2)}) collective-permute-start(bf16[16,32,384]{2,1,0:T(8,128)(2,1)} %get-tuple-element.49), channel_id=1, source_target_pairs={{0,2},{1,3},{2,4},{3,5},{4,6},{5,7},{6,0},{7,1},{8,10},{9,11},{10,... | collective-permute-start | bytes 1179656 | tf_op jit(solution)/shard_map/sums/ppermute | solution.py:402
  115.2 22.3 %collective-permute-start.18 = (bf16[16,32,384]{2,1,0:T(8,128)(2,1)}, bf16[16,32,384]{2,1,0:T(8,128)(2,1)}, u32[]{:S(2)}, u32[]{:S(2)}) collective-permute-start(bf16[16,32,384]{2,1,0:T(8,128)(2,1)} %get-tuple-element.50), channel_id=1, source_target_pairs={{0,4},{1,5},{2,6},{3,7},{4,0},{5,1},{6,2},{7,3},{8,12},{9,13},{10,... | collective-permute-start | bytes 1179656 | tf_op jit(solution)/shard_map/sums/ppermute | solution.py:402
  117.7 19.8 %collective-permute-start.19 = (bf16[16,32,384]{2,1,0:T(8,128)(2,1)}, bf16[16,32,384]{2,1,0:T(8,128)(2,1)}, u32[]{:S(2)}, u32[]{:S(2)}) collective-permute-start(bf16[16,32,384]{2,1,0:T(8,128)(2,1)} %get-tuple-element.51), channel_id=1, source_target_pairs={{0,6},{1,7},{2,0},{3,1},{4,2},{5,3},{6,4},{7,5},{8,14},{9,15},{10,... | collective-permute-start | bytes 1179656 | tf_op jit(solution)/shard_map/sums/ppermute | solution.py:402
  129.9 17.1 %copy-start = (s32[128,2]{0,1:T(2,128)S(1)}, s32[128,2]{0,1:T(2,128)}, u32[]{:S(2)}) copy-start(s32[128,2]{0,1:T(2,128)} %param.9) | copy-start | bytes 3076
  137.4 18.9 %copy-start.1 = (bf16[128,2]{0,1:T(2,128)(2,1)S(1)}, bf16[128,2]{0,1:T(2,128)(2,1)}, u32[]{:S(2)}) copy-start(bf16[128,2]{0,1:T(2,128)(2,1)} %param.10) | copy-start | bytes 1540
  139.8 15.3 %all-to-all-start.2 = ((bf16[16,32,384]{2,1,0:T(8,128)(2,1)}), bf16[16,32,384]{2,1,0:T(8,128)(2,1)S(1)}, u32[]{:S(2)}, u32[]{:S(2)}) async-start(bf16[16,32,384]{2,1,0:T(8,128)(2,1)} %add_convert_fusion), calls=%async_computation.2 | async-start | bytes 786432 | tf_op jit(solution)/shard_map/late_sum/all_to_all | solution.py:410
  147.9 8.3 %collective-permute-start.20 = (bf16[128,512]{1,0:T(8,128)(2,1)S(1)}, bf16[128,512]{1,0:T(8,128)(2,1)S(1)}, u32[]{:S(2)}, u32[]{:S(2)}) collective-permute-start(bf16[128,512]{1,0:T(8,128)(2,1)S(1)} %get-tuple-element.55), channel_id=1, source_target_pairs={{0,2},{1,3},{2,4},{3,5},{4,6},{5,7},{6,0},{7,1},{8,10},{9,11},{10,... | collective-permute-start | bytes 393224 | tf_op jit(solution)/shard_map/finish/ppermute | solution.py:402
  148.7 7.5 %collective-permute-start.21 = (bf16[128,512]{1,0:T(8,128)(2,1)S(1)}, bf16[128,512]{1,0:T(8,128)(2,1)S(1)}, u32[]{:S(2)}, u32[]{:S(2)}) collective-permute-start(bf16[128,512]{1,0:T(8,128)(2,1)S(1)} %get-tuple-element.56), channel_id=1, source_target_pairs={{0,4},{1,5},{2,6},{3,7},{4,0},{5,1},{6,2},{7,3},{8,12},{9,13},{10,... | collective-permute-start | bytes 393224 | tf_op jit(solution)/shard_map/finish/ppermute | solution.py:402
  150.3 6.1 %collective-permute-start.22 = (bf16[128,512]{1,0:T(8,128)(2,1)S(1)}, bf16[128,512]{1,0:T(8,128)(2,1)S(1)}, u32[]{:S(2)}, u32[]{:S(2)}) collective-permute-start(bf16[128,512]{1,0:T(8,128)(2,1)S(1)} %get-tuple-element.57), channel_id=1, source_target_pairs={{0,6},{1,7},{2,0},{3,1},{4,2},{5,3},{6,4},{7,5},{8,14},{9,15},{10,... | collective-permute-start | bytes 393224 | tf_op jit(solution)/shard_map/finish/ppermute | solution.py:402

commit v5 on v4

--- a/solution.py
+++ b/solution.py
@@ -9,6 +9,7 @@
 F32 = jnp.float32
 VMEM_LIMIT = 62 * 1024 * 1024
 SMALL_LIMIT = 16 * 1024 * 1024
+SHADOW_LIMIT = 56 * 1024 * 1024
 EXPERTS = 8
 CAP = 64
 EARLY = 32
@@ -82,7 +83,7 @@
     return ((t // 2 + dy) % 4) * 2 + core
 
 
-def plain_call(body, t, ins, outs, scratch, copies, flops, nbytes):
+def plain_call(body, t, ins, outs, scratch, copies, flops, nbytes, limit=VMEM_LIMIT):
     anywhere = pl.BlockSpec(memory_space=pltpu.HBM)
     return pl.pallas_call(
         body,
@@ -91,7 +92,7 @@
         out_specs=[anywhere] * len(outs),
         scratch_shapes=[pltpu.VMEM(shape, dtype) for shape, dtype in scratch]
         + [pltpu.SemaphoreType.DMA((copies,))],
-        compiler_params=pltpu.CompilerParams(vmem_limit_bytes=VMEM_LIMIT),
+        compiler_params=pltpu.CompilerParams(vmem_limit_bytes=limit),
         cost_estimate=pl.CostEstimate(flops=flops, bytes_accessed=nbytes, transcendentals=0),
     )(t, *ins)
 
@@ -515,6 +516,7 @@
             27,
             1,
             1,
+            SHADOW_LIMIT,
         )
     with jax.named_scope("weights_down"):
         (grad_down,) = plain_call(
@@ -527,6 +529,7 @@
             13,
             1,
             1,
+            SHADOW_LIMIT,
         )
     with jax.named_scope("late_sum"):
         mine = after(late[0], grad_down)

time: 158 us -> 157 us (level)
  transfers between devices with their start and end apart: 27 -> 27, of which waited for: 11 -> 13; matrix products, arithmetic and copies ran while one was open for 6% -> 5% of each run, Pallas kernels for 29% -> 29%
where the time goes in v5:
time: 157 us
  Pallas kernels  64.2 us (41%)
  starting transfers between devices  53 us (34%)
  waiting for transfers between devices  28.1 us (18%)
  local copies, waits for them, and re-layouts  9.64 us (6%)
    pallas_call x7, Pallas kernels, plain_call(): pl.pallas_call(body, out_shape=outs, in_specs=[pl.BlockSpec(memory_space=...  56.7 us
    all_to_all x4, starting transfers between devices, exchange(): lax.all_to_all(x, ('dp', 'ctx'), split_axis=0, concat_axis=0, tiled=True)  32.6 us
    ppermute x13, waiting for transfers between devices, from_y(): lax.ppermute(x, 'tensor', [(i, (i // 2 - dy) % 4 * 2 + i % 2) for i in ra...  22 us
    ppermute x13, starting transfers between devices, from_y(): lax.ppermute(x, 'tensor', [(i, (i // 2 - dy) % 4 * 2 + i % 2) for i in ra...  18.7 us
    all_to_all x4, waiting for transfers between devices, exchange(): lax.all_to_all(x, ('dp', 'ctx'), split_axis=0, concat_axis=0, tiled=True)  4.1 us
    slice x2, local copies, waits for them, and re-layouts, on_device(): far_xs = [from_y(down1[:HALF], 3), from_y(up1[HALF:], 1)]  3.57 us
    squeeze x1, local copies, waits for them, and re-layouts, sibling_rows(): lax.dynamic_index_in_dim(w.reshape(4, 2, COLS, HID), 1 - core, 1, False)  3.43 us
    pallas_call x1, Pallas kernels, on_device(): call(dispatch_g_body, sds((16, CAP, wide)), VMEM_LIMIT, flops=2 * 10 ** 8...  3.41 us
  transfers between devices with their start and end apart: 27, of which 13 were waited for; matrix products, arithmetic and copies ran while one was open for 5% of the time, Pallas kernels for 29%

profile of v5, /device:TPU:2, one launch (start us, length us, event | category | flops | bytes accessed | tf_op | source)
XLA Modules:
  0.0 156.7 jit_solution(5967899444363931416)
XLA Ops:
  0.6 2.2 %dispatch.3 = bf16[16,64,384]{2,1,0:T(8,128)(2,1)} custom-call(s32[2,128]{1,0:T(2,128)} %bitcast.30, bf16[128,384]{1,0:T(8,128)(2,1)} %tokens.1), custom_call_target="tpu_custom_call" | custom-call | flops 100000000 | bytes 1048576 | tf_op jit(solution)/shard_map/dispatch/pallas_call | solution.py:421
  2.8 8.3 %all-to-all-start = ((bf16[16,64,384]{2,1,0:T(8,128)(2,1)}), bf16[16,64,384]{2,1,0:T(8,128)(2,1)S(1)}, u32[]{:S(2)}, u32[]{:S(2)}) async-start(bf16[16,64,384]{2,1,0:T(8,128)(2,1)} %dispatch.3), calls=%async_computation | async-start | bytes 1572864 | tf_op jit(solution)/shard_map/dispatch/all_to_all | solution.py:411
  11.1 3.2 %collective-permute-start.1 = (bf16[128,384]{1,0:T(8,128)(2,1)}, bf16[128,384]{1,0:T(8,128)(2,1)S(1)}, u32[]{:S(2)}, u32[]{:S(2)}) collective-permute-start(bf16[128,384]{1,0:T(8,128)(2,1)} %g0.1), channel_id=1, source_target_pairs={{0,4},{1,5},{2,6},{3,7},{4,0},{5,1},{6,2},{7,3},{8,12},{9,13},{10,... | collective-permute-start | bytes 294920 | tf_op jit(solution)/shard_map/dispatch/ppermute | solution.py:403
  14.3 1.1 collective-permute-start
  15.4 1.0 collective-permute-start.2
  16.3 1.8 %collective-permute-done.1.g2 = bf16[128,384]{1,0:T(8,128)(2,1)S(1)} collective-permute-done((bf16[128,384]{1,0:T(8,128)(2,1)}, bf16[128,384]{1,0:T(8,128)(2,1)S(1)}, u32[]{:S(2)}, u32[]{:S(2)}) %collective-permute-start.1) | collective-permute-done | bytes 98336 | tf_op jit(solution)/shard_map/dispatch/ppermute | solution.py:403
  18.1 1.2 collective-permute-done.g1
  19.3 2.1 %collective-permute-done.2.g3 = bf16[128,384]{1,0:T(8,128)(2,1)S(1)} collective-permute-done((bf16[128,384]{1,0:T(8,128)(2,1)}, bf16[128,384]{1,0:T(8,128)(2,1)S(1)}, u32[]{:S(2)}, u32[]{:S(2)}) %collective-permute-start.2) | collective-permute-done | bytes 98336 | tf_op jit(solution)/shard_map/dispatch/ppermute | solution.py:403
  21.4 0.6 copy-done.13
  22.0 3.4 %dispatch.2 = bf16[16,64,1536]{2,1,0:T(8,128)(2,1)} custom-call(s32[2,128]{1,0:T(2,128)} %bitcast.31, bf16[2,128]{1,0:T(2,128)(2,1)} %bitcast.34, bf16[128,384]{1,0:T(8,128)(2,1)} %g0.1, bf16[128,384]{1,0:T(8,128)(2,1)} %copy-done.12, bf16[128,384]{1,0:T(8,128)(2,1)} %copy-done.11, bf16[128,384]{1,0:T(8,128)(2,1)} %copy-done.13), custom_call_target="tpu_custom_call" | custom-call | flops 200000000 | bytes 4194304 | tf_op jit(solution)/shard_map/dispatch/pallas_call | solution.py:423
  25.5 0.9 copy-done.3
  26.4 7.5 %all-to-all-start.1 = ((bf16[16,64,1536]{2,1,0:T(8,128)(2,1)}), bf16[16,64,1536]{2,1,0:T(8,128)(2,1)}, u32[]{:S(2)}, u32[]{:S(2)}) async-start(bf16[16,64,1536]{2,1,0:T(8,128)(2,1)} %dispatch.2), calls=%async_computation.1 | async-start | bytes 6291456 | tf_op jit(solution)/shard_map/gather/all_to_all | solution.py:411
  33.9 0.6 collective-permute-start.7
  34.4 1.5 collective-permute-start.5
  35.9 3.4 %dynamic-slice_bitcast_fusion = (bf16[4,384,512]{2,1,0:T(8,128)(2,1)}, bf16[4,384,512]{2,1,0:T(8,128)(2,1)}) fusion(bf16[4,2,384,512]{3,2,1,0:T(8,128)(2,1)} %bitcast.40, s32[]{:T(128)S(6)} %select_n.13, bf16[4,2,384,512]{3,2,1,0:T(8,128)(2,1)S(1)} %bitcast.39), kind=kLoop, calls=%fused_computation | loop fusion | bytes 6291460 | tf_op jit(solution)/shard_map/gather/jit(dynamic_index_in_dim)/squeeze | solution.py:435
  39.3 11.6 %collective-permute-done.7.refs_1_ = bf16[1024,384]{1,0:T(8,128)(2,1)} collective-permute-done((bf16[1024,384]{1,0:T(8,128)(2,1)}, bf16[1024,384]{1,0:T(8,128)(2,1)}, u32[]{:S(2)}, u32[]{:S(2)}) %collective-permute-start.7) | collective-permute-done | bytes 786464 | tf_op jit(solution)/shard_map/gather/ppermute | solution.py:403
  50.9 0.5 collective-permute-start.3
  51.4 2.1 %collective-permute-done.5.refs_2_ = bf16[1024,384]{1,0:T(8,128)(2,1)} collective-permute-done((bf16[1024,384]{1,0:T(8,128)(2,1)}, bf16[1024,384]{1,0:T(8,128)(2,1)}, u32[]{:S(2)}, u32[]{:S(2)}) %collective-permute-start.5) | collective-permute-done | bytes 786464 | tf_op jit(solution)/shard_map/gather/ppermute | solution.py:403
  53.5 1.8 %slice.9 = bf16[512,384]{1,0:T(8,128)(2,1)} slice(bf16[1024,384]{1,0:T(8,128)(2,1)} %collective-permute-done.7.refs_1_), slice={[512:1024], [0:384]} | slice | bytes 786432 | tf_op jit(solution)/shard_map/gather/slice | solution.py:430
  55.3 1.3 collective-permute-start.8
  56.6 1.8 %slice.8 = bf16[512,384]{1,0:T(8,128)(2,1)} slice(bf16[1024,384]{1,0:T(8,128)(2,1)} %collective-permute-done.5.refs_2_), slice={[0:512], [0:384]} | slice | bytes 786432 | tf_op jit(solution)/shard_map/gather/slice | solution.py:430
  58.4 0.7 collective-permute-start.6
  59.3 9.5 %forward.2.refs_4_ = f32[1024,1024]{1,0:T(8,128)} custom-call(s32[1]{0:T(128)} %bitcast.2.t, bf16[1024,384]{1,0:T(8,128)(2,1)} %bitcast.47, bf16[1024,384]{1,0:T(8,128)(2,1)} %collective-permute-done.7.refs_1_, bf16[1024,384]{1,0:T(8,128)(2,1)} %collective-permute-done.5.refs_2_, bf16[1024,384]{1,0:T(8,128)(2,1)} %copy-done.5, bf16[1024,384]{1,0:T(8,128)(2,1)} %copy-done.6, ...), custom_call_target="tpu_custom_call" | custom-call | flops 1 | bytes 1 | tf_op jit(solution)/shard_map/forward/pallas_call | solution.py:88
  68.9 1.8 %collective-permute-done.6.refs_0_.refs_6_ = bf16[512,384]{1,0:T(8,128)(2,1)} collective-permute-done((bf16[512,384]{1,0:T(8,128)(2,1)}, bf16[512,384]{1,0:T(8,128)(2,1)}, u32[]{:S(2)}, u32[]{:S(2)}) %collective-permute-start.6) | collective-permute-done | bytes 393248 | tf_op jit(solution)/shard_map/gather/ppermute | solution.py:403
  71.2 1.4 collective-permute-done.12.refs_2_.refs_8_
  72.6 0.6 collective-permute-done.13.refs_3_.refs_9_
  73.2 0.5 all-to-all-done.1
  73.9 5.8 %forward.3 = (f32[1024,512]{1,0:T(8,128)}, f32[1024,512]{1,0:T(8,128)}, bf16[1024,512]{1,0:T(8,128)(2,1)}) custom-call(s32[1]{0:T(128)} %bitcast.2.t, bf16[512,384]{1,0:T(8,128)(2,1)} %collective-permute-done.6.refs_0_.refs_6_, bf16[512,384]{1,0:T(8,128)(2,1)} %collective-permute-done.8.refs_1_.refs_7_, bf16[512,384]{1,0:T(8,128)(2,1)} %copy-done.7, ...), custom_call_target="tpu_custom_call" | custom-call | flops 1 | bytes 1 | tf_op jit(solution)/shard_map/forward/pallas_call | solution.py:88
  79.7 8.3 %backward.1 = (bf16[1024,1024]{1,0:T(8,128)(2,1)}, bf16[1024,128]{1,0:T(8,128)(2,1)}) custom-call(s32[1]{0:T(128)} %bitcast.2.t, bf16[1024,1536]{1,0:T(8,128)(2,1)} %bitcast.4.own, bf16[1024,1536]{1,0:T(8,128)(2,1)} %collective-permute-done.14.sib, f32[1024,512]{1,0:T(8,128)} %get-tuple-element.39.act, f32[1024,512]{1,0:T(8,128)} %get-tuple-element.40.slope, ...), custom_call_target="tpu_custom_call" | custom-call | flops 1 | bytes 1 | tf_op jit(solution)/shard_map/backward/pallas_call | solution.py:88
  88.7 7.1 %sums.2 = bf16[1024,1536]{1,0:T(8,128)(2,1)} custom-call(s32[1]{0:T(128)} %bitcast.2.t, bf16[1024,1024]{1,0:T(8,128)(2,1)} %get-tuple-element.45.grads, bf16[3072,512]{1,0:T(8,128)(2,1)} %bitcast.38, bf16[3072,512]{1,0:T(8,128)(2,1)} %bitcast.43), custom_call_target="tpu_custom_call" | custom-call | flops 1 | bytes 1 | tf_op jit(solution)/shard_map/sums/pallas_call | solution.py:88
  95.8 0.7 copy-done.10
  96.5 7.6 %sums.3 = (bf16[16,32,1664]{2,1,0:T(8,128)(2,1)}, bf16[16,32,384]{2,1,0:T(8,128)(2,1)}, bf16[16,32,384]{2,1,0:T(8,128)(2,1)}, bf16[16,32,384]{2,1,0:T(8,128)(2,1)}, bf16[16,32,384]{2,1,0:T(8,128)(2,1)}) custom-call(s32[1]{0:T(128)} %bitcast.2.t, bf16[16,64,1536]{2,1,0:T(8,128)(2,1)} %bitcast.44, bf16[16,64,1024]{2,1,0:T(8,128)(2,1)} %bitcast.13.grads_sib, ...), custom_call_target="tpu_custom_call" | custom-call | flops 1 | bytes 1 | tf_op jit(solution)/shard_map/sums/pallas_call | solution.py:88
  104.1 10.4 %all-to-all-start.3 = ((bf16[16,32,1664]{2,1,0:T(8,128)(2,1)}), bf16[16,32,1664]{2,1,0:T(8,128)(2,1)S(1)}, u32[]{:S(2)}, u32[]{:S(2)}) async-start(bf16[16,32,1664]{2,1,0:T(8,128)(2,1)} %get-tuple-element.52), calls=%async_computation.3 | async-start | bytes 3407872 | tf_op jit(solution)/shard_map/sums/all_to_all | solution.py:411
  114.5 0.9 collective-permute-start.17
  115.4 2.5 %collective-permute-start.18 = (bf16[16,32,384]{2,1,0:T(8,128)(2,1)S(1)}, bf16[16,32,384]{2,1,0:T(8,128)(2,1)S(1)}, u32[]{:S(2)}, u32[]{:S(2)}) collective-permute-start(bf16[16,32,384]{2,1,0:T(8,128)(2,1)S(1)} %copy-done.15), channel_id=1, source_target_pairs={{0,4},{1,5},{2,6},{3,7},{4,0},{5,1},{6,2},{7,3},{8,12},{9,13},{10,... | collective-permute-start | bytes 1179656 | tf_op jit(solution)/shard_map/sums/ppermute | solution.py:403
  117.9 1.3 collective-permute-start.19
  119.2 10.9 %weights_gate_up.1 = (bf16[3072,512]{1,0:T(8,128)(2,1)}, bf16[3072,512]{1,0:T(8,128)(2,1)}) custom-call(s32[1]{0:T(128)} %bitcast.2.t, bf16[1024,1024]{1,0:T(8,128)(2,1)} %get-tuple-element.45.grads, bf16[1024,384]{1,0:T(8,128)(2,1)} %bitcast.48, bf16[1024,384]{1,0:T(8,128)(2,1)} %collective-permute-done.7.refs_1_, ...), custom_call_target="tpu_custom_call" | custom-call | flops 1 | bytes 1 | tf_op jit(solution)/shard_map/weights_gate_up/pallas_call | solution.py:88
  130.1 7.6 %weights_down.1 = bf16[512,3072]{1,0:T(8,128)(2,1)} custom-call(s32[1]{0:T(128)} %bitcast.2.t, bf16[1024,512]{1,0:T(8,128)(2,1)} %get-tuple-element.47.hidden, bf16[1024,1536]{1,0:T(8,128)(2,1)} %bitcast.4.own, bf16[1024,1536]{1,0:T(8,128)(2,1)} %collective-permute-done.14.sib), custom_call_target="tpu_custom_call" | custom-call | flops 1 | bytes 1 | tf_op jit(solution)/shard_map/weights_down/pallas_call | solution.py:88
  137.8 1.0 add_convert_fusion
  138.7 1.1 all-to-all-done.3
  139.8 6.4 %all-to-all-start.2 = ((bf16[16,32,384]{2,1,0:T(8,128)(2,1)}), bf16[16,32,384]{2,1,0:T(8,128)(2,1)S(1)}, u32[]{:S(2)}, u32[]{:S(2)}) async-start(bf16[16,32,384]{2,1,0:T(8,128)(2,1)} %add_convert_fusion), calls=%async_computation.2 | async-start | bytes 786432 | tf_op jit(solution)/shard_map/late_sum/all_to_all | solution.py:411
  146.2 0.8 finish.2
  147.1 0.9 collective-permute-start.20
  148.0 2.5 %collective-permute-start.21 = (bf16[128,512]{1,0:T(8,128)(2,1)S(1)}, bf16[128,512]{1,0:T(8,128)(2,1)S(1)}, u32[]{:S(2)}, u32[]{:S(2)}) collective-permute-start(bf16[128,512]{1,0:T(8,128)(2,1)S(1)} %get-tuple-element.56), channel_id=1, source_target_pairs={{0,4},{1,5},{2,6},{3,7},{4,0},{5,1},{6,2},{7,3},{8,12},{9,13},{10,... | collective-permute-start | bytes 393224 | tf_op jit(solution)/shard_map/finish/ppermute | solution.py:403
  150.5 1.3 collective-permute-start.22
  151.8 2.5 %all-to-all-done.2 = bf16[16,32,384]{2,1,0:T(8,128)(2,1)S(1)} async-done(((bf16[16,32,384]{2,1,0:T(8,128)(2,1)}), bf16[16,32,384]{2,1,0:T(8,128)(2,1)S(1)}, u32[]{:S(2)}, u32[]{:S(2)}) %all-to-all-start.2) | async-done | bytes 393248 | tf_op jit(solution)/shard_map/late_sum/all_to_all | solution.py:411
  154.3 0.9 collective-permute-done.21.m2
  155.6 1.1 finish.3
  (55 shorter events, 2.2 us)
Async XLA Ops:
  2.8 22.7 %all-to-all-start = ((bf16[16,64,384]{2,1,0:T(8,128)(2,1)}), bf16[16,64,384]{2,1,0:T(8,128)(2,1)S(1)}, u32[]{:S(2)}, u32[]{:S(2)}) async-start(bf16[16,64,384]{2,1,0:T(8,128)(2,1)} %dispatch.3), calls=%async_computation | async-start | bytes 1572864 | tf_op jit(solution)/shard_map/dispatch/all_to_all | solution.py:411
  11.1 7.0 %collective-permute-start.1 = (bf16[128,384]{1,0:T(8,128)(2,1)}, bf16[128,384]{1,0:T(8,128)(2,1)S(1)}, u32[]{:S(2)}, u32[]{:S(2)}) collective-permute-start(bf16[128,384]{1,0:T(8,128)(2,1)} %g0.1), channel_id=1, source_target_pairs={{0,4},{1,5},{2,6},{3,7},{4,0},{5,1},{6,2},{7,3},{8,12},{9,13},{10,... | collective-permute-start | bytes 294920 | tf_op jit(solution)/shard_map/dispatch/ppermute | solution.py:403
  14.3 5.0 %collective-permute-start = (bf16[128,384]{1,0:T(8,128)(2,1)}, bf16[128,384]{1,0:T(8,128)(2,1)S(1)}, u32[]{:S(2)}, u32[]{:S(2)}) collective-permute-start(bf16[128,384]{1,0:T(8,128)(2,1)} %g0.1), channel_id=1, source_target_pairs={{0,6},{1,7},{2,0},{3,1},{4,2},{5,3},{6,4},{7,5},{8,14},{9,15},{10,... | collective-permute-start | bytes 294920 | tf_op jit(solution)/shard_map/dispatch/ppermute | solution.py:403
  15.4 6.0 %collective-permute-start.2 = (bf16[128,384]{1,0:T(8,128)(2,1)}, bf16[128,384]{1,0:T(8,128)(2,1)S(1)}, u32[]{:S(2)}, u32[]{:S(2)}) collective-permute-start(bf16[128,384]{1,0:T(8,128)(2,1)} %g0.1), channel_id=1, source_target_pairs={{0,2},{1,3},{2,4},{3,5},{4,6},{5,7},{6,0},{7,1},{8,10},{9,11},{10,... | collective-permute-start | bytes 294920 | tf_op jit(solution)/shard_map/dispatch/ppermute | solution.py:403
  18.1 3.3 %copy-start.11 = (bf16[128,384]{1,0:T(8,128)(2,1)}, bf16[128,384]{1,0:T(8,128)(2,1)S(1)}, u32[]{:S(2)}) copy-start(bf16[128,384]{1,0:T(8,128)(2,1)S(1)} %collective-permute-done.1.g2) | copy-start | bytes 294916
  19.3 2.1 %copy-start.12 = (bf16[128,384]{1,0:T(8,128)(2,1)}, bf16[128,384]{1,0:T(8,128)(2,1)S(1)}, u32[]{:S(2)}) copy-start(bf16[128,384]{1,0:T(8,128)(2,1)S(1)} %collective-permute-done.g1) | copy-start | bytes 294916
  21.4 0.6 copy-start.13
  25.5 0.9 copy-start.3
  26.4 9.5 %copy-start.2 = (bf16[1,3072,512]{2,1,0:T(8,128)(2,1)S(1)}, bf16[1,3072,512]{2,1,0:T(8,128)(2,1)}, u32[]{:S(2)}) copy-start(bf16[1,3072,512]{2,1,0:T(8,128)(2,1)} %param.11) | copy-start | bytes 9437188
  26.4 47.3 %all-to-all-start.1 = ((bf16[16,64,1536]{2,1,0:T(8,128)(2,1)}), bf16[16,64,1536]{2,1,0:T(8,128)(2,1)}, u32[]{:S(2)}, u32[]{:S(2)}) async-start(bf16[16,64,1536]{2,1,0:T(8,128)(2,1)} %dispatch.2), calls=%async_computation.1 | async-start | bytes 6291456 | tf_op jit(solution)/shard_map/gather/all_to_all | solution.py:411
  33.9 17.1 %collective-permute-start.7 = (bf16[1024,384]{1,0:T(8,128)(2,1)}, bf16[1024,384]{1,0:T(8,128)(2,1)}, u32[]{:S(2)}, u32[]{:S(2)}) collective-permute-start(bf16[1024,384]{1,0:T(8,128)(2,1)} %bitcast.45), channel_id=1, source_target_pairs={{0,6},{1,7},{2,0},{3,1},{4,2},{5,3},{6,4},{7,5},{8,14},{9,15},{10,... | collective-permute-start | bytes 2359304 | tf_op jit(solution)/shard_map/gather/ppermute | solution.py:403
  34.4 19.1 %collective-permute-start.5 = (bf16[1024,384]{1,0:T(8,128)(2,1)}, bf16[1024,384]{1,0:T(8,128)(2,1)}, u32[]{:S(2)}, u32[]{:S(2)}) collective-permute-start(bf16[1024,384]{1,0:T(8,128)(2,1)} %bitcast.46), channel_id=1, source_target_pairs={{0,2},{1,3},{2,4},{3,5},{4,6},{5,7},{6,0},{7,1},{8,10},{9,11},{10,... | collective-permute-start | bytes 2359304 | tf_op jit(solution)/shard_map/gather/ppermute | solution.py:403
  35.9 3.4 %copy-start.4 = (bf16[16,64,384]{2,1,0:T(8,128)(2,1)S(1)}, bf16[16,64,384]{2,1,0:T(8,128)(2,1)}, u32[]{:S(2)}) copy-start(bf16[16,64,384]{2,1,0:T(8,128)(2,1)} %copy-done.3) | copy-start | bytes 2359300
  39.3 16.0 %collective-permute-start.9 = (bf16[1024,384]{1,0:T(8,128)(2,1)S(1)}, bf16[1024,384]{1,0:T(8,128)(2,1)S(1)}, u32[]{:S(2)}, u32[]{:S(2)}) collective-permute-start(bf16[1024,384]{1,0:T(8,128)(2,1)S(1)} %bitcast.49), channel_id=1, source_target_pairs={{0,1},{1,0},{2,3},{3,2},{4,5},{5,4},{6,7},{7,6},{8,9},{9,8},{10,11... | collective-permute-start | bytes 2359304 | tf_op jit(solution)/shard_map/gather/ppermute | solution.py:408
  50.9 7.5 %collective-permute-start.10 = (bf16[1024,384]{1,0:T(8,128)(2,1)}, bf16[1024,384]{1,0:T(8,128)(2,1)S(1)}, u32[]{:S(2)}, u32[]{:S(2)}) collective-permute-start(bf16[1024,384]{1,0:T(8,128)(2,1)} %collective-permute-done.7.refs_1_), channel_id=1, source_target_pairs={{0,1},{1,0},{2,3},{3,2},{4,5},{5,4},{6,7},{7,6},{8,9},{9,8},{10,11... | collective-permute-start | bytes 2359304 | tf_op jit(solution)/shard_map/gather/ppermute | solution.py:408
  50.9 20.3 %collective-permute-start.3 = (bf16[4,384,512]{2,1,0:T(8,128)(2,1)}, bf16[4,384,512]{2,1,0:T(8,128)(2,1)}, u32[]{:S(2)}, u32[]{:S(2)}) collective-permute-start(bf16[4,384,512]{2,1,0:T(8,128)(2,1)} %get-tuple-element.34), channel_id=1, source_target_pairs={{0,1},{1,0},{2,3},{3,2},{4,5},{5,4},{6,7},{7,6},{8,9},{9,8},{10,11... | collective-permute-start | bytes 4718600 | tf_op jit(solution)/shard_map/gather/ppermute | solution.py:408
  51.4 19.8 %collective-permute-start.4 = (bf16[4,384,512]{2,1,0:T(8,128)(2,1)}, bf16[4,384,512]{2,1,0:T(8,128)(2,1)}, u32[]{:S(2)}, u32[]{:S(2)}) collective-permute-start(bf16[4,384,512]{2,1,0:T(8,128)(2,1)} %get-tuple-element.35), channel_id=1, source_target_pairs={{0,1},{1,0},{2,3},{3,2},{4,5},{5,4},{6,7},{7,6},{8,9},{9,8},{10,11... | collective-permute-start | bytes 4718600 | tf_op jit(solution)/shard_map/gather/ppermute | solution.py:408
  53.5 5.6 %collective-permute-start.11 = (bf16[1024,384]{1,0:T(8,128)(2,1)}, bf16[1024,384]{1,0:T(8,128)(2,1)}, u32[]{:S(2)}, u32[]{:S(2)}) collective-permute-start(bf16[1024,384]{1,0:T(8,128)(2,1)} %collective-permute-done.5.refs_2_), channel_id=1, source_target_pairs={{0,1},{1,0},{2,3},{3,2},{4,5},{5,4},{6,7},{7,6},{8,9},{9,8},{10,11... | collective-permute-start | bytes 2359304 | tf_op jit(solution)/shard_map/gather/ppermute | solution.py:408
  55.3 3.9 %copy-start.5 = (bf16[1024,384]{1,0:T(8,128)(2,1)}, bf16[1024,384]{1,0:T(8,128)(2,1)S(1)}, u32[]{:S(2)}) copy-start(bf16[1024,384]{1,0:T(8,128)(2,1)S(1)} %collective-permute-done.9.refs_3_) | copy-start | bytes 2359300
  55.3 13.5 %collective-permute-start.8 = (bf16[512,384]{1,0:T(8,128)(2,1)}, bf16[512,384]{1,0:T(8,128)(2,1)}, u32[]{:S(2)}, u32[]{:S(2)}) collective-permute-start(bf16[512,384]{1,0:T(8,128)(2,1)} %slice.9), channel_id=1, source_target_pairs={{0,6},{1,7},{2,0},{3,1},{4,2},{5,3},{6,4},{7,5},{8,14},{9,15},{10,... | collective-permute-start | bytes 1179656 | tf_op jit(solution)/shard_map/gather/ppermute | solution.py:403
  58.4 0.9 copy-start.6
  58.4 12.3 %collective-permute-start.6 = (bf16[512,384]{1,0:T(8,128)(2,1)}, bf16[512,384]{1,0:T(8,128)(2,1)}, u32[]{:S(2)}, u32[]{:S(2)}) collective-permute-start(bf16[512,384]{1,0:T(8,128)(2,1)} %slice.8), channel_id=1, source_target_pairs={{0,2},{1,3},{2,4},{3,5},{4,6},{5,7},{6,0},{7,1},{8,10},{9,11},{10,... | collective-permute-start | bytes 1179656 | tf_op jit(solution)/shard_map/gather/ppermute | solution.py:403
  70.7 1.9 %collective-permute-start.12 = (bf16[512,384]{1,0:T(8,128)(2,1)}, bf16[512,384]{1,0:T(8,128)(2,1)S(1)}, u32[]{:S(2)}, u32[]{:S(2)}) collective-permute-start(bf16[512,384]{1,0:T(8,128)(2,1)} %collective-permute-done.6.refs_0_.refs_6_), channel_id=1, source_target_pairs={{0,1},{1,0},{2,3},{3,2},{4,5},{5,4},{6,7},{7,6},{8,9},{9,8},{10,11... | collective-permute-start | bytes 1179656 | tf_op jit(solution)/shard_map/forward/ppermute | solution.py:408
  70.7 2.5 %collective-permute-start.13 = (bf16[512,384]{1,0:T(8,128)(2,1)}, bf16[512,384]{1,0:T(8,128)(2,1)S(1)}, u32[]{:S(2)}, u32[]{:S(2)}) collective-permute-start(bf16[512,384]{1,0:T(8,128)(2,1)} %collective-permute-done.8.refs_1_.refs_7_), channel_id=1, source_target_pairs={{0,1},{1,0},{2,3},{3,2},{4,5},{5,4},{6,7},{7,6},{8,9},{9,8},{10,11... | collective-permute-start | bytes 1179656 | tf_op jit(solution)/shard_map/forward/ppermute | solution.py:408
  72.6 1.1 copy-start.7
  73.2 0.7 copy-start.8
  73.7 6.0 %collective-permute-start.14 = (bf16[1024,1536]{1,0:T(8,128)(2,1)}, bf16[1024,1536]{1,0:T(8,128)(2,1)}, u32[]{:S(2)}, u32[]{:S(2)}) collective-permute-start(bf16[1024,1536]{1,0:T(8,128)(2,1)} %bitcast.4.own), channel_id=1, source_target_pairs={{0,1},{1,0},{2,3},{3,2},{4,5},{5,4},{6,7},{7,6},{8,9},{9,8},{10,11... | collective-permute-start | bytes 9437192 | tf_op jit(solution)/shard_map/forward/ppermute | solution.py:408
  88.0 7.8 %collective-permute-start.15 = (bf16[1024,1024]{1,0:T(8,128)(2,1)}, bf16[1024,1024]{1,0:T(8,128)(2,1)}, u32[]{:S(2)}, u32[]{:S(2)}) collective-permute-start(bf16[1024,1024]{1,0:T(8,128)(2,1)} %get-tuple-element.45.grads), channel_id=1, source_target_pairs={{0,1},{1,0},{2,3},{3,2},{4,5},{5,4},{6,7},{7,6},{8,9},{9,8},{10,11... | collective-permute-start | bytes 6291464 | tf_op jit(solution)/shard_map/backward/ppermute | solution.py:408
  88.4 7.4 %collective-permute-start.16 = (bf16[1024,128]{1,0:T(8,128)(2,1)}, bf16[1024,128]{1,0:T(8,128)(2,1)S(1)}, u32[]{:S(2)}, u32[]{:S(2)}) collective-permute-start(bf16[1024,128]{1,0:T(8,128)(2,1)} %get-tuple-element.43), channel_id=1, source_target_pairs={{0,1},{1,0},{2,3},{3,2},{4,5},{5,4},{6,7},{7,6},{8,9},{9,8},{10,11... | collective-permute-start | bytes 786440 | tf_op jit(solution)/shard_map/backward/ppermute | solution.py:408
  95.8 0.7 copy-start.10
  104.1 10.4 %copy-start.16 = (bf16[16,32,384]{2,1,0:T(8,128)(2,1)S(1)}, bf16[16,32,384]{2,1,0:T(8,128)(2,1)}, u32[]{:S(2)}) copy-start(bf16[16,32,384]{2,1,0:T(8,128)(2,1)} %get-tuple-element.49) | copy-start | bytes 1179652
  104.1 11.3 %copy-start.15 = (bf16[16,32,384]{2,1,0:T(8,128)(2,1)S(1)}, bf16[16,32,384]{2,1,0:T(8,128)(2,1)}, u32[]{:S(2)}) copy-start(bf16[16,32,384]{2,1,0:T(8,128)(2,1)} %get-tuple-element.50) | copy-start | bytes 1179652
  104.1 13.8 %copy-start.14 = (bf16[16,32,384]{2,1,0:T(8,128)(2,1)S(1)}, bf16[16,32,384]{2,1,0:T(8,128)(2,1)}, u32[]{:S(2)}) copy-start(bf16[16,32,384]{2,1,0:T(8,128)(2,1)} %get-tuple-element.51) | copy-start | bytes 1179652
  104.1 35.8 %all-to-all-start.3 = ((bf16[16,32,1664]{2,1,0:T(8,128)(2,1)}), bf16[16,32,1664]{2,1,0:T(8,128)(2,1)S(1)}, u32[]{:S(2)}, u32[]{:S(2)}) async-start(bf16[16,32,1664]{2,1,0:T(8,128)(2,1)} %get-tuple-element.52), calls=%async_computation.3 | async-start | bytes 3407872 | tf_op jit(solution)/shard_map/sums/all_to_all | solution.py:411
  114.5 23.2 %collective-permute-start.17 = (bf16[16,32,384]{2,1,0:T(8,128)(2,1)S(1)}, bf16[16,32,384]{2,1,0:T(8,128)(2,1)S(1)}, u32[]{:S(2)}, u32[]{:S(2)}) collective-permute-start(bf16[16,32,384]{2,1,0:T(8,128)(2,1)S(1)} %copy-done.16), channel_id=1, source_target_pairs={{0,2},{1,3},{2,4},{3,5},{4,6},{5,7},{6,0},{7,1},{8,10},{9,11},{10,... | collective-permute-start | bytes 1179656 | tf_op jit(solution)/shard_map/sums/ppermute | solution.py:403
  115.4 22.3 %collective-permute-start.18 = (bf16[16,32,384]{2,1,0:T(8,128)(2,1)S(1)}, bf16[16,32,384]{2,1,0:T(8,128)(2,1)S(1)}, u32[]{:S(2)}, u32[]{:S(2)}) collective-permute-start(bf16[16,32,384]{2,1,0:T(8,128)(2,1)S(1)} %copy-done.15), channel_id=1, source_target_pairs={{0,4},{1,5},{2,6},{3,7},{4,0},{5,1},{6,2},{7,3},{8,12},{9,13},{10,... | collective-permute-start | bytes 1179656 | tf_op jit(solution)/shard_map/sums/ppermute | solution.py:403
  117.9 19.9 %collective-permute-start.19 = (bf16[16,32,384]{2,1,0:T(8,128)(2,1)S(1)}, bf16[16,32,384]{2,1,0:T(8,128)(2,1)S(1)}, u32[]{:S(2)}, u32[]{:S(2)}) collective-permute-start(bf16[16,32,384]{2,1,0:T(8,128)(2,1)S(1)} %copy-done.14), channel_id=1, source_target_pairs={{0,6},{1,7},{2,0},{3,1},{4,2},{5,3},{6,4},{7,5},{8,14},{9,15},{10,... | collective-permute-start | bytes 1179656 | tf_op jit(solution)/shard_map/sums/ppermute | solution.py:403
  130.1 7.7 %copy-start.9 = (bf16[16,32,384]{2,1,0:T(8,128)(2,1)S(1)}, bf16[16,32,384]{2,1,0:T(8,128)(2,1)}, u32[]{:S(2)}) copy-start(bf16[16,32,384]{2,1,0:T(8,128)(2,1)} %get-tuple-element.48) | copy-start | bytes 1179652
  130.1 16.1 %copy-start = (s32[128,2]{0,1:T(2,128)S(1)}, s32[128,2]{0,1:T(2,128)}, u32[]{:S(2)}) copy-start(s32[128,2]{0,1:T(2,128)} %param.9) | copy-start | bytes 3076
  137.7 17.9 %copy-start.1 = (bf16[128,2]{0,1:T(2,128)(2,1)S(1)}, bf16[128,2]{0,1:T(2,128)(2,1)}, u32[]{:S(2)}) copy-start(bf16[128,2]{0,1:T(2,128)(2,1)} %param.10) | copy-start | bytes 1540
  139.8 14.4 %all-to-all-start.2 = ((bf16[16,32,384]{2,1,0:T(8,128)(2,1)}), bf16[16,32,384]{2,1,0:T(8,128)(2,1)S(1)}, u32[]{:S(2)}, u32[]{:S(2)}) async-start(bf16[16,32,384]{2,1,0:T(8,128)(2,1)} %add_convert_fusion), calls=%async_computation.2 | async-start | bytes 786432 | tf_op jit(solution)/shard_map/late_sum/all_to_all | solution.py:411
  147.1 7.2 %collective-permute-start.20 = (bf16[128,512]{1,0:T(8,128)(2,1)S(1)}, bf16[128,512]{1,0:T(8,128)(2,1)S(1)}, u32[]{:S(2)}, u32[]{:S(2)}) collective-permute-start(bf16[128,512]{1,0:T(8,128)(2,1)S(1)} %get-tuple-element.55), channel_id=1, source_target_pairs={{0,2},{1,3},{2,4},{3,5},{4,6},{5,7},{6,0},{7,1},{8,10},{9,11},{10,... | collective-permute-start | bytes 393224 | tf_op jit(solution)/shard_map/finish/ppermute | solution.py:403
  148.0 7.2 %collective-permute-start.21 = (bf16[128,512]{1,0:T(8,128)(2,1)S(1)}, bf16[128,512]{1,0:T(8,128)(2,1)S(1)}, u32[]{:S(2)}, u32[]{:S(2)}) collective-permute-start(bf16[128,512]{1,0:T(8,128)(2,1)S(1)} %get-tuple-element.56), channel_id=1, source_target_pairs={{0,4},{1,5},{2,6},{3,7},{4,0},{5,1},{6,2},{7,3},{8,12},{9,13},{10,... | collective-permute-start | bytes 393224 | tf_op jit(solution)/shard_map/finish/ppermute | solution.py:403
  150.5 5.2 %collective-permute-start.22 = (bf16[128,512]{1,0:T(8,128)(2,1)S(1)}, bf16[128,512]{1,0:T(8,128)(2,1)S(1)}, u32[]{:S(2)}, u32[]{:S(2)}) collective-permute-start(bf16[128,512]{1,0:T(8,128)(2,1)S(1)} %get-tuple-element.57), channel_id=1, source_target_pairs={{0,6},{1,7},{2,0},{3,1},{4,2},{5,3},{6,4},{7,5},{8,14},{9,15},{10,... | collective-permute-start | bytes 393224 | tf_op jit(solution)/shard_map/finish/ppermute | solution.py:403
